TPU v7x, 32 devices: a whole 2x2x4 slice. The times are simulated.
32 devices in a mesh: row: 4 (over z), col: 8 (over y, x, core).
Axes of the slice: x: 2, y: 2, z: 4, core: 2. Of those that a mesh axis runs over, the one named last changes fastest.
Arguments:
- video_scores_in: float32 [32768, 128], P(('col', 'row')), may hold values from -6 to 6
- audio_seed: int32 [32768], P(('row', 'col')), may hold values from 0 to 255
- video_seed: int32 [32768], P(('col', 'row')), may hold values from 0 to 255
- tile_values: bfloat16 [4, 8, 320, 128, 128], P('row', 'col'), may hold values from 0 to 1
- tile_rows: int32 [4, 8, 320], P('row', 'col'), may hold values from 0 to 63, as said below
- tile_cols: int32 [4, 8, 320], P('row', 'col'), may hold values from 0 to 31, as said below
- tile_count: int32 [4, 8], P('row', 'col'), may hold values from 64 to 320, as said below
Outputs:
- audio_scores: float32 [32768, 128], P(('row', 'col'))
- video_scores: float32 [32768, 128], P(('col', 'row'))
Inputs may be any that keep to these rules, and one draw needn't show every extreme that they name: `tile_rows`: every tile row of a cell's row group and every tile column of its column group is named by some live slot of that cell; two slots may name the same tile position, and then both add. `tile_cols`: see tile_rows. `tile_count`: loads differ widely between cells; some cell uses all 320 slots.
All inputs are finite; a program needn't handle non-finite values.
Results may differ from a plain program's by a relative error of at most 0.005.
Values may be sent and summed in bfloat16 or wider, within the bound.
No kernel may reach another device: no remote copies, remote signals or barrier semaphores. Data moves between devices by JAX's collectives and lax.ppermute only.
A program may use at most 192 MiB of HBM per device.

v0:
```python
import jax
import jax.numpy as jnp
from jax import lax
from jax.sharding import PartitionSpec as P

blend_weight = 0.75


def blend(total, masses, seed_ids):
    classes = total.shape[1]
    labels = (seed_ids[:, None] == jnp.arange(classes, dtype=jnp.int32)[None, :]).astype(
        jnp.float32
    )
    return blend_weight * total / jnp.sqrt(masses)[:, None] + (1.0 - blend_weight) * labels


def block_pieces(tile_vals, row_ids, col_ids, live_count, offset, per_block):
    fragment_values = lax.dynamic_slice_in_dim(tile_vals, offset, per_block, 0)
    piece_rows = lax.dynamic_slice_in_dim(row_ids, offset, per_block, 0)
    piece_cols = lax.dynamic_slice_in_dim(col_ids, offset, per_block, 0)
    alive_mask = offset + jnp.arange(per_block, dtype=jnp.int32) < live_count
    return (fragment_values, piece_rows, piece_cols, alive_mask)


def pick_tiles(panel_flat, index_list, table_size):
    chooser = (index_list[:, None] == jnp.arange(table_size, dtype=jnp.int32)[None, :]).astype(
        jnp.bfloat16
    )
    return jnp.dot(chooser, panel_flat, preferred_element_type=jnp.float32).astype(jnp.bfloat16)


def place_sums(index_list, alive_mask, values, table_size):
    placer = (
        (jnp.arange(table_size, dtype=jnp.int32)[:, None] == index_list[None, :])
        & alive_mask[None, :]
    ).astype(jnp.bfloat16)
    flat_values = values.reshape(values.shape[0], -1)
    upper_part = flat_values.astype(jnp.bfloat16)
    lower_part = (flat_values - upper_part.astype(jnp.float32)).astype(jnp.bfloat16)
    placed = jnp.dot(placer, upper_part, preferred_element_type=jnp.float32) + jnp.dot(
        placer, lower_part, preferred_element_type=jnp.float32
    )
    return placed.reshape((table_size,) + values.shape[1:])


def spread_forward(
    tile_vals,
    row_ids,
    col_ids,
    live_count,
    video_flat,
    rows_block,
    cols_block,
    per_block,
    loop_limit,
):
    tile_size = tile_vals.shape[1]
    classes = video_flat.shape[1] // tile_size

    def spread_one_block(block, totals):
        fragment_values, piece_rows, piece_cols, alive_mask = block_pieces(
            tile_vals, row_ids, col_ids, live_count, block * per_block, per_block
        )
        selected_entries = pick_tiles(video_flat, piece_cols, cols_block).reshape(
            per_block, tile_size, classes
        )
        weighted_products = jnp.einsum(
            "efr,erj->efj", fragment_values, selected_entries, preferred_element_type=jnp.float32
        )
        masses = jnp.sum(fragment_values, axis=2, dtype=jnp.float32)
        return (
            totals[0] + place_sums(piece_rows, alive_mask, weighted_products, rows_block),
            totals[1] + place_sums(piece_rows, alive_mask, masses, rows_block),
        )

    initial = (
        jnp.zeros((rows_block, tile_size, classes), jnp.float32),
        jnp.zeros((rows_block, tile_size), jnp.float32),
    )
    return lax.fori_loop(0, loop_limit, spread_one_block, initial)


def propagate_reverse(
    tile_vals,
    row_ids,
    col_ids,
    live_count,
    audio_flat,
    rows_block,
    cols_block,
    per_block,
    loop_limit,
):
    tile_size = tile_vals.shape[1]
    classes = audio_flat.shape[1] // tile_size

    def propagate_one_block(block, totals):
        fragment_values, piece_rows, piece_cols, alive_mask = block_pieces(
            tile_vals, row_ids, col_ids, live_count, block * per_block, per_block
        )
        selected_entries = pick_tiles(audio_flat, piece_rows, rows_block).reshape(
            per_block, tile_size, classes
        )
        weighted_products = jnp.einsum(
            "nhv,nhk->nvk", fragment_values, selected_entries, preferred_element_type=jnp.float32
        )
        masses = jnp.sum(fragment_values, axis=1, dtype=jnp.float32)
        return (
            totals[0] + place_sums(piece_cols, alive_mask, weighted_products, cols_block),
            totals[1] + place_sums(piece_cols, alive_mask, masses, cols_block),
        )

    initial = (
        jnp.zeros((cols_block, tile_size, classes), jnp.float32),
        jnp.zeros((cols_block, tile_size), jnp.float32),
    )
    return lax.fori_loop(0, loop_limit, propagate_one_block, initial)


def body(video_scores_in, audio_seed, video_seed, tile_values, tile_rows, tile_cols, tile_count):
    tile_vals = tile_values[0, 0]
    row_ids = tile_rows[0, 0]
    col_ids = tile_cols[0, 0]
    live_count = tile_count[0, 0]
    tiles_dev = tile_vals.shape[0]
    tile_size = tile_vals.shape[1]
    shard_rows, classes = video_scores_in.shape
    rows_block = shard_rows * lax.axis_size("col") // tile_size
    cols_block = shard_rows * lax.axis_size("row") // tile_size
    block_count = tiles_dev // rows_block
    gathered = lax.all_gather(video_scores_in.astype(jnp.bfloat16), "row", axis=0, tiled=True)
    video_flat = gathered.reshape(cols_block, tile_size * classes)
    forward_sum, forward_mass = spread_forward(
        tile_vals,
        row_ids,
        col_ids,
        live_count,
        video_flat,
        rows_block,
        cols_block,
        rows_block,
        block_count,
    )
    forward_sum = forward_sum.reshape(rows_block * tile_size, classes)
    forward_mass = forward_mass.reshape(rows_block * tile_size)
    total, masses = lax.psum((forward_sum, forward_mass), "col")
    seeds_all = lax.all_gather(audio_seed, "col", axis=0, tiled=True)
    audio_full = blend(total, masses, seeds_all)
    audio_scores = lax.dynamic_slice_in_dim(
        audio_full, lax.axis_index("col") * shard_rows, shard_rows, 0
    )
    audio_half = audio_full.astype(jnp.bfloat16)
    audio_flat = audio_half.reshape(rows_block, tile_size * classes)
    back_sum, back_mass = propagate_reverse(
        tile_vals,
        row_ids,
        col_ids,
        live_count,
        audio_flat,
        rows_block,
        cols_block,
        rows_block,
        block_count,
    )
    total_back, mass_back = (
        lax.psum_scatter(
            back_sum.reshape(cols_block * tile_size, classes),
            "row",
            scatter_dimension=0,
            tiled=True,
        ),
        lax.psum_scatter(
            back_mass.reshape(cols_block * tile_size), "row", scatter_dimension=0, tiled=True
        ),
    )
    video_scores = blend(total_back, mass_back, video_seed)
    return (audio_scores, video_scores)


def solution(mesh):
    in_specs = (
        P(("col", "row"), None),
        P(("row", "col")),
        P(("col", "row")),
        P("row", "col", None, None, None),
        P("row", "col", None),
        P("row", "col", None),
        P("row", "col"),
    )
    out_specs = (P(("row", "col"), None), P(("col", "row"), None))
    return jax.shard_map(body, mesh=mesh, in_specs=in_specs, out_specs=out_specs, check_vma=False)
```

profile of v0, /device:TPU:0, one launch (start us, length us, event | category | flops | bytes accessed | tf_op | source)
XLA Modules:
  0.0 356.3 jit_solution(10867925765586906317)
XLA Ops:
  7.2 1.8 convert_element_type.134
  10.5 30.3 %all-gather.2.cloned.1.call-done = bf16[4096,128]{1,0:T(8,128)(2,1)} async-done(((bf16[1024,128]{1,0:T(8,128)(2,1)}), bf16[4096,128]{1,0:T(8,128)(2,1)}) %all-gather.2.cloned.1.call-update) | async-done | bytes 1048592 | tf_op jit(solution)/shard_map/all_gather | solution.py:131
  42.3 90.8 %while.32 = (s32[]{:T(128)}, f32[64,128,128]{2,1,0:T(8,128)}, f32[64,128]{1,0:T(8,128)S(1)}, s32[320]{0:T(512)S(1)}, s32[]{:T(128)}, /*index=5*/bf16[320,128,128...) while((s32[]{:T(128)}, f32[64,128,128]{2,1,0:T(8,128)}, ...), condition=%wide.region_2.0_spmd.clone, body=%wide.region_0.0_spmd.clone.sunk | while | flops 616654976 | bytes 93555520 | solution.py:80
  44.5 2.4 fusion.99
  46.9 2.8 fusion.100
  49.6 2.9 fusion.101
  54.7 3.7 %bitcast_add_fusion.4 = (f32[64,128,128]{2,1,0:T(8,128)S(1)}, f32[64,128]{1,0:T(8,128)S(1)}) fusion(f32[8,8,128,128]{3,2,1,0:T(8,128)S(1)} %copy.45, f32[64,128,128]{2,1,0:T(8,128)S(1)} %copy-done, pred[]{:T(512)S(6)} %compare.6, bf16[320,128,128]{2,1,0:T(8,128)(2,1)} %get-tuple-element.523, s32[]{:T(128)S(6)} %select_n.26), kind=kLoop, calls=%fused_computation.2.clone.1 | loop fusion | flops 4186112 | bytes 14712837 | tf_op jit(solution)/shard_map/while/body/eval_jaxpr/add | solution.py:72
  58.7 1.8 copy-done.1
  62.6 2.4 fusion.99
  65.0 2.8 fusion.100
  67.8 2.9 fusion.101
  72.9 3.7 %bitcast_add_fusion.4 = (f32[64,128,128]{2,1,0:T(8,128)S(1)}, f32[64,128]{1,0:T(8,128)S(1)}) fusion(f32[8,8,128,128]{3,2,1,0:T(8,128)S(1)} %copy.45, f32[64,128,128]{2,1,0:T(8,128)S(1)} %copy-done, pred[]{:T(512)S(6)} %compare.6, bf16[320,128,128]{2,1,0:T(8,128)(2,1)} %get-tuple-element.523, s32[]{:T(128)S(6)} %select_n.26), kind=kLoop, calls=%fused_computation.2.clone.1 | loop fusion | flops 4186112 | bytes 14712837 | tf_op jit(solution)/shard_map/while/body/eval_jaxpr/add | solution.py:72
  76.8 1.8 copy-done.1
  80.8 2.4 fusion.99
  83.2 2.8 fusion.100
  85.9 2.9 fusion.101
  91.0 3.7 %bitcast_add_fusion.4 = (f32[64,128,128]{2,1,0:T(8,128)S(1)}, f32[64,128]{1,0:T(8,128)S(1)}) fusion(f32[8,8,128,128]{3,2,1,0:T(8,128)S(1)} %copy.45, f32[64,128,128]{2,1,0:T(8,128)S(1)} %copy-done, pred[]{:T(512)S(6)} %compare.6, bf16[320,128,128]{2,1,0:T(8,128)(2,1)} %get-tuple-element.523, s32[]{:T(128)S(6)} %select_n.26), kind=kLoop, calls=%fused_computation.2.clone.1 | loop fusion | flops 4186112 | bytes 14712837 | tf_op jit(solution)/shard_map/while/body/eval_jaxpr/add | solution.py:72
  95.0 1.8 copy-done.1
  99.0 2.4 fusion.99
  101.3 2.8 fusion.100
  104.1 2.9 fusion.101
  109.2 3.7 %bitcast_add_fusion.4 = (f32[64,128,128]{2,1,0:T(8,128)S(1)}, f32[64,128]{1,0:T(8,128)S(1)}) fusion(f32[8,8,128,128]{3,2,1,0:T(8,128)S(1)} %copy.45, f32[64,128,128]{2,1,0:T(8,128)S(1)} %copy-done, pred[]{:T(512)S(6)} %compare.6, bf16[320,128,128]{2,1,0:T(8,128)(2,1)} %get-tuple-element.523, s32[]{:T(128)S(6)} %select_n.26), kind=kLoop, calls=%fused_computation.2.clone.1 | loop fusion | flops 4186112 | bytes 14712837 | tf_op jit(solution)/shard_map/while/body/eval_jaxpr/add | solution.py:72
  113.2 1.8 copy-done.1
  117.1 2.4 fusion.99
  119.5 2.8 fusion.100
  122.3 2.9 fusion.101
  127.3 3.7 %bitcast_add_fusion.4 = (f32[64,128,128]{2,1,0:T(8,128)S(1)}, f32[64,128]{1,0:T(8,128)S(1)}) fusion(f32[8,8,128,128]{3,2,1,0:T(8,128)S(1)} %copy.45, f32[64,128,128]{2,1,0:T(8,128)S(1)} %copy-done, pred[]{:T(512)S(6)} %compare.6, bf16[320,128,128]{2,1,0:T(8,128)(2,1)} %get-tuple-element.523, s32[]{:T(128)S(6)} %select_n.26), kind=kLoop, calls=%fused_computation.2.clone.1 | loop fusion | flops 4186112 | bytes 14712837 | tf_op jit(solution)/shard_map/while/body/eval_jaxpr/add | solution.py:72
  131.3 1.8 copy-done.1
  133.2 13.8 %copy.11 = bf16[1,1,320,128,128]{3,4,2,1,0:T(8,128)(2,1)} copy(bf16[1,1,320,128,128]{4,3,2,1,0:T(8,128)(2,1)} %bitcast.93) | data formatting | bytes 20971520 | tf_op args[3]
  147.0 10.0 %all_gather.7 = s32[8192]{0:T(1024)S(1)} all-gather(s32[1024]{0:T(1024)S(1)} %copy-done.4), channel_id=1, replica_groups=mesh['row'=4,'col'=8] {'col'}, dimensions={0}, use_global_device_ids=true | all-gather | bytes 36864 | tf_op jit(solution)/shard_map/all_gather | solution.py:147
  157.0 23.8 %psum.15 = f32[8192]{0:T(1024)S(1)} all-reduce(f32[8192]{0:T(1024)S(1)} %bitcast.95), channel_id=1, replica_groups=mesh['row'=4,'col'=8] {'col'}, use_global_device_ids=true, to_apply=%region_4.0 | all-reduce | flops 8192 | bytes 65536 | tf_op jit(solution)/shard_map/psum | solution.py:146
  180.8 33.2 %all-reduce.3.cloned.1.call-done = f32[8192,128]{1,0:T(8,128)} async-done(((f32[8192,128]{1,0:T(8,128)}), f32[8192,128]{1,0:T(8,128)}) %all-reduce.3.cloned.1.call-update) | async-done | bytes 4194320 | tf_op jit(solution)/shard_map/psum | solution.py:146
  214.0 9.8 %fusion.54 = (bf16[8192,128]{1,0:T(8,128)(2,1)}, f32[8192,128]{1,0:T(8,128)}) fusion(s32[8192]{0:T(1024)S(1)} %all_gather.7, f32[8192]{0:T(1024)S(1)} %sqrt.6, f32[8192,128]{1,0:T(8,128)} %all-reduce.3.cloned.1.call-done), kind=kLoop, calls=%fused_computation.70 | loop fusion | flops 6291456 | bytes 10551296 | tf_op jit(solution)/shard_map/convert_element_type | solution.py:152
  223.8 4.2 %reshape.85 = bf16[64,16384]{1,0:T(8,128)(2,1)} reshape(bf16[8192,128]{1,0:T(8,128)(2,1)} %get-tuple-element.388) | data formatting | bytes 4194304 | tf_op jit(solution)/shard_map/reshape | solution.py:153
  228.0 73.8 %while.33 = (s32[]{:T(128)}, f32[32,128,128]{2,1,0:T(8,128)S(1)}, f32[32,128]{1,0:T(8,128)S(1)}, s32[320]{0:T(512)S(1)}, s32[]{:T(128)}, /*index=5*/bf16[320,128...) while((s32[]{:T(128)}, f32[32,128,128]{2,1,0:T(8,128)S(1)}, ...), condition=%wide.region_7.0_spmd.clone, body=%wide.region_5.0_spmd.clone.sunk | while | flops 546898048 | bytes 44206860 | solution.py:117
  228.8 2.2 convert_reduce_fusion.3
  231.3 2.3 fusion.113
  234.2 2.4 fusion.114
  236.6 2.5 fusion.115
  239.1 2.6 fusion.116
  243.6 2.2 convert_reduce_fusion.3
  246.1 2.3 fusion.113
  249.0 2.4 fusion.114
  251.3 2.5 fusion.115
  253.9 2.6 fusion.116
  258.3 2.2 convert_reduce_fusion.3
  260.8 2.3 fusion.113
  263.7 2.4 fusion.114
  266.1 2.5 fusion.115
  268.6 2.6 fusion.116
  273.1 2.2 convert_reduce_fusion.3
  275.6 2.3 fusion.113
  278.5 2.4 fusion.114
  280.9 2.5 fusion.115
  283.4 2.6 fusion.116
  287.9 2.2 convert_reduce_fusion.3
  290.3 2.3 fusion.113
  293.3 2.4 fusion.114
  295.6 2.5 fusion.115
  298.2 2.6 fusion.116
  304.4 19.3 %all-reduce = f32[4096]{0:T(1024)S(1)} all-reduce(f32[4096]{0:T(1024)S(1)} %bitcast.96), channel_id=3, replica_groups=mesh['row'=4,'col'=8] {'row'}, use_global_device_ids=true, to_apply=%region_9.0.clone | all-reduce | flops 4096 | bytes 32768
  323.8 1.9 constant_dynamic-slice_fusion
  325.6 22.0 %reduce-scatter.2.cloned.1.call-done = f32[1024,128]{1,0:T(8,128)} async-done(((f32[4096,128]{1,0:T(8,128)}), f32[1024,128]{1,0:T(8,128)}) %reduce-scatter.2.cloned.1.call-update) | async-done | bytes 524304 | tf_op jit(solution)/shard_map/reduce_scatter | solution.py:166
  347.6 2.2 select_add_fusion.1
  (119 shorter events, 40.9 us)
Async XLA Ops:
  7.2 33.6 %all-gather.2.cloned.1.call-start = ((), (), s32[]{:S(2)}) async-start(), calls=%async_computation.1 | async-start | bytes 1310720 | tf_op jit(solution)/shard_map/all_gather | solution.py:131
  9.0 205.0 %all-reduce.3.cloned.1.call-start = ((), (), s32[]{:S(2)}) async-start(), calls=%async_computation.2 | async-start | bytes 8388608 | tf_op jit(solution)/shard_map/psum | solution.py:146
  52.5 2.2 copy-start
  58.4 2.1 copy-start.1
  70.7 2.2 copy-start
  76.6 2.1 copy-start.1
  88.8 2.2 copy-start
  94.7 2.1 copy-start.1
  107.0 2.2 copy-start
  112.9 2.1 copy-start.1
  125.2 2.2 copy-start
  131.0 2.1 copy-start.1
  133.1 214.5 %reduce-scatter.2.cloned.1.call-start = ((), (), s32[]{:S(2)}) async-start(), calls=%async_computation.3 | async-start | bytes 2621440 | tf_op jit(solution)/shard_map/reduce_scatter | solution.py:166
  133.2 13.8 %copy-start.4 = (s32[1024]{0:T(1024)S(1)}, s32[1024]{0:T(1024)}, u32[]{:S(2)}) copy-start(s32[1024]{0:T(1024)} %param.12) | copy-start | bytes 12292
  228.0 75.2 %copy-start.5 = (u32[32]{0:T(128)S(1)}, u32[32]{0:T(128)}, u32[]{:S(2)}) copy-start(u32[32]{0:T(128)} %constant.97) | copy-start | bytes 388
  228.0 119.6 %copy-start.3 = (s32[1024]{0:T(1024)S(1)}, s32[1024]{0:T(1024)}, u32[]{:S(2)}) copy-start(s32[1024]{0:T(1024)} %param.13) | copy-start | bytes 12292
  301.8 1.4 copy-start.2
Sparse Core Ops, SparseCore 0:
  10.1 30.6 all-gather.1
  133.3 80.7 all-reduce.2
  303.3 44.2 reduce-scatter.1
where the time goes:
time: 358 us; the launch traced here: 356 us
  matrix products  95.8 us (27%)
  waiting for transfers between devices  85.6 us (24%)
  other arithmetic  54.2 us (15%)
  blocking collectives  53.1 us (15%)
  local copies, waits for them, and re-layouts  52.4 us (15%)
  between operations  14.5 us (4%)
    psum x1, waiting for transfers between devices, body(): total, masses = lax.psum((forward_sum, forward_mass), 'col')  33.2 us
    all_gather x1, waiting for transfers between devices, body(): lax.all_gather(video_scores_in.astype(jnp.bfloat16), 'row', axis=0, tiled...  30.3 us
    dot_general x20, matrix products, place_sums(): jnp.dot(placer, lower_part, preferred_element_type=jnp.float32)  29 us
    dot_general x20, matrix products, place_sums(): jnp.dot(placer, upper_part, preferred_element_type=jnp.float32)  27.9 us
    while x40, local copies, waits for them, and re-layouts  27.5 us
    psum x1, blocking collectives, body(): total, masses = lax.psum((forward_sum, forward_mass), 'col')  23.8 us
    reduce_scatter x1, waiting for transfers between devices, body(): lax.psum_scatter(back_sum.reshape(cols_block * tile_size, classes), 'row'...  22 us
    unnamed x1, blocking collectives  19.3 us
  transfers between devices with their start and end apart: 3, of which 3 were waited for; matrix products, arithmetic and copies ran while one was open for 5% of the time, Pallas kernels for 0%

commit v1 on v0

v1 whole, which is shorter than its diff:
```python
import functools

import jax
import jax.numpy as jnp
from jax import lax
from jax.experimental import pallas as pl
from jax.experimental.pallas import tpu as pltpu
from jax.sharding import PartitionSpec as P

BLEND = 0.75
CHUNKS = 1
GROUP = 32
VMEM = pl.BlockSpec(memory_space=pltpu.VMEM)
NT = (((1,), (1,)), ((), ()))
NN = (((1,), (0,)), ((), ()))


def params(mib):
    return pltpu.CompilerParams(vmem_limit_bytes=mib * 2**20)


def split_half(mass):
    high = mass.astype(jnp.bfloat16)
    low = (mass - high.astype(jnp.float32)).astype(jnp.bfloat16)
    return jnp.concatenate([high.astype(jnp.float32), low.astype(jnp.float32)], axis=0).astype(
        jnp.bfloat16
    )


def prep_kernel(video_ref, *out_refs):
    tiles = video_ref.shape[0] // 128
    width = out_refs[0].shape[0] // tiles
    for t in range(tiles):
        flipped = video_ref[t * 128 : (t + 1) * 128, :].T.astype(jnp.bfloat16)
        for k, out_ref in enumerate(out_refs):
            out_ref[t * width : (t + 1) * width, :] = flipped[k * width : (k + 1) * width, :]


def prep(video, chunks):
    rows, classes = video.shape
    width = classes // chunks
    shape = jax.ShapeDtypeStruct((rows // 128 * width, 128), jnp.bfloat16)
    return pl.pallas_call(
        prep_kernel, out_shape=[shape] * chunks, in_specs=[VMEM], out_specs=[VMEM] * chunks
    )(video)


def sweep_kernel(
    info, to_ids, from_ids, tiles_ref, *refs, pieces, outs, with_mass, transposed, width, shard
):
    piece_refs = refs[:pieces]
    out_refs = refs[pieces : pieces + outs]
    panel, acc, mass = refs[pieces + outs :]
    step = pl.program_id(0)
    group = tiles_ref.shape[0]
    lhs_rows = width + (16 if with_mass else 0)
    dummy = acc.shape[0] - 1

    @pl.when(step == 0)
    def _():
        for m, piece in enumerate(piece_refs):
            for t in range(shard):
                panel[m * shard + t, :width, :] = piece[t * width : (t + 1) * width, :]
        if with_mass:

            def ones(n, carry):
                panel[n, width:, :] = jnp.ones((16, 128), jnp.bfloat16)
                return carry

            lax.fori_loop(0, panel.shape[0], ones, 0)
            mass[...] = jnp.zeros_like(mass)

        def clear(n, carry):
            acc[n] = jnp.zeros((width, 128), jnp.float32)
            return carry

        lax.fori_loop(0, acc.shape[0], clear, 0)

    live = info[2]

    @pl.when(step * group < live)
    def _():
        for g in range(group):
            slot = step * group + g
            to = jnp.where(slot < live, to_ids[slot] ^ info[0], dummy)
            source = from_ids[slot] ^ info[1]
            product = lax.dot_general(
                panel[source],
                tiles_ref[g],
                NT if transposed else NN,
                preferred_element_type=jnp.float32,
            )
            acc[to] += product[:width]
            if with_mass:
                mass[to] += product[width : width + 8]

    @pl.when(step == pl.num_programs(0) - 1)
    def _():
        per_out = dummy // shard // outs
        for h in range(outs):
            out_ref = out_refs[h]
            for s in range(per_out):
                base = (s * outs + h) * shard
                for t in range(shard):
                    out_ref[s, t * width : (t + 1) * width, :] = acc[base + t].astype(out_ref.dtype)
                if with_mass:
                    own = jnp.concatenate([mass[base + t, 0:1, :] for t in range(shard)], axis=0)
                    out_ref[s, shard * width :, :] = split_half(own)


def sweep(info, to_ids, from_ids, tiles, pieces, to_tiles, outs, with_mass, transposed, width):
    slots = tiles.shape[0]
    shard = pieces[0].shape[0] // width
    group = GROUP
    rows = shard * width + (2 * shard if with_mass else 0)
    lhs_rows = width + (16 if with_mass else 0)
    per_out = to_tiles // shard // outs
    kernel = functools.partial(
        sweep_kernel,
        pieces=len(pieces),
        outs=outs,
        with_mass=with_mass,
        transposed=transposed,
        width=width,
        shard=shard,
    )

    def block(b, info, to_ids, from_ids):
        return (jnp.minimum(b, (info[2] - 1) // group), 0, 0)

    def whole2(b, *_):
        return (0, 0)

    def whole3(b, *_):
        return (0, 0, 0)

    return pl.pallas_call(
        kernel,
        grid_spec=pltpu.PrefetchScalarGridSpec(
            num_scalar_prefetch=3,
            grid=(slots // group,),
            in_specs=[pl.BlockSpec((group, 128, 128), block)]
            + [pl.BlockSpec(p.shape, whole2) for p in pieces],
            out_specs=[pl.BlockSpec((per_out, rows, 128), whole3)] * outs,
            scratch_shapes=[
                pltpu.VMEM((len(pieces) * shard, lhs_rows, 128), jnp.bfloat16),
                pltpu.VMEM((to_tiles + 1, width, 128), jnp.float32),
                pltpu.VMEM((to_tiles + 1, 8, 128), jnp.float32),
            ],
        ),
        out_shape=[jax.ShapeDtypeStruct((per_out, rows, 128), jnp.bfloat16)] * outs,
        compiler_params=params(56),
    )(info, to_ids, from_ids, tiles, *pieces)


def pair_sum_kernel(keep_ref, got_ref, *out_refs, with_mass, body_rows):
    for s, out_ref in enumerate(out_refs):
        total = keep_ref[s, :body_rows].astype(jnp.float32) + got_ref[s, :body_rows].astype(
            jnp.float32
        )
        out_ref[:body_rows, :] = total.astype(out_ref.dtype)
        if with_mass:
            mass = both_halves(keep_ref[s, body_rows:]) + both_halves(got_ref[s, body_rows:])
            if s == 0:
                out_ref[body_rows:, :] = jnp.concatenate([mass, jnp.zeros_like(mass)], axis=0)
            else:
                out_ref[body_rows:, :] = split_half(mass)


def both_halves(block):
    wide = block.astype(jnp.float32)
    half = wide.shape[0] // 2
    return wide[:half] + wide[half:]


def pair_sum(keep, got, with_mass, body_rows):
    count, rows, _ = keep.shape
    shapes = [
        jax.ShapeDtypeStruct((rows, 128), jnp.float32 if s == 0 else jnp.bfloat16)
        for s in range(count)
    ]
    return pl.pallas_call(
        functools.partial(pair_sum_kernel, with_mass=with_mass, body_rows=body_rows),
        out_shape=shapes,
        in_specs=[VMEM] * 2,
        out_specs=[VMEM] * count,
        compiler_params=params(48),
    )(keep, got)


def mix(own, scale, seeds, t, width, first):
    classes = lax.broadcasted_iota(jnp.int32, (width, 128), 0) + first
    labels = jnp.where(classes == seeds[t : t + 1, :], 1.0 - BLEND, 0.0)
    return own * scale[t : t + 1, :] + labels


def audio_kernel(seed_ref, own_ref, *refs, width, shard, first, with_mass):
    refs = list(refs)
    half_ref, full_ref, mass_out = refs[-3:]
    mass_in = None if with_mass else refs[0]
    got = refs[:-3] if with_mass else refs[1:-3]
    body = shard * width
    if with_mass:
        mass = own_ref[body : body + shard, :]
        for g in got:
            mass += both_halves(g[body:])
    else:
        mass = mass_in[...]
    mass_out[...] = mass
    scale = BLEND / jnp.sqrt(mass)
    seeds = seed_ref[...]
    for t in range(shard):
        span = slice(t * width, (t + 1) * width)
        total = own_ref[span, :].astype(jnp.float32)
        for g in got:
            total += g[span, :].astype(jnp.float32)
        scores = mix(total, scale, seeds, t, width, first)
        half_ref[span, :] = scores.astype(jnp.bfloat16)
        full_ref[span, :] = scores


def audio_blend(seeds, own, got, mass, width, first):
    shard = seeds.shape[0]
    args = [seeds, own] + ([] if mass is None else [mass]) + list(got)
    return pl.pallas_call(
        functools.partial(
            audio_kernel, width=width, shard=shard, first=first, with_mass=mass is None
        ),
        out_shape=[
            jax.ShapeDtypeStruct((shard * width, 128), jnp.bfloat16),
            jax.ShapeDtypeStruct((shard * width, 128), jnp.float32),
            jax.ShapeDtypeStruct((shard, 128), jnp.float32),
        ],
        in_specs=[VMEM] * len(args),
        out_specs=[VMEM] * 3,
        compiler_params=params(48),
    )(*args)


def flip_kernel(*refs):
    out_ref = refs[-1]
    width = 128 // (len(refs) - 1)
    for t in range(out_ref.shape[0] // 128):
        parts = [r[t * width : (t + 1) * width, :] for r in refs[:-1]]
        out_ref[t * 128 : (t + 1) * 128, :] = jnp.concatenate(parts, axis=0).T


def flip(parts):
    rows = parts[0].shape[0] * len(parts)
    return pl.pallas_call(
        flip_kernel,
        out_shape=jax.ShapeDtypeStruct((rows, 128), jnp.float32),
        in_specs=[VMEM] * len(parts),
        out_specs=VMEM,
        compiler_params=params(48),
    )(*parts)


def video_kernel(seed_ref, *refs, chunks, width, shard):
    out_ref = refs[-1]
    count = len(refs[:-1]) // chunks
    body = shard * width
    mass = sum(both_halves(r[body:]) for r in refs[:count])
    scale = BLEND / jnp.sqrt(mass)
    seeds = seed_ref[...]
    for t in range(shard):
        span = slice(t * width, (t + 1) * width)
        parts = []
        for k in range(chunks):
            total = refs[k * count][span, :].astype(jnp.float32)
            for r in refs[k * count + 1 : (k + 1) * count]:
                total += r[span, :].astype(jnp.float32)
            parts.append(mix(total, scale, seeds, t, width, k * width))
        out_ref[t * 128 : (t + 1) * 128, :] = jnp.concatenate(parts, axis=0).T


def video_blend(seeds, pieces, width):
    shard = seeds.shape[0]
    flat = [p for chunk in pieces for p in chunk]
    return pl.pallas_call(
        functools.partial(video_kernel, chunks=len(pieces), width=width, shard=shard),
        out_shape=jax.ShapeDtypeStruct((shard * 128, 128), jnp.float32),
        in_specs=[VMEM] * (1 + len(flat)),
        out_specs=VMEM,
        compiler_params=params(48),
    )(seeds, *flat)


def partner(value, axis, mask):
    size = lax.axis_size(axis)
    return lax.ppermute(value, axis, [(i, i ^ mask) for i in range(size)])


def body(video_scores_in, audio_seed, video_seed, tile_values, tile_rows, tile_cols, tile_count):
    tiles = tile_values[0, 0]
    rows, cols = tile_rows[0, 0], tile_cols[0, 0]
    shard = video_scores_in.shape[0] // 128
    chunks, width = CHUNKS, 128 // CHUNKS
    n_row, n_col = lax.axis_size("row"), lax.axis_size("col")
    row_mask = lax.axis_index("row") * shard
    col_mask = lax.axis_index("col") * shard
    live = tile_count[0, 0]
    forward_info = jnp.stack([col_mask, row_mask, live]).astype(jnp.int32)
    reverse_info = jnp.stack([row_mask, col_mask, live]).astype(jnp.int32)
    audio_seeds = audio_seed.reshape(shard, 128)
    video_seeds = video_seed.reshape(shard, 128)

    panels = []
    for own in prep(video_scores_in, chunks):
        panels.append([own] + [partner(own, "row", m) for m in range(1, n_row)])
    halves, fulls, mass = [], [], None
    for k in range(chunks):
        first = k == 0
        keep, send = sweep(
            forward_info, rows, cols, tiles, panels[k], n_col * shard, 2, first, True, width
        )
        got = partner(send, "col", 1)
        own, *others = pair_sum(keep, got, first, shard * width)
        arrived = [partner(x, "col", 2 * (s + 1)) for s, x in enumerate(others)]
        half, full, mass = audio_blend(audio_seeds, own, arrived, mass, width, k * width)
        halves.append(half)
        fulls.append(full)
    results = []
    for k in range(chunks):
        mine = [halves[k]] + [partner(halves[k], "col", m) for m in range(2, n_col, 2)]
        pieces = [q for p in mine for q in (p, partner(p, "col", 1))]
        (sums,) = sweep(
            reverse_info, cols, rows, tiles, pieces, n_row * shard, 1, k == 0, False, width
        )
        results.append([sums[0]] + [partner(sums[m], "row", m) for m in range(1, n_row)])
    return flip(fulls), video_blend(video_seeds, results, width)


def solution(mesh):
    in_specs = (
        P(("col", "row"), None),
        P(("row", "col")),
        P(("col", "row")),
        P("row", "col", None, None, None),
        P("row", "col", None),
        P("row", "col", None),
        P("row", "col"),
    )
    out_specs = (P(("row", "col"), None), P(("col", "row"), None))
    return jax.shard_map(body, mesh=mesh, in_specs=in_specs, out_specs=out_specs, check_vma=False)
```

time: 358 us -> 119 us (0.33)
  the two profiles are of different devices: /device:TPU:0 before, /device:TPU:7 now
where the time goes in v1:
time: 119 us
  waiting for transfers between devices  57.3 us (48%)
  Pallas kernels  33.8 us (28%)
  starting transfers between devices  18.3 us (15%)
  local copies, waits for them, and re-layouts  4.31 us (4%)
  other arithmetic  3.86 us (3%)
  between operations  1.39 us (1%)
    ppermute x17, waiting for transfers between devices, partner(): return lax.ppermute(value, axis, [(i, i ^ mask) for i in range(size)])  57.3 us
    pallas_call x2, Pallas kernels, sweep(): pl.pallas_call(kernel, grid_spec=pltpu.PrefetchScalarGridSpec(num_scalar_...  29 us
    ppermute x17, starting transfers between devices, partner(): return lax.ppermute(value, axis, [(i, i ^ mask) for i in range(size)])  18.3 us
    unnamed x28, local copies, waits for them, and re-layouts  3.04 us
    unnamed x2, other arithmetic  2.55 us
  transfers between devices with their start and end apart: 17, of which 11 were waited for; matrix products, arithmetic and copies ran while one was open for 3% of the time, Pallas kernels for 1%

profile of v1, /device:TPU:7, one launch (start us, length us, event | category | flops | bytes accessed | tf_op | source)
XLA Modules:
  0.0 118.9 jit_solution(3485406784821245517)
XLA Ops:
  0.6 1.9 %shard_map.86.refs_0_ = bf16[1024,128]{1,0:T(8,128)(2,1)} custom-call(f32[1024,128]{1,0:T(8,128)} %video_ref.1), custom_call_target="tpu_custom_call" | custom-call | tf_op jit(solution)/shard_map/pallas_call | solution.py:43
  2.5 3.3 %collective-permute-start.2 = (bf16[1024,128]{1,0:T(8,128)(2,1)}, bf16[1024,128]{1,0:T(8,128)(2,1)S(1)}, u32[]{:S(2)}, u32[]{:S(2)}) collective-permute-start(bf16[1024,128]{1,0:T(8,128)(2,1)} %shard_map.86.refs_0_), channel_id=1, source_target_pairs={{0,24},{8,16},{16,8},{24,0},{1,25},{9,17},{17,9},{25,1},{2,26},{10... | collective-permute-start | bytes 786440 | tf_op jit(solution)/shard_map/ppermute | solution.py:291
  5.8 0.0 collective-permute-start.1
  5.8 0.3 collective-permute-start
  6.8 1.3 %reduce.to_ids.from_ids = s32[320]{0:T(512)} reduce(s32[1,1,320]{2,1,0:T(1,128)} %param.11, s32[]{:T(128)} %constant.14), dimensions={0,1}, to_apply=%param.11.reduce_sub_computation | reduce | bytes 2564 | tf_op args[4]
  8.0 1.3 %reduce.1.from_ids.to_ids = s32[320]{0:T(512)} reduce(s32[1,1,320]{2,1,0:T(1,128)} %param.12, s32[]{:T(128)} %constant.14), dimensions={0,1}, to_apply=%param.12.reduce_sub_computation | reduce | bytes 2564 | tf_op args[5]
  9.3 0.6 add_add_fusion.info
  10.0 2.0 %collective-permute-done.2.refs_3_ = bf16[1024,128]{1,0:T(8,128)(2,1)S(1)} collective-permute-done((bf16[1024,128]{1,0:T(8,128)(2,1)}, bf16[1024,128]{1,0:T(8,128)(2,1)S(1)}, u32[]{:S(2)}, u32[]{:S(2)}) %collective-permute-start.2) | collective-permute-done | bytes 262176 | tf_op jit(solution)/shard_map/ppermute | solution.py:291
  12.0 0.0 copy-start.8
  12.0 16.0 %collective-permute-done.1.refs_2_ = bf16[1024,128]{1,0:T(8,128)(2,1)S(1)} collective-permute-done((bf16[1024,128]{1,0:T(8,128)(2,1)}, bf16[1024,128]{1,0:T(8,128)(2,1)S(1)}, u32[]{:S(2)}, u32[]{:S(2)}) %collective-permute-start.1) | collective-permute-done | bytes 262176 | tf_op jit(solution)/shard_map/ppermute | solution.py:291
  28.0 0.0 collective-permute-done.refs_1_
  28.0 0.0 copy-start.11
  28.0 0.0 copy-done.8
  28.0 0.7 copy-done.9
  28.7 0.1 copy-done.11
  28.7 14.6 %shard_map.87 = (bf16[4,1040,128]{2,1,0:T(8,128)(2,1)}, bf16[4,1040,128]{2,1,0:T(8,128)(2,1)}) custom-call(s32[3]{0:T(128)} %add_add_fusion.info, s32[320]{0:T(512)} %reduce.to_ids.from_ids, s32[320]{0:T(512)} %reduce.1.from_ids.to_ids, bf16[320,128,128]{2,1,0:T(8,128)(2,1)} %bitcast.18, bf16[1024,128]{1,0:T(8,128)(2,1)} %shard_map.86.refs_0_, ...), custom_call_target="tpu_custom_call" | custom-call | tf_op jit(solution)/shard_map/pallas_call | solution.py:137
  43.3 0.0 collective-permute-start.3
  43.3 2.9 %collective-permute-done.3.got_ref = bf16[4,1040,128]{2,1,0:T(8,128)(2,1)S(1)} collective-permute-done((bf16[4,1040,128]{2,1,0:T(8,128)(2,1)}, bf16[4,1040,128]{2,1,0:T(8,128)(2,1)S(1)}, u32[]{:S(2)}, u32[]{:S(2)}) %collective-permute-start.3) | collective-permute-done | bytes 1064992 | tf_op jit(solution)/shard_map/ppermute | solution.py:291
  46.2 0.0 copy-start
  46.2 1.2 %copy-done = bf16[4,1040,128]{2,1,0:T(8,128)(2,1)S(1)} copy-done((bf16[4,1040,128]{2,1,0:T(8,128)(2,1)S(1)}, bf16[4,1040,128]{2,1,0:T(8,128)(2,1)}, u32[]{:S(2)}) %copy-start) | copy-done | bytes 1064984
  47.4 0.2 shard_map.88
  47.7 0.1 collective-permute-start.4
  47.7 0.1 collective-permute-start.5
  47.8 2.6 %collective-permute-start.6 = (bf16[1040,128]{1,0:T(8,128)(2,1)S(1)}, bf16[1040,128]{1,0:T(8,128)(2,1)S(1)}, u32[]{:S(2)}, u32[]{:S(2)}) collective-permute-start(bf16[1040,128]{1,0:T(8,128)(2,1)S(1)} %get-tuple-element.15), channel_id=1, source_target_pairs={{0,6},{1,7},{2,4},{3,5},{4,2},{5,3},{6,0},{7,1},{8,14},{9,15},{10,... | collective-permute-start | bytes 798728 | tf_op jit(solution)/shard_map/ppermute | solution.py:291
  50.4 5.2 %collective-permute-done.4.refs_0_ = bf16[1040,128]{1,0:T(8,128)(2,1)S(1)} collective-permute-done((bf16[1040,128]{1,0:T(8,128)(2,1)S(1)}, bf16[1040,128]{1,0:T(8,128)(2,1)S(1)}, u32[]{:S(2)}, u32[]{:S(2)}) %collective-permute-start.4) | collective-permute-done | bytes 266272 | tf_op jit(solution)/shard_map/ppermute | solution.py:291
  55.6 5.8 %collective-permute-done.5.refs_1_ = bf16[1040,128]{1,0:T(8,128)(2,1)S(1)} collective-permute-done((bf16[1040,128]{1,0:T(8,128)(2,1)S(1)}, bf16[1040,128]{1,0:T(8,128)(2,1)S(1)}, u32[]{:S(2)}, u32[]{:S(2)}) %collective-permute-start.5) | collective-permute-done | bytes 266272 | tf_op jit(solution)/shard_map/ppermute | solution.py:291
  61.4 0.0 collective-permute-done.6.refs_2_
  61.4 0.0 copy-done.2
  61.4 0.6 shard_map.89
  62.0 1.1 collective-permute-start.12
  63.1 1.1 collective-permute-start.10
  64.3 0.4 collective-permute-start.8
  64.7 1.8 %collective-permute-start.7 = (bf16[1024,128]{1,0:T(8,128)(2,1)S(1)}, bf16[1024,128]{1,0:T(8,128)(2,1)S(1)}, u32[]{:S(2)}, u32[]{:S(2)}) collective-permute-start(bf16[1024,128]{1,0:T(8,128)(2,1)S(1)} %get-tuple-element.17.refs_0_), channel_id=1, source_target_pairs={{0,1},{1,0},{2,3},{3,2},{4,5},{5,4},{6,7},{7,6},{8,9},{9,8},{10,11... | collective-permute-start | bytes 786440 | tf_op jit(solution)/shard_map/ppermute | solution.py:291
  66.5 3.4 %collective-permute-done.12.refs_6_ = bf16[1024,128]{1,0:T(8,128)(2,1)S(1)} collective-permute-done((bf16[1024,128]{1,0:T(8,128)(2,1)S(1)}, bf16[1024,128]{1,0:T(8,128)(2,1)S(1)}, u32[]{:S(2)}, u32[]{:S(2)}) %collective-permute-start.12) | collective-permute-done | bytes 262176 | tf_op jit(solution)/shard_map/ppermute | solution.py:291
  69.8 3.3 %collective-permute-start.13 = (bf16[1024,128]{1,0:T(8,128)(2,1)S(1)}, bf16[1024,128]{1,0:T(8,128)(2,1)S(1)}, u32[]{:S(2)}, u32[]{:S(2)}) collective-permute-start(bf16[1024,128]{1,0:T(8,128)(2,1)S(1)} %collective-permute-done.12.refs_6_), channel_id=1, source_target_pairs={{0,1},{1,0},{2,3},{3,2},{4,5},{5,4},{6,7},{7,6},{8,9},{9,8},{10,11... | collective-permute-start | bytes 786440 | tf_op jit(solution)/shard_map/ppermute | solution.py:291
  73.1 3.6 %collective-permute-done.10.refs_4_ = bf16[1024,128]{1,0:T(8,128)(2,1)S(1)} collective-permute-done((bf16[1024,128]{1,0:T(8,128)(2,1)S(1)}, bf16[1024,128]{1,0:T(8,128)(2,1)S(1)}, u32[]{:S(2)}, u32[]{:S(2)}) %collective-permute-start.10) | collective-permute-done | bytes 262176 | tf_op jit(solution)/shard_map/ppermute | solution.py:291
  76.8 0.5 collective-permute-start.11
  77.3 0.0 collective-permute-done.8.refs_2_
  77.3 0.1 collective-permute-start.9
  77.3 0.7 add_add_fusion.1.info
  78.0 0.0 collective-permute-done.7.refs_1_
  78.0 0.0 collective-permute-done.13.refs_7_
  78.0 0.0 copy-start.10
  78.0 0.4 collective-permute-done.11.refs_5_
  78.4 0.4 collective-permute-done.9.refs_3_
  78.8 0.0 copy-done.1
  78.8 0.0 copy-done.4
  78.8 0.0 copy-done.5
  78.8 0.0 copy-done.6
  78.8 0.0 copy-done.7
  78.8 0.0 copy-done.10
  78.8 0.3 copy-done.12
  79.1 0.7 copy-done.13
  79.8 14.4 %shard_map.91 = bf16[4,1040,128]{2,1,0:T(8,128)(2,1)} custom-call(s32[3]{0:T(128)} %add_add_fusion.1.info, s32[320]{0:T(512)} %reduce.1.from_ids.to_ids, s32[320]{0:T(512)} %reduce.to_ids.from_ids, bf16[320,128,128]{2,1,0:T(8,128)(2,1)} %bitcast.19, bf16[1024,128]{1,0:T(8,128)(2,1)} %copy-done.1, bf16[1024,128]{1,0:T(8,128)(2,1)} %copy-done.7, ...), custom_call_target="tpu_custom_call" | custom-call | tf_op jit(solution)/shard_map/pallas_call | solution.py:137
  94.3 1.3 %slice_bitcast_fusion = (bf16[1040,128]{1,0:T(8,128)(2,1)S(1)}, bf16[1040,128]{1,0:T(8,128)(2,1)S(1)}, bf16[1040,128]{1,0:T(8,128)(2,1)S(1)}, bf16[1040,128]{1,0:T(8,128)(2,1)S(1)}) fusion(bf16[4,1040,128]{2,1,0:T(8,128)(2,1)} %shard_map.91), kind=kLoop, calls=%fused_computation | loop fusion | bytes 2129920 | tf_op jit(solution)/shard_map/squeeze | solution.py:330
  95.5 0.1 collective-permute-start.16
  95.6 0.1 collective-permute-start.15
  95.7 3.5 %collective-permute-start.14 = (bf16[1040,128]{1,0:T(8,128)(2,1)S(1)}, bf16[1040,128]{1,0:T(8,128)(2,1)S(1)}, u32[]{:S(2)}, u32[]{:S(2)}) collective-permute-start(bf16[1040,128]{1,0:T(8,128)(2,1)S(1)} %get-tuple-element.20), channel_id=1, source_target_pairs={{0,8},{8,0},{16,24},{24,16},{1,9},{9,1},{17,25},{25,17},{2,10},{10... | collective-permute-start | bytes 798728 | tf_op jit(solution)/shard_map/ppermute | solution.py:291
  99.2 1.0 shard_map.90
  100.1 5.4 %collective-permute-done.16.refs_3_ = bf16[1040,128]{1,0:T(8,128)(2,1)S(1)} collective-permute-done((bf16[1040,128]{1,0:T(8,128)(2,1)S(1)}, bf16[1040,128]{1,0:T(8,128)(2,1)S(1)}, u32[]{:S(2)}, u32[]{:S(2)}) %collective-permute-start.16) | collective-permute-done | bytes 266272 | tf_op jit(solution)/shard_map/ppermute | solution.py:291
  105.6 12.2 %collective-permute-done.15.refs_2_ = bf16[1040,128]{1,0:T(8,128)(2,1)S(1)} collective-permute-done((bf16[1040,128]{1,0:T(8,128)(2,1)S(1)}, bf16[1040,128]{1,0:T(8,128)(2,1)S(1)}, u32[]{:S(2)}, u32[]{:S(2)}) %collective-permute-start.15) | collective-permute-done | bytes 266272 | tf_op jit(solution)/shard_map/ppermute | solution.py:291
  117.8 0.0 collective-permute-done.14.refs_1_
  117.8 0.0 copy-done.3
  117.8 1.1 shard_map.92
  (10 shorter events, 0.0 us)
Async XLA Ops:
  2.5 9.4 %collective-permute-start.2 = (bf16[1024,128]{1,0:T(8,128)(2,1)}, bf16[1024,128]{1,0:T(8,128)(2,1)S(1)}, u32[]{:S(2)}, u32[]{:S(2)}) collective-permute-start(bf16[1024,128]{1,0:T(8,128)(2,1)} %shard_map.86.refs_0_), channel_id=1, source_target_pairs={{0,24},{8,16},{16,8},{24,0},{1,25},{9,17},{17,9},{25,1},{2,26},{10... | collective-permute-start | bytes 786440 | tf_op jit(solution)/shard_map/ppermute | solution.py:291
  5.8 22.1 %collective-permute-start.1 = (bf16[1024,128]{1,0:T(8,128)(2,1)}, bf16[1024,128]{1,0:T(8,128)(2,1)S(1)}, u32[]{:S(2)}, u32[]{:S(2)}) collective-permute-start(bf16[1024,128]{1,0:T(8,128)(2,1)} %shard_map.86.refs_0_), channel_id=1, source_target_pairs={{0,16},{8,24},{16,0},{24,8},{1,17},{9,25},{17,1},{25,9},{2,18},{10... | collective-permute-start | bytes 786440 | tf_op jit(solution)/shard_map/ppermute | solution.py:291
  5.8 22.1 %collective-permute-start = (bf16[1024,128]{1,0:T(8,128)(2,1)}, bf16[1024,128]{1,0:T(8,128)(2,1)S(1)}, u32[]{:S(2)}, u32[]{:S(2)}) collective-permute-start(bf16[1024,128]{1,0:T(8,128)(2,1)} %shard_map.86.refs_0_), channel_id=1, source_target_pairs={{0,8},{8,0},{16,24},{24,16},{1,9},{9,1},{17,25},{25,17},{2,10},{10... | collective-permute-start | bytes 786440 | tf_op jit(solution)/shard_map/ppermute | solution.py:291
  12.0 16.0 %copy-start.8 = (bf16[1024,128]{1,0:T(8,128)(2,1)}, bf16[1024,128]{1,0:T(8,128)(2,1)S(1)}, u32[]{:S(2)}) copy-start(bf16[1024,128]{1,0:T(8,128)(2,1)S(1)} %collective-permute-done.2.refs_3_) | copy-start | bytes 786436
  27.9 0.7 copy-start.9
  28.0 0.8 copy-start.11
  43.3 2.9 %collective-permute-start.3 = (bf16[4,1040,128]{2,1,0:T(8,128)(2,1)}, bf16[4,1040,128]{2,1,0:T(8,128)(2,1)S(1)}, u32[]{:S(2)}, u32[]{:S(2)}) collective-permute-start(bf16[4,1040,128]{2,1,0:T(8,128)(2,1)} %get-tuple-element.11), channel_id=1, source_target_pairs={{0,1},{1,0},{2,3},{3,2},{4,5},{5,4},{6,7},{7,6},{8,9},{9,8},{10,11... | collective-permute-start | bytes 3194888 | tf_op jit(solution)/shard_map/ppermute | solution.py:291
  46.2 1.2 %copy-start = (bf16[4,1040,128]{2,1,0:T(8,128)(2,1)S(1)}, bf16[4,1040,128]{2,1,0:T(8,128)(2,1)}, u32[]{:S(2)}) copy-start(bf16[4,1040,128]{2,1,0:T(8,128)(2,1)} %get-tuple-element.10.keep_ref) | copy-start | bytes 3194884
  47.4 14.0 %copy-start.2 = (s32[1024]{0:T(1024)S(1)}, s32[1024]{0:T(1024)}, u32[]{:S(2)}) copy-start(s32[1024]{0:T(1024)} %param.8) | copy-start | bytes 12292
  47.7 7.9 %collective-permute-start.4 = (bf16[1040,128]{1,0:T(8,128)(2,1)S(1)}, bf16[1040,128]{1,0:T(8,128)(2,1)S(1)}, u32[]{:S(2)}, u32[]{:S(2)}) collective-permute-start(bf16[1040,128]{1,0:T(8,128)(2,1)S(1)} %get-tuple-element.13), channel_id=1, source_target_pairs={{0,2},{1,3},{2,0},{3,1},{4,6},{5,7},{6,4},{7,5},{8,10},{9,11},{10,... | collective-permute-start | bytes 798728 | tf_op jit(solution)/shard_map/ppermute | solution.py:291
  47.7 13.6 %collective-permute-start.5 = (bf16[1040,128]{1,0:T(8,128)(2,1)S(1)}, bf16[1040,128]{1,0:T(8,128)(2,1)S(1)}, u32[]{:S(2)}, u32[]{:S(2)}) collective-permute-start(bf16[1040,128]{1,0:T(8,128)(2,1)S(1)} %get-tuple-element.14), channel_id=1, source_target_pairs={{0,4},{1,5},{2,6},{3,7},{4,0},{5,1},{6,2},{7,3},{8,12},{9,13},{10,... | collective-permute-start | bytes 798728 | tf_op jit(solution)/shard_map/ppermute | solution.py:291
  47.8 13.5 %collective-permute-start.6 = (bf16[1040,128]{1,0:T(8,128)(2,1)S(1)}, bf16[1040,128]{1,0:T(8,128)(2,1)S(1)}, u32[]{:S(2)}, u32[]{:S(2)}) collective-permute-start(bf16[1040,128]{1,0:T(8,128)(2,1)S(1)} %get-tuple-element.15), channel_id=1, source_target_pairs={{0,6},{1,7},{2,4},{3,5},{4,2},{5,3},{6,0},{7,1},{8,14},{9,15},{10,... | collective-permute-start | bytes 798728 | tf_op jit(solution)/shard_map/ppermute | solution.py:291
  62.0 16.8 %copy-start.1 = (bf16[1024,128]{1,0:T(8,128)(2,1)}, bf16[1024,128]{1,0:T(8,128)(2,1)S(1)}, u32[]{:S(2)}) copy-start(bf16[1024,128]{1,0:T(8,128)(2,1)S(1)} %get-tuple-element.17.refs_0_) | copy-start | bytes 786436
  62.0 7.8 %collective-permute-start.12 = (bf16[1024,128]{1,0:T(8,128)(2,1)S(1)}, bf16[1024,128]{1,0:T(8,128)(2,1)S(1)}, u32[]{:S(2)}, u32[]{:S(2)}) collective-permute-start(bf16[1024,128]{1,0:T(8,128)(2,1)S(1)} %get-tuple-element.17.refs_0_), channel_id=1, source_target_pairs={{0,6},{1,7},{2,4},{3,5},{4,2},{5,3},{6,0},{7,1},{8,14},{9,15},{10,... | collective-permute-start | bytes 786440 | tf_op jit(solution)/shard_map/ppermute | solution.py:291
  63.1 13.6 %collective-permute-start.10 = (bf16[1024,128]{1,0:T(8,128)(2,1)S(1)}, bf16[1024,128]{1,0:T(8,128)(2,1)S(1)}, u32[]{:S(2)}, u32[]{:S(2)}) collective-permute-start(bf16[1024,128]{1,0:T(8,128)(2,1)S(1)} %get-tuple-element.17.refs_0_), channel_id=1, source_target_pairs={{0,4},{1,5},{2,6},{3,7},{4,0},{5,1},{6,2},{7,3},{8,12},{9,13},{10,... | collective-permute-start | bytes 786440 | tf_op jit(solution)/shard_map/ppermute | solution.py:291
  64.3 13.0 %collective-permute-start.8 = (bf16[1024,128]{1,0:T(8,128)(2,1)S(1)}, bf16[1024,128]{1,0:T(8,128)(2,1)S(1)}, u32[]{:S(2)}, u32[]{:S(2)}) collective-permute-start(bf16[1024,128]{1,0:T(8,128)(2,1)S(1)} %get-tuple-element.17.refs_0_), channel_id=1, source_target_pairs={{0,2},{1,3},{2,0},{3,1},{4,6},{5,7},{6,4},{7,5},{8,10},{9,11},{10,... | collective-permute-start | bytes 786440 | tf_op jit(solution)/shard_map/ppermute | solution.py:291
  64.7 13.3 %collective-permute-start.7 = (bf16[1024,128]{1,0:T(8,128)(2,1)S(1)}, bf16[1024,128]{1,0:T(8,128)(2,1)S(1)}, u32[]{:S(2)}, u32[]{:S(2)}) collective-permute-start(bf16[1024,128]{1,0:T(8,128)(2,1)S(1)} %get-tuple-element.17.refs_0_), channel_id=1, source_target_pairs={{0,1},{1,0},{2,3},{3,2},{4,5},{5,4},{6,7},{7,6},{8,9},{9,8},{10,11... | collective-permute-start | bytes 786440 | tf_op jit(solution)/shard_map/ppermute | solution.py:291
  69.8 9.0 %copy-start.4 = (bf16[1024,128]{1,0:T(8,128)(2,1)}, bf16[1024,128]{1,0:T(8,128)(2,1)S(1)}, u32[]{:S(2)}) copy-start(bf16[1024,128]{1,0:T(8,128)(2,1)S(1)} %collective-permute-done.12.refs_6_) | copy-start | bytes 786436
  69.8 8.2 %collective-permute-start.13 = (bf16[1024,128]{1,0:T(8,128)(2,1)S(1)}, bf16[1024,128]{1,0:T(8,128)(2,1)S(1)}, u32[]{:S(2)}, u32[]{:S(2)}) collective-permute-start(bf16[1024,128]{1,0:T(8,128)(2,1)S(1)} %collective-permute-done.12.refs_6_), channel_id=1, source_target_pairs={{0,1},{1,0},{2,3},{3,2},{4,5},{5,4},{6,7},{7,6},{8,9},{9,8},{10,11... | collective-permute-start | bytes 786440 | tf_op jit(solution)/shard_map/ppermute | solution.py:291
  76.8 2.0 %copy-start.5 = (bf16[1024,128]{1,0:T(8,128)(2,1)}, bf16[1024,128]{1,0:T(8,128)(2,1)S(1)}, u32[]{:S(2)}) copy-start(bf16[1024,128]{1,0:T(8,128)(2,1)S(1)} %collective-permute-done.10.refs_4_) | copy-start | bytes 786436
  76.8 1.7 %collective-permute-start.11 = (bf16[1024,128]{1,0:T(8,128)(2,1)S(1)}, bf16[1024,128]{1,0:T(8,128)(2,1)S(1)}, u32[]{:S(2)}, u32[]{:S(2)}) collective-permute-start(bf16[1024,128]{1,0:T(8,128)(2,1)S(1)} %collective-permute-done.10.refs_4_), channel_id=1, source_target_pairs={{0,1},{1,0},{2,3},{3,2},{4,5},{5,4},{6,7},{7,6},{8,9},{9,8},{10,11... | collective-permute-start | bytes 786440 | tf_op jit(solution)/shard_map/ppermute | solution.py:291
  77.3 1.6 %copy-start.6 = (bf16[1024,128]{1,0:T(8,128)(2,1)}, bf16[1024,128]{1,0:T(8,128)(2,1)S(1)}, u32[]{:S(2)}) copy-start(bf16[1024,128]{1,0:T(8,128)(2,1)S(1)} %collective-permute-done.8.refs_2_) | copy-start | bytes 786436
  77.3 1.5 %collective-permute-start.9 = (bf16[1024,128]{1,0:T(8,128)(2,1)S(1)}, bf16[1024,128]{1,0:T(8,128)(2,1)S(1)}, u32[]{:S(2)}, u32[]{:S(2)}) collective-permute-start(bf16[1024,128]{1,0:T(8,128)(2,1)S(1)} %collective-permute-done.8.refs_2_), channel_id=1, source_target_pairs={{0,1},{1,0},{2,3},{3,2},{4,5},{5,4},{6,7},{7,6},{8,9},{9,8},{10,11... | collective-permute-start | bytes 786440 | tf_op jit(solution)/shard_map/ppermute | solution.py:291
  78.0 0.8 copy-start.7
  78.0 0.8 copy-start.10
  78.4 0.7 copy-start.12
  79.1 0.7 copy-start.13
  94.3 23.6 %copy-start.3 = (s32[1024]{0:T(1024)S(1)}, s32[1024]{0:T(1024)}, u32[]{:S(2)}) copy-start(s32[1024]{0:T(1024)} %param.9) | copy-start | bytes 12292
  95.5 10.0 %collective-permute-start.16 = (bf16[1040,128]{1,0:T(8,128)(2,1)S(1)}, bf16[1040,128]{1,0:T(8,128)(2,1)S(1)}, u32[]{:S(2)}, u32[]{:S(2)}) collective-permute-start(bf16[1040,128]{1,0:T(8,128)(2,1)S(1)} %get-tuple-element.18), channel_id=1, source_target_pairs={{0,24},{8,16},{16,8},{24,0},{1,25},{9,17},{17,9},{25,1},{2,26},{10... | collective-permute-start | bytes 798728 | tf_op jit(solution)/shard_map/ppermute | solution.py:291
  95.6 22.2 %collective-permute-start.15 = (bf16[1040,128]{1,0:T(8,128)(2,1)S(1)}, bf16[1040,128]{1,0:T(8,128)(2,1)S(1)}, u32[]{:S(2)}, u32[]{:S(2)}) collective-permute-start(bf16[1040,128]{1,0:T(8,128)(2,1)S(1)} %get-tuple-element.19), channel_id=1, source_target_pairs={{0,16},{8,24},{16,0},{24,8},{1,17},{9,25},{17,1},{25,9},{2,18},{10... | collective-permute-start | bytes 798728 | tf_op jit(solution)/shard_map/ppermute | solution.py:291
  95.7 22.1 %collective-permute-start.14 = (bf16[1040,128]{1,0:T(8,128)(2,1)S(1)}, bf16[1040,128]{1,0:T(8,128)(2,1)S(1)}, u32[]{:S(2)}, u32[]{:S(2)}) collective-permute-start(bf16[1040,128]{1,0:T(8,128)(2,1)S(1)} %get-tuple-element.20), channel_id=1, source_target_pairs={{0,8},{8,0},{16,24},{24,16},{1,9},{9,1},{17,25},{25,17},{2,10},{10... | collective-permute-start | bytes 798728 | tf_op jit(solution)/shard_map/ppermute | solution.py:291

commit v2 on v1

v2 whole, which is shorter than its diff:
```python
import functools

import jax
import jax.numpy as jnp
from jax import lax
from jax.experimental import pallas as pl
from jax.experimental.pallas import tpu as pltpu
from jax.sharding import PartitionSpec as P

BLEND = 0.75
GROUP = 16
LIMIT = 40
PLACE = 8
VMEM = pl.BlockSpec(memory_space=pltpu.VMEM)
NT = (((1,), (1,)), ((), ()))
NN = (((1,), (0,)), ((), ()))


def params(mib):
    return pltpu.CompilerParams(vmem_limit_bytes=mib * 2**20)


def split_half(mass):
    high = mass.astype(jnp.bfloat16)
    low = (mass - high.astype(jnp.float32)).astype(jnp.bfloat16)
    return jnp.concatenate([high.astype(jnp.float32), low.astype(jnp.float32)], axis=0).astype(
        jnp.bfloat16
    )


def prep_kernel(video_ref, *out_refs):
    tiles = video_ref.shape[0] // 128
    width = out_refs[0].shape[0] // tiles
    for t in range(tiles):
        flipped = video_ref[t * 128 : (t + 1) * 128, :].T.astype(jnp.bfloat16)
        for k, out_ref in enumerate(out_refs):
            out_ref[t * width : (t + 1) * width, :] = flipped[k * width : (k + 1) * width, :]


def prep(video, chunks):
    rows, classes = video.shape
    width = classes // chunks
    shape = jax.ShapeDtypeStruct((rows // 128 * width, 128), jnp.bfloat16)
    return pl.pallas_call(
        prep_kernel, out_shape=[shape] * chunks, in_specs=[VMEM], out_specs=[VMEM] * chunks
    )(video)


def plan_kernel(rows, cols, live_ref, forward_ref, reverse_ref, counts, *, cap, half, shard):
    row_mask, col_mask = lax.axis_index("row") * shard, lax.axis_index("col") * shard
    live = live_ref[0, 0]
    trash = 2 * cap

    def place(block, carry):
        early, late, far, near = carry
        base = block * PLACE
        found = [(rows[0, 0, base + k], cols[0, 0, base + k]) for k in range(PLACE)]
        for k, (row, col) in enumerate(found):
            slot = base + k
            row, col = row ^ col_mask, col ^ row_mask
            high = (col >= half).astype(jnp.int32)
            local = col - high * half
            there = jnp.where(high == 1, cap + late, early)
            back = jnp.where(high == 1, far, cap + near)
            forward = slot | (local << 12) | (row << 20)
            reverse = slot | (row << 12) | (local << 20)
            used = slot < live
            forward_ref[jnp.where(used, there, trash)] = forward
            reverse_ref[jnp.where(used, back, trash)] = reverse
            low = used.astype(jnp.int32) * (1 - high)
            high = used.astype(jnp.int32) * high
            early, late, far, near = early + low, late + high, far + high, near + low
        return early, late, far, near

    zero = jnp.int32(0)
    blocks = lax.div(live + (PLACE - 1), PLACE)
    early, late, far, near = lax.fori_loop(0, blocks, place, (zero, zero, zero, zero))
    counts[0] = early
    counts[1] = late
    counts[2] = far
    counts[3] = near
    counts[4] = live
    row_dummy = (lax.axis_size("col") * shard) << 20
    col_dummy = half << 20

    def pad(n, carry):
        forward_ref[early + n] = row_dummy
        forward_ref[cap + late + n] = row_dummy
        reverse_ref[far + n] = col_dummy
        reverse_ref[cap + near + n] = col_dummy
        return carry

    lax.fori_loop(0, GROUP, pad, 0)


def plan(rows, cols, live, col_tiles, shard):
    cap = rows.shape[2] + GROUP
    smem = pl.BlockSpec(memory_space=pltpu.SMEM)
    codes = jax.ShapeDtypeStruct((2 * cap + 128,), jnp.int32)
    return pl.pallas_call(
        functools.partial(plan_kernel, cap=cap, half=col_tiles // 2, shard=shard),
        out_shape=[codes, codes, jax.ShapeDtypeStruct((8,), jnp.int32)],
        in_specs=[smem] * 3,
        out_specs=[smem] * 3,
    )(rows, cols, live)


def sweep_kernel(
    codes_ref, counts_ref, tiles_ref, *refs, pieces, carried, kind, outs, first, count_at,
    transposed, shard,
):
    piece_refs = refs[:pieces]
    carry_refs = refs[pieces : pieces + carried]
    out_refs = refs[pieces + carried : pieces + carried + outs]
    codes, counts, panel, acc, mass, slots, code_sem, sems = refs[pieces + carried + outs :]
    width = acc.shape[1]
    dummy = acc.shape[0] - 1
    plans = [
        pltpu.make_async_copy(counts_ref, counts, code_sem.at[0]),
        pltpu.make_async_copy(codes_ref, codes, code_sem.at[1]),
    ]
    for copy in plans:
        copy.start()

    def block(b):
        span = pl.ds(b * GROUP, GROUP)
        return pltpu.make_async_copy(tiles_ref.at[span], slots.at[span], sems.at[b])

    def begin(b, carry):
        block(b).start()
        return carry

    def settle(b, carry):
        block(b).wait()
        return carry

    plans[0].wait()
    blocks = lax.div(counts[4] + (GROUP - 1), GROUP)
    lax.fori_loop(0, blocks, begin, 0)
    for m, piece in enumerate(piece_refs):
        for t in range(shard):
            panel[m * shard + t, :width, :] = piece[t * width : (t + 1) * width, :]

    def ones(n, carry):
        panel[n, width:, :] = jnp.ones((16, 128), jnp.bfloat16)
        return carry

    def clear(n, carry):
        acc[n] = jnp.zeros((width, 128), jnp.float32)
        mass[n] = jnp.zeros((8, 128), jnp.float32)
        return carry

    lax.fori_loop(0, panel.shape[0], ones, 0)
    lax.fori_loop(0, dummy, clear, 0)
    plans[1].wait()
    count = counts[count_at]

    def work(g, settled):
        last = jnp.minimum(g * GROUP + (GROUP - 1), count - 1)
        need = lax.div(codes[first + last] & 0xFFF, GROUP) + 1
        lax.fori_loop(settled, need, settle, 0)
        for k in range(GROUP):
            code = codes[first + g * GROUP + k]
            to = lax.shift_right_logical(code, 20)
            product = lax.dot_general(
                panel[lax.shift_right_logical(code, 12) & 0xFF],
                slots[code & 0xFFF],
                NT if transposed else NN,
                preferred_element_type=jnp.float32,
            )
            acc[to] += product[:width]
            mass[to] += product[width : width + 8]
        return jnp.maximum(settled, need)

    groups = lax.div(count + (GROUP - 1), GROUP)
    settled = lax.fori_loop(0, groups, work, jnp.int32(0))
    lax.fori_loop(settled, blocks, settle, 0)

    if kind == "sums":

        def hand(n, carry):
            out_refs[0][n] = acc[n]
            out_refs[1][n] = mass[n]
            return carry

        lax.fori_loop(0, dummy, hand, 0)
        return
    for n in range(dummy // shard):
        target = out_refs[n] if kind == "each" else out_refs[n % outs].at[n // outs]
        tops = []
        for t in range(shard):
            tile, top = acc[n * shard + t], mass[n * shard + t, 0:1, :]
            if carried:
                tile += carry_refs[0][n * shard + t]
                top += carry_refs[1][n * shard + t, 0:1, :]
            target[t * width : (t + 1) * width, :] = tile.astype(jnp.bfloat16)
            tops.append(top)
        target[shard * width :, :] = split_half(jnp.concatenate(tops, axis=0))


def sweep(
    plan_codes, counts, at, count_at, tiles, pieces, carry, to_tiles, shard, kind, transposed
):
    width = pieces[0].shape[0] // shard
    rows = shard * width + 2 * shard
    shards = to_tiles // shard
    if kind == "sums":
        out_shape = [
            jax.ShapeDtypeStruct((to_tiles, width, 128), jnp.float32),
            jax.ShapeDtypeStruct((to_tiles, 8, 128), jnp.float32),
        ]
    elif kind == "pairs":
        out_shape = [jax.ShapeDtypeStruct((shards // 2, rows, 128), jnp.bfloat16)] * 2
    else:
        out_shape = [jax.ShapeDtypeStruct((rows, 128), jnp.bfloat16)] * shards
    slots = tiles.shape[0]
    average = slots // 4
    any_space = pl.BlockSpec(memory_space=pl.ANY)
    return pl.pallas_call(
        functools.partial(
            sweep_kernel,
            pieces=len(pieces),
            carried=len(carry),
            kind=kind,
            outs=len(out_shape),
            first=at * (slots + GROUP),
            count_at=count_at,
            transposed=transposed,
            shard=shard,
        ),
        in_specs=[any_space] * 3 + [VMEM] * (len(pieces) + len(carry)),
        out_specs=[VMEM] * len(out_shape),
        scratch_shapes=[
            pltpu.SMEM(plan_codes.shape, jnp.int32),
            pltpu.SMEM(counts.shape, jnp.int32),
            pltpu.VMEM((len(pieces) * shard, width + 16, 128), jnp.bfloat16),
            pltpu.VMEM((to_tiles + 1, width, 128), jnp.float32),
            pltpu.VMEM((to_tiles + 1, 8, 128), jnp.float32),
            pltpu.VMEM((slots, 128, 128), jnp.bfloat16),
            pltpu.SemaphoreType.DMA((2,)),
            pltpu.SemaphoreType.DMA((slots // GROUP,)),
        ],
        out_shape=out_shape,
        compiler_params=params(LIMIT),
        cost_estimate=pl.CostEstimate(
            flops=2 * average * 128 * 128 * width * 8,
            bytes_accessed=average * 128 * 128 * 2,
            transcendentals=0,
        ),
    )(plan_codes, counts, tiles, *pieces, *carry)


def pair_sum_kernel(keep_ref, got_ref, *out_refs, body_rows):
    for s in list(range(1, len(out_refs))) + [0]:
        out_ref = out_refs[s]
        total = keep_ref[s, :body_rows].astype(jnp.float32)
        total += got_ref[s, :body_rows].astype(jnp.float32)
        mass = both_halves(keep_ref[s, body_rows:]) + both_halves(got_ref[s, body_rows:])
        out_ref[:body_rows, :] = total.astype(out_ref.dtype)
        if s == 0:
            out_ref[body_rows:, :] = jnp.concatenate([mass, jnp.zeros_like(mass)], axis=0)
        else:
            out_ref[body_rows:, :] = split_half(mass)


def both_halves(block):
    wide = block.astype(jnp.float32)
    half = wide.shape[0] // 2
    return wide[:half] + wide[half:]


def pair_sum(keep, got, body_rows):
    count, rows, _ = keep.shape
    shapes = [
        jax.ShapeDtypeStruct((rows, 128), jnp.float32 if s == 0 else jnp.bfloat16)
        for s in range(count)
    ]
    return pl.pallas_call(
        functools.partial(pair_sum_kernel, body_rows=body_rows),
        out_shape=shapes,
        in_specs=[VMEM] * 2,
        out_specs=[VMEM] * count,
        compiler_params=params(48),
    )(keep, got)


def mix(own, scale, seeds, t, width, first):
    classes = lax.broadcasted_iota(jnp.int32, (width, 128), 0) + first
    labels = jnp.where(classes == seeds[t : t + 1, :], 1.0 - BLEND, 0.0)
    return own * scale[t : t + 1, :] + labels


def audio_kernel(seed_ref, own_ref, *refs, width, shard, first, with_mass):
    refs = list(refs)
    half_ref, full_ref, mass_out = refs[-3:]
    mass_in = None if with_mass else refs[0]
    got = refs[:-3] if with_mass else refs[1:-3]
    body = shard * width
    if with_mass:
        mass = own_ref[body : body + shard, :]
        for g in got:
            mass += both_halves(g[body:])
    else:
        mass = mass_in[...]
    mass_out[...] = mass
    scale = BLEND / jnp.sqrt(mass)
    seeds = seed_ref[...]
    for t in range(shard):
        span = slice(t * width, (t + 1) * width)
        total = own_ref[span, :].astype(jnp.float32)
        for g in got:
            total += g[span, :].astype(jnp.float32)
        scores = mix(total, scale, seeds, t, width, first)
        half_ref[span, :] = scores.astype(jnp.bfloat16)
        full_ref[span, :] = scores


def audio_blend(seeds, own, got, mass, width, first):
    shard = seeds.shape[0]
    args = [seeds, own] + ([] if mass is None else [mass]) + list(got)
    return pl.pallas_call(
        functools.partial(
            audio_kernel, width=width, shard=shard, first=first, with_mass=mass is None
        ),
        out_shape=[
            jax.ShapeDtypeStruct((shard * width, 128), jnp.bfloat16),
            jax.ShapeDtypeStruct((shard * width, 128), jnp.float32),
            jax.ShapeDtypeStruct((shard, 128), jnp.float32),
        ],
        in_specs=[VMEM] * len(args),
        out_specs=[VMEM] * 3,
        compiler_params=params(48),
    )(*args)


def flip_kernel(*refs):
    out_ref = refs[-1]
    width = 128 // (len(refs) - 1)
    for t in range(out_ref.shape[0] // 128):
        parts = [r[t * width : (t + 1) * width, :] for r in refs[:-1]]
        out_ref[t * 128 : (t + 1) * 128, :] = jnp.concatenate(parts, axis=0).T


def flip(parts):
    rows = parts[0].shape[0] * len(parts)
    return pl.pallas_call(
        flip_kernel,
        out_shape=jax.ShapeDtypeStruct((rows, 128), jnp.float32),
        in_specs=[VMEM] * len(parts),
        out_specs=VMEM,
        compiler_params=params(48),
    )(*parts)


def video_kernel(seed_ref, *refs, chunks, width, shard):
    out_ref = refs[-1]
    count = len(refs[:-1]) // chunks
    body = shard * width
    mass = sum(both_halves(r[body:]) for r in refs[:count])
    scale = BLEND / jnp.sqrt(mass)
    seeds = seed_ref[...]
    for t in range(shard):
        span = slice(t * width, (t + 1) * width)
        parts = []
        for k in range(chunks):
            total = refs[k * count][span, :].astype(jnp.float32)
            for r in refs[k * count + 1 : (k + 1) * count]:
                total += r[span, :].astype(jnp.float32)
            parts.append(mix(total, scale, seeds, t, width, k * width))
        out_ref[t * 128 : (t + 1) * 128, :] = jnp.concatenate(parts, axis=0).T


def video_blend(seeds, pieces, width):
    shard = seeds.shape[0]
    flat = [p for chunk in pieces for p in chunk]
    return pl.pallas_call(
        functools.partial(video_kernel, chunks=len(pieces), width=width, shard=shard),
        out_shape=jax.ShapeDtypeStruct((shard * 128, 128), jnp.float32),
        in_specs=[VMEM] * (1 + len(flat)),
        out_specs=VMEM,
        compiler_params=params(48),
    )(seeds, *flat)


def partner(value, axis, mask):
    size = lax.axis_size(axis)
    return lax.ppermute(value, axis, [(i, i ^ mask) for i in range(size)])


def body(video_scores_in, audio_seed, video_seed, tile_values, tile_rows, tile_cols, tile_count):
    tiles = tile_values[0, 0]
    shard, width = video_scores_in.shape[0] // 128, 128
    n_row, n_col = lax.axis_size("row"), lax.axis_size("col")
    row_tiles, col_tiles = n_col * shard, n_row * shard
    audio_seeds = audio_seed.reshape(shard, 128)
    video_seeds = video_seed.reshape(shard, 128)

    (own,) = prep(video_scores_in, 1)
    panel = [own] + [partner(own, "row", m) for m in range(1, n_row)]
    forward, reverse, counts = plan(tile_rows, tile_cols, tile_count, col_tiles, shard)
    near, far = panel[: n_row // 2], panel[n_row // 2 :]
    carry = sweep(
        forward, counts, 0, 0, tiles, near, [], row_tiles, shard, "sums", True
    )
    keep, send = sweep(
        forward, counts, 1, 1, tiles, far, carry, row_tiles, shard, "pairs", True
    )
    got = partner(send, "col", 1)
    own, *others = pair_sum(keep, got, shard * width)
    arrived = [partner(x, "col", 2 * (s + 1)) for s, x in enumerate(others)]
    half, full, _ = audio_blend(audio_seeds, own, arrived, None, width, 0)

    mine = [half] + [partner(half, "col", m) for m in range(2, n_col, 2)]
    pieces = [q for p in mine for q in (p, partner(p, "col", 1))]
    far = sweep(reverse, counts, 0, 2, tiles, pieces, [], col_tiles // 2, shard, "each", False)
    near = sweep(reverse, counts, 1, 3, tiles, pieces, [], col_tiles // 2, shard, "each", False)
    sums = list(near) + list(far)
    results = [sums[0]] + [partner(sums[m], "row", m) for m in range(1, n_row)]
    return flip([full]), video_blend(video_seeds, [results], width)


def solution(mesh):
    in_specs = (
        P(("col", "row"), None),
        P(("row", "col")),
        P(("col", "row")),
        P("row", "col", None, None, None),
        P("row", "col", None),
        P("row", "col", None),
        P("row", "col"),
    )
    out_specs = (P(("row", "col"), None), P(("col", "row"), None))
    return jax.shard_map(body, mesh=mesh, in_specs=in_specs, out_specs=out_specs, check_vma=False)
```

time: 119 us -> 102 us (0.86)
  the two profiles are of different devices: /device:TPU:7 before, /device:TPU:0 now
where the time goes in v2:
time: 102 us; the launch traced here: 101 us
  waiting for transfers between devices  51 us (50%)
  Pallas kernels  26 us (25%)
  starting transfers between devices  19.8 us (19%)
  local copies, waits for them, and re-layouts  2.32 us (2%)
  between operations  1.41 us (1%)
    ppermute x17, waiting for transfers between devices, partner(): return lax.ppermute(value, axis, [(i, i ^ mask) for i in range(size)])  51 us
    ppermute x17, starting transfers between devices, partner(): return lax.ppermute(value, axis, [(i, i ^ mask) for i in range(size)])  19.8 us
    pallas_call x4, Pallas kernels, sweep(): pl.pallas_call(functools.partial(sweep_kernel, pieces=len(pieces), carrie...  18.1 us
    pallas_call x1, Pallas kernels, plan(): pl.pallas_call(functools.partial(plan_kernel, cap=cap, half=col_tiles //...  3.14 us
    unnamed x20, local copies, waits for them, and re-layouts  2.32 us
  transfers between devices with their start and end apart: 17, of which 12 were waited for; matrix products, arithmetic and copies ran while one was open for 0% of the time, Pallas kernels for 13%

profile of v2, /device:TPU:0, one launch (start us, length us, event | category | flops | bytes accessed | tf_op | source)
XLA Modules:
  0.0 100.6 jit_solution(6085288359892774702)
XLA Ops:
  0.6 1.9 %shard_map.87.refs_0_ = bf16[1024,128]{1,0:T(8,128)(2,1)} custom-call(f32[1024,128]{1,0:T(8,128)} %video_ref.1), custom_call_target="tpu_custom_call" | custom-call | tf_op jit(solution)/shard_map/pallas_call | solution.py:44
  2.5 3.0 %collective-permute-start.2 = (bf16[1024,128]{1,0:T(8,128)(2,1)}, bf16[1024,128]{1,0:T(8,128)(2,1)S(1)}, u32[]{:S(2)}, u32[]{:S(2)}) collective-permute-start(bf16[1024,128]{1,0:T(8,128)(2,1)} %shard_map.87.refs_0_), channel_id=1, source_target_pairs={{0,8},{8,0},{16,24},{24,16},{1,9},{9,1},{17,25},{25,17},{2,10},{10... | collective-permute-start | bytes 786440 | tf_op jit(solution)/shard_map/ppermute | solution.py:387
  5.5 2.5 %collective-permute-start.1 = (bf16[1024,128]{1,0:T(8,128)(2,1)}, bf16[1024,128]{1,0:T(8,128)(2,1)S(1)}, u32[]{:S(2)}, u32[]{:S(2)}) collective-permute-start(bf16[1024,128]{1,0:T(8,128)(2,1)} %shard_map.87.refs_0_), channel_id=1, source_target_pairs={{0,24},{8,16},{16,8},{24,0},{1,25},{9,17},{17,9},{25,1},{2,26},{10... | collective-permute-start | bytes 786440 | tf_op jit(solution)/shard_map/ppermute | solution.py:387
  8.0 0.1 collective-permute-start
  8.8 3.1 %shard_map.86 = (s32[800]{0:T(1024)}, s32[800]{0:T(1024)}, s32[8]{0:T(128)}) custom-call(s32[1,1,320]{2,1,0:T(1,128)} %rows.1, s32[1,1,320]{2,1,0:T(1,128)} %cols.1, s32[1,1]{1,0:T(1,128)S(6)} %copy.9.live_ref), custom_call_target="tpu_custom_call" | custom-call | tf_op jit(solution)/shard_map/pallas_call | solution.py:100
  11.9 0.6 collective-permute-done.2.refs_1_
  12.6 0.0 copy-start
  12.6 0.9 copy-done
  13.5 0.0 copy-start.1
  13.5 0.7 copy-done.1
  14.2 0.0 copy-start.3
  14.2 0.7 copy-done.3
  14.9 5.0 %shard_map.88 = (f32[64,128,128]{2,1,0:T(8,128)S(1)}, f32[64,8,128]{2,1,0:T(8,128)S(1)}) custom-call(s32[800]{0:T(1024)S(1)} %copy-done.1, s32[8]{0:T(128)S(1)} %copy-done.3, bf16[320,128,128]{2,1,0:T(8,128)(2,1)} %bitcast.3, bf16[1024,128]{1,0:T(8,128)(2,1)S(1)} %copy-done, bf16[1024,128]{1,0:T(8,128)(2,1)S(1)} %collective-permute-done.2.refs_1_), custom_call_target="tpu_custom_call" | custom-call | flops 2684354560 | bytes 2621440 | tf_op jit(solution)/shard_map/pallas_call | solution.py:219
  19.9 1.2 %collective-permute-done.1.refs_1_ = bf16[1024,128]{1,0:T(8,128)(2,1)S(1)} collective-permute-done((bf16[1024,128]{1,0:T(8,128)(2,1)}, bf16[1024,128]{1,0:T(8,128)(2,1)S(1)}, u32[]{:S(2)}, u32[]{:S(2)}) %collective-permute-start.1) | collective-permute-done | bytes 262176 | tf_op jit(solution)/shard_map/ppermute | solution.py:387
  21.1 10.1 %collective-permute-done.refs_0_ = bf16[1024,128]{1,0:T(8,128)(2,1)S(1)} collective-permute-done((bf16[1024,128]{1,0:T(8,128)(2,1)}, bf16[1024,128]{1,0:T(8,128)(2,1)S(1)}, u32[]{:S(2)}, u32[]{:S(2)}) %collective-permute-start) | collective-permute-done | bytes 262176 | tf_op jit(solution)/shard_map/ppermute | solution.py:387
  31.2 0.0 slice-start
  31.2 0.0 slice-start.1
  31.2 0.0 slice-start.2
  31.2 5.0 %shard_map.89 = (bf16[4,1040,128]{2,1,0:T(8,128)(2,1)S(1)}, bf16[4,1040,128]{2,1,0:T(8,128)(2,1)S(1)}) custom-call(s32[800]{0:T(1024)S(1)} %copy-done.1, s32[8]{0:T(128)S(1)} %copy-done.3, bf16[320,128,128]{2,1,0:T(8,128)(2,1)} %bitcast.4, bf16[1024,128]{1,0:T(8,128)(2,1)S(1)} %collective-permute-done.refs_0_, ...), custom_call_target="tpu_custom_call" | custom-call | flops 2684354560 | bytes 2621440 | tf_op jit(solution)/shard_map/pallas_call | solution.py:219
  36.2 0.1 collective-permute-start.3
  36.3 2.7 %collective-permute-done.3.got_ref = bf16[4,1040,128]{2,1,0:T(8,128)(2,1)S(1)} collective-permute-done((bf16[4,1040,128]{2,1,0:T(8,128)(2,1)S(1)}, bf16[4,1040,128]{2,1,0:T(8,128)(2,1)S(1)}, u32[]{:S(2)}, u32[]{:S(2)}) %collective-permute-start.3) | collective-permute-done | bytes 1064992 | tf_op jit(solution)/shard_map/ppermute | solution.py:387
  39.0 0.0 copy-start.5
  39.0 0.2 shard_map.90
  39.2 0.0 copy-start.2
  39.2 0.0 copy-start.4
  39.3 1.5 %collective-permute-start.4 = (bf16[1040,128]{1,0:T(8,128)(2,1)S(1)}, bf16[1040,128]{1,0:T(8,128)(2,1)S(1)}, u32[]{:S(2)}, u32[]{:S(2)}) collective-permute-start(bf16[1040,128]{1,0:T(8,128)(2,1)S(1)} %get-tuple-element.26), channel_id=1, source_target_pairs={{0,2},{1,3},{2,0},{3,1},{4,6},{5,7},{6,4},{7,5},{8,10},{9,11},{10,... | collective-permute-start | bytes 798728 | tf_op jit(solution)/shard_map/ppermute | solution.py:387
  40.8 1.0 %collective-permute-start.5 = (bf16[1040,128]{1,0:T(8,128)(2,1)S(1)}, bf16[1040,128]{1,0:T(8,128)(2,1)S(1)}, u32[]{:S(2)}, u32[]{:S(2)}) collective-permute-start(bf16[1040,128]{1,0:T(8,128)(2,1)S(1)} %get-tuple-element.27), channel_id=1, source_target_pairs={{0,4},{1,5},{2,6},{3,7},{4,0},{5,1},{6,2},{7,3},{8,12},{9,13},{10,... | collective-permute-start | bytes 798728 | tf_op jit(solution)/shard_map/ppermute | solution.py:387
  41.8 1.0 collective-permute-start.6
  42.8 5.7 %collective-permute-done.4.refs_0_ = bf16[1040,128]{1,0:T(8,128)(2,1)S(1)} collective-permute-done((bf16[1040,128]{1,0:T(8,128)(2,1)S(1)}, bf16[1040,128]{1,0:T(8,128)(2,1)S(1)}, u32[]{:S(2)}, u32[]{:S(2)}) %collective-permute-start.4) | collective-permute-done | bytes 266272 | tf_op jit(solution)/shard_map/ppermute | solution.py:387
  48.6 6.1 %collective-permute-done.5.refs_1_ = bf16[1040,128]{1,0:T(8,128)(2,1)S(1)} collective-permute-done((bf16[1040,128]{1,0:T(8,128)(2,1)S(1)}, bf16[1040,128]{1,0:T(8,128)(2,1)S(1)}, u32[]{:S(2)}, u32[]{:S(2)}) %collective-permute-start.5) | collective-permute-done | bytes 266272 | tf_op jit(solution)/shard_map/ppermute | solution.py:387
  54.7 0.0 collective-permute-done.6.refs_2_
  54.7 0.0 copy-done.5
  54.7 0.6 shard_map.91
  55.3 1.3 %collective-permute-start.12 = (bf16[1024,128]{1,0:T(8,128)(2,1)S(1)}, bf16[1024,128]{1,0:T(8,128)(2,1)S(1)}, u32[]{:S(2)}, u32[]{:S(2)}) collective-permute-start(bf16[1024,128]{1,0:T(8,128)(2,1)S(1)} %get-tuple-element.31.refs_0_), channel_id=1, source_target_pairs={{0,6},{1,7},{2,4},{3,5},{4,2},{5,3},{6,0},{7,1},{8,14},{9,15},{10,... | collective-permute-start | bytes 786440 | tf_op jit(solution)/shard_map/ppermute | solution.py:387
  56.6 0.8 collective-permute-start.10
  57.5 1.3 %collective-permute-start.8 = (bf16[1024,128]{1,0:T(8,128)(2,1)S(1)}, bf16[1024,128]{1,0:T(8,128)(2,1)S(1)}, u32[]{:S(2)}, u32[]{:S(2)}) collective-permute-start(bf16[1024,128]{1,0:T(8,128)(2,1)S(1)} %get-tuple-element.31.refs_0_), channel_id=1, source_target_pairs={{0,2},{1,3},{2,0},{3,1},{4,6},{5,7},{6,4},{7,5},{8,10},{9,11},{10,... | collective-permute-start | bytes 786440 | tf_op jit(solution)/shard_map/ppermute | solution.py:387
  58.8 0.0 collective-permute-start.7
  58.8 6.7 %collective-permute-done.12.refs_6_ = bf16[1024,128]{1,0:T(8,128)(2,1)S(1)} collective-permute-done((bf16[1024,128]{1,0:T(8,128)(2,1)S(1)}, bf16[1024,128]{1,0:T(8,128)(2,1)S(1)}, u32[]{:S(2)}, u32[]{:S(2)}) %collective-permute-start.12) | collective-permute-done | bytes 262176 | tf_op jit(solution)/shard_map/ppermute | solution.py:387
  65.5 0.0 collective-permute-start.13
  65.5 3.5 %collective-permute-done.10.refs_4_ = bf16[1024,128]{1,0:T(8,128)(2,1)S(1)} collective-permute-done((bf16[1024,128]{1,0:T(8,128)(2,1)S(1)}, bf16[1024,128]{1,0:T(8,128)(2,1)S(1)}, u32[]{:S(2)}, u32[]{:S(2)}) %collective-permute-start.10) | collective-permute-done | bytes 262176 | tf_op jit(solution)/shard_map/ppermute | solution.py:387
  69.0 0.0 collective-permute-start.11
  69.0 0.0 collective-permute-done.8.refs_2_
  69.0 0.5 collective-permute-start.9
  69.5 0.0 collective-permute-done.7.refs_1_
  69.5 0.0 collective-permute-done.13.refs_7_
  69.5 1.0 %collective-permute-done.11.refs_5_ = bf16[1024,128]{1,0:T(8,128)(2,1)S(1)} collective-permute-done((bf16[1024,128]{1,0:T(8,128)(2,1)S(1)}, bf16[1024,128]{1,0:T(8,128)(2,1)S(1)}, u32[]{:S(2)}, u32[]{:S(2)}) %collective-permute-start.11) | collective-permute-done | bytes 262176 | tf_op jit(solution)/shard_map/ppermute | solution.py:387
  70.5 0.4 collective-permute-done.9.refs_3_
  70.9 0.0 slice-done
  70.9 0.0 slice-done.1
  70.9 0.0 slice-done.2
  70.9 0.0 copy-done.2
  70.9 0.0 copy-done.4
  70.9 3.8 %shard_map.94 = (bf16[1040,128]{1,0:T(8,128)(2,1)S(1)}, bf16[1040,128]{1,0:T(8,128)(2,1)S(1)}) custom-call(s32[800]{0:T(1024)S(1)} %copy-done.2, s32[8]{0:T(128)S(1)} %copy-done.4, bf16[320,128,128]{2,1,0:T(8,128)(2,1)S(1)} %bitcast.7, bf16[1024,128]{1,0:T(8,128)(2,1)S(1)} %get-tuple-element.31.refs_0_, ...), custom_call_target="tpu_custom_call" | custom-call | flops 2684354560 | bytes 2621440 | tf_op jit(solution)/shard_map/pallas_call | solution.py:219
  74.7 0.8 collective-permute-start.15
  75.6 0.0 copy-start.6
  75.6 5.7 %collective-permute-start.16 = (bf16[1040,128]{1,0:T(8,128)(2,1)S(1)}, bf16[1040,128]{1,0:T(8,128)(2,1)S(1)}, u32[]{:S(2)}, u32[]{:S(2)}) collective-permute-start(bf16[1040,128]{1,0:T(8,128)(2,1)S(1)} %get-tuple-element.35), channel_id=1, source_target_pairs={{0,24},{8,16},{16,8},{24,0},{1,25},{9,17},{17,9},{25,1},{2,26},{10... | collective-permute-start | bytes 798728 | tf_op jit(solution)/shard_map/ppermute | solution.py:387
  81.2 4.3 %shard_map.93 = (bf16[1040,128]{1,0:T(8,128)(2,1)S(1)}, bf16[1040,128]{1,0:T(8,128)(2,1)S(1)}) custom-call(s32[800]{0:T(1024)S(1)} %copy-done.2, s32[8]{0:T(128)S(1)} %copy-done.4, bf16[320,128,128]{2,1,0:T(8,128)(2,1)S(1)} %bitcast.8, bf16[1024,128]{1,0:T(8,128)(2,1)S(1)} %get-tuple-element.31.refs_0_, ...), custom_call_target="tpu_custom_call" | custom-call | flops 2684354560 | bytes 2621440 | tf_op jit(solution)/shard_map/pallas_call | solution.py:219
  85.5 0.1 collective-permute-start.14
  85.6 1.0 shard_map.92
  86.6 9.9 %collective-permute-done.15.refs_2_ = bf16[1040,128]{1,0:T(8,128)(2,1)S(1)} collective-permute-done((bf16[1040,128]{1,0:T(8,128)(2,1)S(1)}, bf16[1040,128]{1,0:T(8,128)(2,1)S(1)}, u32[]{:S(2)}, u32[]{:S(2)}) %collective-permute-start.15) | collective-permute-done | bytes 266272 | tf_op jit(solution)/shard_map/ppermute | solution.py:387
  96.5 0.0 collective-permute-done.16.refs_3_
  96.5 3.0 %collective-permute-done.14.refs_1_ = bf16[1040,128]{1,0:T(8,128)(2,1)S(1)} collective-permute-done((bf16[1040,128]{1,0:T(8,128)(2,1)S(1)}, bf16[1040,128]{1,0:T(8,128)(2,1)S(1)}, u32[]{:S(2)}, u32[]{:S(2)}) %collective-permute-start.14) | collective-permute-done | bytes 266272 | tf_op jit(solution)/shard_map/ppermute | solution.py:387
  99.5 0.0 copy-done.6
  99.5 1.1 %shard_map.95 = f32[1024,128]{1,0:T(8,128)} custom-call(s32[8,128]{1,0:T(8,128)S(1)} %bitcast.10, bf16[1040,128]{1,0:T(8,128)(2,1)S(1)} %get-tuple-element.32.refs_0_, bf16[1040,128]{1,0:T(8,128)(2,1)S(1)} %collective-permute-done.14.refs_1_, bf16[1040,128]{1,0:T(8,128)(2,1)S(1)} %collective-permute-done.15.refs_2_, ...), custom_call_target="tpu_custom_call" | custom-call | tf_op jit(solution)/shard_map/pallas_call | solution.py:376
  (1 shorter events, 0.0 us)
Async XLA Ops:
  2.5 10.1 %collective-permute-start.2 = (bf16[1024,128]{1,0:T(8,128)(2,1)}, bf16[1024,128]{1,0:T(8,128)(2,1)S(1)}, u32[]{:S(2)}, u32[]{:S(2)}) collective-permute-start(bf16[1024,128]{1,0:T(8,128)(2,1)} %shard_map.87.refs_0_), channel_id=1, source_target_pairs={{0,8},{8,0},{16,24},{24,16},{1,9},{9,1},{17,25},{25,17},{2,10},{10... | collective-permute-start | bytes 786440 | tf_op jit(solution)/shard_map/ppermute | solution.py:387
  5.5 15.6 %collective-permute-start.1 = (bf16[1024,128]{1,0:T(8,128)(2,1)}, bf16[1024,128]{1,0:T(8,128)(2,1)S(1)}, u32[]{:S(2)}, u32[]{:S(2)}) collective-permute-start(bf16[1024,128]{1,0:T(8,128)(2,1)} %shard_map.87.refs_0_), channel_id=1, source_target_pairs={{0,24},{8,16},{16,8},{24,0},{1,25},{9,17},{17,9},{25,1},{2,26},{10... | collective-permute-start | bytes 786440 | tf_op jit(solution)/shard_map/ppermute | solution.py:387
  8.0 23.2 %collective-permute-start = (bf16[1024,128]{1,0:T(8,128)(2,1)}, bf16[1024,128]{1,0:T(8,128)(2,1)S(1)}, u32[]{:S(2)}, u32[]{:S(2)}) collective-permute-start(bf16[1024,128]{1,0:T(8,128)(2,1)} %shard_map.87.refs_0_), channel_id=1, source_target_pairs={{0,16},{8,24},{16,0},{24,8},{1,17},{9,25},{17,1},{25,9},{2,18},{10... | collective-permute-start | bytes 786440 | tf_op jit(solution)/shard_map/ppermute | solution.py:387
  12.6 0.9 copy-start
  13.5 0.7 copy-start.1
  14.2 0.7 copy-start.3
  31.2 39.7 %slice-start = ((s8[10485760]{0:T(1024)(128)(4,1)}), s8[4194304]{0:T(1024)(128)(4,1)S(1)}, s32[]{:S(2)}) async-start(s8[10485760]{0:T(1024)(128)(4,1)} %bitcast.5), calls=%async_computation | async-start | bytes 8388608
  31.2 39.7 %slice-start.1 = ((s8[10485760]{0:T(1024)(128)(4,1)}), s8[4194304]{0:T(1024)(128)(4,1)S(1)}, s32[]{:S(2)}) async-start(s8[10485760]{0:T(1024)(128)(4,1)} %bitcast.5), calls=%async_computation.1 | async-start | bytes 8388608
  31.2 39.7 %slice-start.2 = ((s8[10485760]{0:T(1024)(128)(4,1)}), s8[2097152]{0:T(1024)(128)(4,1)S(1)}, s32[]{:S(2)}) async-start(s8[10485760]{0:T(1024)(128)(4,1)} %bitcast.5), calls=%async_computation.2 | async-start | bytes 4194304
  36.2 2.7 %collective-permute-start.3 = (bf16[4,1040,128]{2,1,0:T(8,128)(2,1)S(1)}, bf16[4,1040,128]{2,1,0:T(8,128)(2,1)S(1)}, u32[]{:S(2)}, u32[]{:S(2)}) collective-permute-start(bf16[4,1040,128]{2,1,0:T(8,128)(2,1)S(1)} %get-tuple-element.24), channel_id=1, source_target_pairs={{0,1},{1,0},{2,3},{3,2},{4,5},{5,4},{6,7},{7,6},{8,9},{9,8},{10,11... | collective-permute-start | bytes 3194888 | tf_op jit(solution)/shard_map/ppermute | solution.py:387
  39.0 15.7 %copy-start.5 = (s32[1024]{0:T(1024)S(1)}, s32[1024]{0:T(1024)}, u32[]{:S(2)}) copy-start(s32[1024]{0:T(1024)} %param.8) | copy-start | bytes 12292
  39.2 31.7 %copy-start.2 = (s32[800]{0:T(1024)S(1)}, s32[800]{0:T(1024)}, u32[]{:S(2)}) copy-start(s32[800]{0:T(1024)} %get-tuple-element.30.codes_ref) | copy-start | bytes 9604
  39.2 31.7 %copy-start.4 = (s32[8]{0:T(128)S(1)}, s32[8]{0:T(128)}, u32[]{:S(2)}) copy-start(s32[8]{0:T(128)} %get-tuple-element.20.counts_ref) | copy-start | bytes 100
  39.3 9.3 %collective-permute-start.4 = (bf16[1040,128]{1,0:T(8,128)(2,1)S(1)}, bf16[1040,128]{1,0:T(8,128)(2,1)S(1)}, u32[]{:S(2)}, u32[]{:S(2)}) collective-permute-start(bf16[1040,128]{1,0:T(8,128)(2,1)S(1)} %get-tuple-element.26), channel_id=1, source_target_pairs={{0,2},{1,3},{2,0},{3,1},{4,6},{5,7},{6,4},{7,5},{8,10},{9,11},{10,... | collective-permute-start | bytes 798728 | tf_op jit(solution)/shard_map/ppermute | solution.py:387
  40.8 13.9 %collective-permute-start.5 = (bf16[1040,128]{1,0:T(8,128)(2,1)S(1)}, bf16[1040,128]{1,0:T(8,128)(2,1)S(1)}, u32[]{:S(2)}, u32[]{:S(2)}) collective-permute-start(bf16[1040,128]{1,0:T(8,128)(2,1)S(1)} %get-tuple-element.27), channel_id=1, source_target_pairs={{0,4},{1,5},{2,6},{3,7},{4,0},{5,1},{6,2},{7,3},{8,12},{9,13},{10,... | collective-permute-start | bytes 798728 | tf_op jit(solution)/shard_map/ppermute | solution.py:387
  41.8 12.9 %collective-permute-start.6 = (bf16[1040,128]{1,0:T(8,128)(2,1)S(1)}, bf16[1040,128]{1,0:T(8,128)(2,1)S(1)}, u32[]{:S(2)}, u32[]{:S(2)}) collective-permute-start(bf16[1040,128]{1,0:T(8,128)(2,1)S(1)} %get-tuple-element.28), channel_id=1, source_target_pairs={{0,6},{1,7},{2,4},{3,5},{4,2},{5,3},{6,0},{7,1},{8,14},{9,15},{10,... | collective-permute-start | bytes 798728 | tf_op jit(solution)/shard_map/ppermute | solution.py:387
  55.3 10.2 %collective-permute-start.12 = (bf16[1024,128]{1,0:T(8,128)(2,1)S(1)}, bf16[1024,128]{1,0:T(8,128)(2,1)S(1)}, u32[]{:S(2)}, u32[]{:S(2)}) collective-permute-start(bf16[1024,128]{1,0:T(8,128)(2,1)S(1)} %get-tuple-element.31.refs_0_), channel_id=1, source_target_pairs={{0,6},{1,7},{2,4},{3,5},{4,2},{5,3},{6,0},{7,1},{8,14},{9,15},{10,... | collective-permute-start | bytes 786440 | tf_op jit(solution)/shard_map/ppermute | solution.py:387
  56.6 12.3 %collective-permute-start.10 = (bf16[1024,128]{1,0:T(8,128)(2,1)S(1)}, bf16[1024,128]{1,0:T(8,128)(2,1)S(1)}, u32[]{:S(2)}, u32[]{:S(2)}) collective-permute-start(bf16[1024,128]{1,0:T(8,128)(2,1)S(1)} %get-tuple-element.31.refs_0_), channel_id=1, source_target_pairs={{0,4},{1,5},{2,6},{3,7},{4,0},{5,1},{6,2},{7,3},{8,12},{9,13},{10,... | collective-permute-start | bytes 786440 | tf_op jit(solution)/shard_map/ppermute | solution.py:387
  57.5 11.5 %collective-permute-start.8 = (bf16[1024,128]{1,0:T(8,128)(2,1)S(1)}, bf16[1024,128]{1,0:T(8,128)(2,1)S(1)}, u32[]{:S(2)}, u32[]{:S(2)}) collective-permute-start(bf16[1024,128]{1,0:T(8,128)(2,1)S(1)} %get-tuple-element.31.refs_0_), channel_id=1, source_target_pairs={{0,2},{1,3},{2,0},{3,1},{4,6},{5,7},{6,4},{7,5},{8,10},{9,11},{10,... | collective-permute-start | bytes 786440 | tf_op jit(solution)/shard_map/ppermute | solution.py:387
  58.8 10.7 %collective-permute-start.7 = (bf16[1024,128]{1,0:T(8,128)(2,1)S(1)}, bf16[1024,128]{1,0:T(8,128)(2,1)S(1)}, u32[]{:S(2)}, u32[]{:S(2)}) collective-permute-start(bf16[1024,128]{1,0:T(8,128)(2,1)S(1)} %get-tuple-element.31.refs_0_), channel_id=1, source_target_pairs={{0,1},{1,0},{2,3},{3,2},{4,5},{5,4},{6,7},{7,6},{8,9},{9,8},{10,11... | collective-permute-start | bytes 786440 | tf_op jit(solution)/shard_map/ppermute | solution.py:387
  65.5 4.0 %collective-permute-start.13 = (bf16[1024,128]{1,0:T(8,128)(2,1)S(1)}, bf16[1024,128]{1,0:T(8,128)(2,1)S(1)}, u32[]{:S(2)}, u32[]{:S(2)}) collective-permute-start(bf16[1024,128]{1,0:T(8,128)(2,1)S(1)} %collective-permute-done.12.refs_6_), channel_id=1, source_target_pairs={{0,1},{1,0},{2,3},{3,2},{4,5},{5,4},{6,7},{7,6},{8,9},{9,8},{10,11... | collective-permute-start | bytes 786440 | tf_op jit(solution)/shard_map/ppermute | solution.py:387
  69.0 1.5 %collective-permute-start.11 = (bf16[1024,128]{1,0:T(8,128)(2,1)S(1)}, bf16[1024,128]{1,0:T(8,128)(2,1)S(1)}, u32[]{:S(2)}, u32[]{:S(2)}) collective-permute-start(bf16[1024,128]{1,0:T(8,128)(2,1)S(1)} %collective-permute-done.10.refs_4_), channel_id=1, source_target_pairs={{0,1},{1,0},{2,3},{3,2},{4,5},{5,4},{6,7},{7,6},{8,9},{9,8},{10,11... | collective-permute-start | bytes 786440 | tf_op jit(solution)/shard_map/ppermute | solution.py:387
  69.0 1.9 %collective-permute-start.9 = (bf16[1024,128]{1,0:T(8,128)(2,1)S(1)}, bf16[1024,128]{1,0:T(8,128)(2,1)S(1)}, u32[]{:S(2)}, u32[]{:S(2)}) collective-permute-start(bf16[1024,128]{1,0:T(8,128)(2,1)S(1)} %collective-permute-done.8.refs_2_), channel_id=1, source_target_pairs={{0,1},{1,0},{2,3},{3,2},{4,5},{5,4},{6,7},{7,6},{8,9},{9,8},{10,11... | collective-permute-start | bytes 786440 | tf_op jit(solution)/shard_map/ppermute | solution.py:387
  74.7 21.8 %collective-permute-start.15 = (bf16[1040,128]{1,0:T(8,128)(2,1)S(1)}, bf16[1040,128]{1,0:T(8,128)(2,1)S(1)}, u32[]{:S(2)}, u32[]{:S(2)}) collective-permute-start(bf16[1040,128]{1,0:T(8,128)(2,1)S(1)} %get-tuple-element.34), channel_id=1, source_target_pairs={{0,16},{8,24},{16,0},{24,8},{1,17},{9,25},{17,1},{25,9},{2,18},{10... | collective-permute-start | bytes 798728 | tf_op jit(solution)/shard_map/ppermute | solution.py:387
  75.6 23.9 %copy-start.6 = (s32[1024]{0:T(1024)S(1)}, s32[1024]{0:T(1024)}, u32[]{:S(2)}) copy-start(s32[1024]{0:T(1024)} %param.9) | copy-start | bytes 12292
  75.6 20.9 %collective-permute-start.16 = (bf16[1040,128]{1,0:T(8,128)(2,1)S(1)}, bf16[1040,128]{1,0:T(8,128)(2,1)S(1)}, u32[]{:S(2)}, u32[]{:S(2)}) collective-permute-start(bf16[1040,128]{1,0:T(8,128)(2,1)S(1)} %get-tuple-element.35), channel_id=1, source_target_pairs={{0,24},{8,16},{16,8},{24,0},{1,25},{9,17},{17,9},{25,1},{2,26},{10... | collective-permute-start | bytes 798728 | tf_op jit(solution)/shard_map/ppermute | solution.py:387
  85.5 14.0 %collective-permute-start.14 = (bf16[1040,128]{1,0:T(8,128)(2,1)S(1)}, bf16[1040,128]{1,0:T(8,128)(2,1)S(1)}, u32[]{:S(2)}, u32[]{:S(2)}) collective-permute-start(bf16[1040,128]{1,0:T(8,128)(2,1)S(1)} %get-tuple-element.33), channel_id=1, source_target_pairs={{0,8},{8,0},{16,24},{24,16},{1,9},{9,1},{17,25},{25,17},{2,10},{10... | collective-permute-start | bytes 798728 | tf_op jit(solution)/shard_map/ppermute | solution.py:387

commit v3 on v2

v3 whole, which is shorter than its diff:
```python
import functools

import jax
import jax.numpy as jnp
from jax import lax
from jax.experimental import pallas as pl
from jax.experimental.pallas import tpu as pltpu
from jax.sharding import PartitionSpec as P

BLEND = 0.75
GROUP = 32
PLACE = 8
NT = (((1,), (1,)), ((), ()))
VMEM = pl.BlockSpec(memory_space=pltpu.VMEM)


def params(mib):
    return pltpu.CompilerParams(vmem_limit_bytes=mib * 2**20)


def split_half(mass):
    high = mass.astype(jnp.bfloat16)
    low = (mass - high.astype(jnp.float32)).astype(jnp.bfloat16)
    return jnp.concatenate([high.astype(jnp.float32), low.astype(jnp.float32)], axis=0).astype(
        jnp.bfloat16
    )


def prep_kernel(video_ref, out_ref):
    out_ref[...] = video_ref[...].astype(jnp.bfloat16)


def prep(video):
    return pl.pallas_call(
        prep_kernel,
        out_shape=jax.ShapeDtypeStruct(video.shape, jnp.bfloat16),
        in_specs=[VMEM],
        out_specs=VMEM,
        compiler_params=params(48),
    )(video)


def plan_kernel(rows, cols, live_ref, _, forward_ref, reverse_ref, counts, *, cap, half, shard):
    row_mask, col_mask = lax.axis_index("row") * shard, lax.axis_index("col") * shard
    live = live_ref[0, 0]
    trash = 2 * cap

    def place(block, carry):
        early, late, far, near = carry
        base = block * PLACE
        found = [(rows[0, 0, base + k], cols[0, 0, base + k]) for k in range(PLACE)]
        for k, (row, col) in enumerate(found):
            slot = base + k
            row, col = row ^ col_mask, col ^ row_mask
            high = (col >= half).astype(jnp.int32)
            local = col - high * half
            there = jnp.where(high == 1, cap + late, early)
            back = jnp.where(high == 1, far, cap + near)
            forward = slot | (local << 12) | (row << 20)
            reverse = slot | (row << 12) | (local << 20)
            used = slot < live
            forward_ref[jnp.where(used, there, trash)] = forward
            reverse_ref[jnp.where(used, back, trash)] = reverse
            low = used.astype(jnp.int32) * (1 - high)
            high = used.astype(jnp.int32) * high
            early, late, far, near = early + low, late + high, far + high, near + low
        return early, late, far, near

    zero = jnp.int32(0)
    blocks = lax.div(live + (PLACE - 1), PLACE)
    early, late, far, near = lax.fori_loop(0, blocks, place, (zero, zero, zero, zero))
    counts[0] = early
    counts[1] = late
    counts[2] = far
    counts[3] = near
    counts[4] = live
    row_dummy = (lax.axis_size("col") * shard) << 20
    col_dummy = half << 20

    def pad(n, carry):
        forward_ref[early + n] = row_dummy
        forward_ref[cap + late + n] = row_dummy
        reverse_ref[far + n] = col_dummy
        reverse_ref[cap + near + n] = col_dummy
        return carry

    lax.fori_loop(0, GROUP, pad, 0)


def plan(rows, cols, live, tiles, col_tiles, shard):
    cap = rows.shape[2] + GROUP
    smem = pl.BlockSpec(memory_space=pltpu.SMEM)
    codes = jax.ShapeDtypeStruct((2 * cap + 128,), jnp.int32)
    return pl.pallas_call(
        functools.partial(plan_kernel, cap=cap, half=col_tiles // 2, shard=shard),
        out_shape=[codes, codes, jax.ShapeDtypeStruct((8,), jnp.int32)],
        in_specs=[smem] * 3 + [VMEM],
        out_specs=[smem] * 3,
        compiler_params=grant(0, [tiles]),
        cost_estimate=pl.CostEstimate(flops=4 * 10**9, bytes_accessed=0, transcendentals=0),
    )(rows, cols, live, tiles)


def fill_panel(panel, piece_refs):
    tiles = piece_refs[0].shape[0] // 128
    for m, piece in enumerate(piece_refs):
        for t in range(tiles):
            panel[m * tiles + t] = piece[t * 128 : (t + 1) * 128, :]


def clear(*sums):
    def one(n, carry):
        for ref in sums:
            ref[n] = jnp.zeros(ref.shape[1:], jnp.float32)
        return carry

    lax.fori_loop(0, sums[0].shape[0] - 1, one, 0)


def groups(count):
    return lax.div(count + (GROUP - 1), GROUP)


def fold_rows(tile):
    return jnp.sum(tile.reshape(16, 8, 128), axis=0)


def early_kernel(codes, counts, tiles_ref, *refs):
    *piece_refs, sums_ref, weights_ref, panel, acc, mass = refs
    dummy = acc.shape[0] - 1
    cap = tiles_ref.shape[0] + GROUP
    fill_panel(panel, piece_refs)
    clear(acc, mass)
    ones = jnp.ones((16, 128), jnp.bfloat16)

    def work(g, carry):
        for k in range(GROUP):
            code = codes[g * GROUP + k]
            part = panel[lax.shift_right_logical(code, 12) & 0xFF]
            acc[lax.shift_right_logical(code, 20)] += jnp.dot(
                tiles_ref[code & 0xFFF], part, preferred_element_type=jnp.float32
            )
        return carry

    lax.fori_loop(0, groups(counts[0]), work, 0)
    for base, at in ((0, 0), (cap, 1)):

        def weigh(g, carry):
            for k in range(GROUP):
                code = codes[base + g * GROUP + k]
                tile = tiles_ref[code & 0xFFF]
                sums = lax.dot_general(ones, tile, NT, preferred_element_type=jnp.float32)
                mass[lax.shift_right_logical(code, 20)] += sums[:8]
            return carry

        lax.fori_loop(0, groups(counts[at]), weigh, 0)

    def hand(n, carry):
        sums_ref[n] = acc[n]
        weights_ref[n] = mass[n]
        return carry

    lax.fori_loop(0, dummy, hand, 0)


def grant(scratch, arrays):
    size = sum(x.size * x.dtype.itemsize for x in arrays)
    return params((scratch + (size if size > 24 * 2**20 else 0)) // 2**20 + 5)


def effort(slots):
    average = slots // 4
    return pl.CostEstimate(
        flops=16 * average * 128**3, bytes_accessed=average * 128 * 256, transcendentals=0
    )


def early_sweep(codes, counts, tiles, pieces, row_tiles):
    smem, slots = pl.BlockSpec(memory_space=pltpu.SMEM), tiles.shape[0]
    out_shape = [
        jax.ShapeDtypeStruct((row_tiles, 128, 128), jnp.float32),
        jax.ShapeDtypeStruct((row_tiles, 8, 128), jnp.float32),
    ]
    scratch = 4 * (row_tiles + 1) * 136 * 128 + sum(p.size for p in pieces) * 2
    return pl.pallas_call(
        early_kernel,
        in_specs=[smem] * 2 + [VMEM] * (1 + len(pieces)),
        out_specs=[VMEM] * 2,
        scratch_shapes=[
            pltpu.VMEM((sum(p.shape[0] for p in pieces) // 128, 128, 128), jnp.bfloat16),
            pltpu.VMEM((row_tiles + 1, 128, 128), jnp.float32),
            pltpu.VMEM((row_tiles + 1, 8, 128), jnp.float32),
        ],
        out_shape=out_shape,
        compiler_params=grant(scratch, [tiles, *pieces, *out_shape]),
        cost_estimate=effort(slots),
    )(codes, counts, tiles, *pieces)


def late_kernel(codes, counts, tiles_ref, sums_ref, weights_ref, *refs, first, at, shard):
    *piece_refs, keep_ref, send_ref, panel, acc = refs
    fill_panel(panel, piece_refs)
    clear(acc)

    def work(g, carry):
        for k in range(GROUP):
            code = codes[first + g * GROUP + k]
            part = panel[lax.shift_right_logical(code, 12) & 0xFF]
            acc[lax.shift_right_logical(code, 20)] += jnp.dot(
                tiles_ref[code & 0xFFF], part, preferred_element_type=jnp.float32
            )
        return carry

    lax.fori_loop(0, groups(counts[at]), work, 0)
    for n in range((acc.shape[0] - 1) // shard):
        target = (keep_ref, send_ref)[n % 2].at[n // 2]
        tops = []
        for t in range(shard):
            tile = acc[n * shard + t] + sums_ref[n * shard + t]
            target[t * 128 : (t + 1) * 128, :] = tile.astype(jnp.bfloat16)
            tops.append(weights_ref[n * shard + t, 0:1, :])
        target[shard * 128 :, :] = split_half(jnp.concatenate(tops, axis=0))


def late_sweep(codes, counts, tiles, sums, weights, pieces, shard):
    smem, slots, row_tiles = pl.BlockSpec(memory_space=pltpu.SMEM), tiles.shape[0], sums.shape[0]
    rows = shard * 130
    out_shape = [jax.ShapeDtypeStruct((row_tiles // shard // 2, rows, 128), jnp.bfloat16)] * 2
    scratch = 4 * (row_tiles + 1) * 128**2 + sum(p.size for p in pieces) * 2
    return pl.pallas_call(
        functools.partial(late_kernel, first=slots + GROUP, at=1, shard=shard),
        in_specs=[smem] * 2 + [VMEM] * (3 + len(pieces)),
        out_specs=[VMEM] * 2,
        scratch_shapes=[
            pltpu.VMEM((sum(p.shape[0] for p in pieces) // 128, 128, 128), jnp.bfloat16),
            pltpu.VMEM((row_tiles + 1, 128, 128), jnp.float32),
        ],
        out_shape=out_shape,
        compiler_params=grant(scratch, [tiles, sums, weights, *pieces, *out_shape]),
        cost_estimate=effort(slots),
    )(codes, counts, tiles, sums, weights, *pieces)


def reverse_kernel(codes, counts, tiles_ref, *refs, pieces, first, at, shard):
    piece_refs, out_refs, (panel, acc, mass) = refs[:pieces], refs[pieces:-3], refs[-3:]
    fill_panel(panel, piece_refs)
    clear(acc, mass)

    def work(g, carry):
        for k in range(GROUP):
            code = codes[first + g * GROUP + k]
            to = lax.shift_right_logical(code, 20)
            tile = tiles_ref[code & 0xFFF]
            part = panel[lax.shift_right_logical(code, 12) & 0xFF]
            acc[to] += jnp.dot(part, tile, preferred_element_type=jnp.float32)
            mass[to] += fold_rows(tile.astype(jnp.float32))
        return carry

    lax.fori_loop(0, groups(counts[at]), work, 0)
    for n, target in enumerate(out_refs):
        tops = []
        for t in range(shard):
            target[t * 128 : (t + 1) * 128, :] = acc[n * shard + t].astype(jnp.bfloat16)
            tops.append(jnp.sum(mass[n * shard + t], axis=0, keepdims=True))
        target[shard * 128 :, :] = split_half(jnp.concatenate(tops, axis=0))


def reverse_sweep(codes, counts, part, tiles, pieces, col_tiles, shard):
    smem, slots = pl.BlockSpec(memory_space=pltpu.SMEM), tiles.shape[0]
    out_shape = [jax.ShapeDtypeStruct((shard * 130, 128), jnp.bfloat16)] * (col_tiles // shard)
    scratch = 4 * (col_tiles + 1) * 136 * 128 + sum(p.size for p in pieces) * 2
    return pl.pallas_call(
        functools.partial(
            reverse_kernel,
            pieces=len(pieces),
            first=part * (slots + GROUP),
            at=2 + part,
            shard=shard,
        ),
        in_specs=[smem] * 2 + [VMEM] * (1 + len(pieces)),
        out_specs=[VMEM] * len(out_shape),
        scratch_shapes=[
            pltpu.VMEM((sum(p.shape[0] for p in pieces) // 128, 128, 128), jnp.bfloat16),
            pltpu.VMEM((col_tiles + 1, 128, 128), jnp.float32),
            pltpu.VMEM((col_tiles + 1, 8, 128), jnp.float32),
        ],
        out_shape=out_shape,
        compiler_params=grant(scratch, [tiles, *pieces, *out_shape]),
        cost_estimate=effort(slots),
    )(codes, counts, tiles, *pieces)


def pair_sum_kernel(keep_ref, got_ref, *out_refs, body_rows):
    for s in list(range(1, len(out_refs))) + [0]:
        out_ref = out_refs[s]
        total = keep_ref[s, :body_rows].astype(jnp.float32)
        total += got_ref[s, :body_rows].astype(jnp.float32)
        mass = both_halves(keep_ref[s, body_rows:]) + both_halves(got_ref[s, body_rows:])
        out_ref[:body_rows, :] = total.astype(out_ref.dtype)
        if s == 0:
            out_ref[body_rows:, :] = jnp.concatenate([mass, jnp.zeros_like(mass)], axis=0)
        else:
            out_ref[body_rows:, :] = split_half(mass)


def both_halves(block):
    wide = block.astype(jnp.float32)
    half = wide.shape[0] // 2
    return wide[:half] + wide[half:]


def pair_sum(keep, got, body_rows):
    count, rows, _ = keep.shape
    shapes = [
        jax.ShapeDtypeStruct((rows, 128), jnp.float32 if s == 0 else jnp.bfloat16)
        for s in range(count)
    ]
    return pl.pallas_call(
        functools.partial(pair_sum_kernel, body_rows=body_rows),
        out_shape=shapes,
        in_specs=[VMEM] * 2,
        out_specs=[VMEM] * count,
        compiler_params=params(48),
    )(keep, got)


def spread(row):
    return jnp.broadcast_to(row, (128, 128))


def audio_kernel(label_ref, own_ref, *refs, shard):
    got, (half_ref, full_ref) = refs[:-2], refs[-2:]
    body = shard * 128
    mass = own_ref[body : body + shard, :]
    for g in got:
        mass += both_halves(g[body:])
    scale = BLEND / jnp.sqrt(mass)
    for t in range(shard):
        span = slice(t * 128, (t + 1) * 128)
        total = own_ref[span, :]
        for g in got:
            total += g[span, :].astype(jnp.float32)
        scores = total * spread(scale[t : t + 1, :]).T + label_ref[span, :]
        full_ref[span, :] = scores
        half_ref[span, :] = scores.T.astype(jnp.bfloat16)


def audio_blend(labels, own, got):
    shard = labels.shape[0] // 128
    shape = (shard * 128, 128)
    return pl.pallas_call(
        functools.partial(audio_kernel, shard=shard),
        out_shape=[
            jax.ShapeDtypeStruct(shape, jnp.bfloat16),
            jax.ShapeDtypeStruct(shape, jnp.float32),
        ],
        in_specs=[VMEM] * (2 + len(got)),
        out_specs=[VMEM] * 2,
        compiler_params=params(48),
    )(labels, own, *got)


def video_kernel(seed_ref, *refs, shard):
    got, out_ref = refs[:-1], refs[-1]
    body = shard * 128
    scale = BLEND / jnp.sqrt(sum(both_halves(r[body:]) for r in got))
    seeds = seed_ref[...]
    classes = lax.broadcasted_iota(jnp.int32, (128, 128), 0)
    for t in range(shard):
        span = slice(t * 128, (t + 1) * 128)
        total = sum(r[span, :].astype(jnp.float32) for r in got)
        labels = jnp.where(classes == seeds[t : t + 1, :], 1.0 - BLEND, 0.0)
        out_ref[span, :] = (total * scale[t : t + 1, :] + labels).T


def video_blend(seeds, pieces):
    shard = seeds.shape[0]
    return pl.pallas_call(
        functools.partial(video_kernel, shard=shard),
        out_shape=jax.ShapeDtypeStruct((shard * 128, 128), jnp.float32),
        in_specs=[VMEM] * (1 + len(pieces)),
        out_specs=VMEM,
        compiler_params=params(48),
    )(seeds, *pieces)


def partner(value, axis, mask):
    size = lax.axis_size(axis)
    return lax.ppermute(value, axis, [(i, i ^ mask) for i in range(size)])


def body(video_scores_in, audio_seed, video_seed, tile_values, tile_rows, tile_cols, tile_count):
    tiles = tile_values[0, 0]
    shard = video_scores_in.shape[0] // 128
    n_row, n_col = lax.axis_size("row"), lax.axis_size("col")
    row_tiles, col_tiles = n_col * shard, n_row * shard
    classes = jnp.arange(128, dtype=jnp.int32)[None, :]
    labels = jnp.where(audio_seed[:, None] == classes, jnp.float32(1.0 - BLEND), jnp.float32(0.0))
    video_seeds = video_seed.reshape(shard, 128)

    own = prep(video_scores_in)
    panel = [own] + [partner(own, "row", m) for m in range(1, n_row)]
    forward, reverse, counts = plan(tile_rows, tile_cols, tile_count, tiles, col_tiles, shard)
    near, far = panel[: n_row // 2], panel[n_row // 2 :]
    sums, weights = early_sweep(forward, counts, tiles, near, row_tiles)
    keep, send = late_sweep(forward, counts, tiles, sums, weights, far, shard)
    got = partner(send, "col", 1)
    own, *others = pair_sum(keep, got, shard * 128)
    arrived = [partner(x, "col", 2 * (s + 1)) for s, x in enumerate(others)]
    half, audio_scores = audio_blend(labels, own, arrived)

    mine = [half] + [partner(half, "col", m) for m in range(2, n_col, 2)]
    pieces = [q for p in mine for q in (p, partner(p, "col", 1))]
    far = reverse_sweep(reverse, counts, 0, tiles, pieces, col_tiles // 2, shard)
    near = reverse_sweep(reverse, counts, 1, tiles, pieces, col_tiles // 2, shard)
    sums = list(near) + list(far)
    results = [sums[0]] + [partner(sums[m], "row", m) for m in range(1, n_row)]
    return audio_scores, video_blend(video_seeds, results)


def solution(mesh):
    in_specs = (
        P(("col", "row"), None),
        P(("row", "col")),
        P(("col", "row")),
        P("row", "col", None, None, None),
        P("row", "col", None),
        P("row", "col", None),
        P("row", "col"),
    )
    out_specs = (P(("row", "col"), None), P(("col", "row"), None))
    return jax.shard_map(body, mesh=mesh, in_specs=in_specs, out_specs=out_specs, check_vma=False)
```

time: 102 us -> 95.8 us (0.939); the launches traced: 101 us -> 96.2 us
  Pallas kernels: 26 us -> 20.7 us
  local copies, waits for them, and re-layouts: 2.32 us -> 7.04 us
  waiting for transfers between devices: 51 us -> 46.5 us
    pallas_call x8 -> x7, Pallas kernels: 22.7 us -> 17.1 us  [the longest x1 7.14 us: early_sweep(): pl.pallas_call(early_kernel, in_specs=[smem] * 2 + [VMEM] * (1 + len(piec...]
    unnamed x20 -> x14, local copies, waits for them, and re-layouts: 2.32 us -> 7.04 us
    ppermute x17, waiting for transfers between devices: 51 us -> 46.5 us  [partner(): return lax.ppermute(value, axis, [(i, i ^ mask) for i in range(size)])]
where the time goes in v3:
time: 95.8 us; the launch traced here: 96.2 us
  waiting for transfers between devices  46.5 us (49%)
  Pallas kernels  20.7 us (22%)
  starting transfers between devices  20.4 us (21%)
  local copies, waits for them, and re-layouts  7.04 us (7%)
  between operations  1.38 us (1%)
    ppermute x17, waiting for transfers between devices, partner(): return lax.ppermute(value, axis, [(i, i ^ mask) for i in range(size)])  46.5 us
    ppermute x17, starting transfers between devices, partner(): return lax.ppermute(value, axis, [(i, i ^ mask) for i in range(size)])  20.4 us
    pallas_call x1, Pallas kernels, early_sweep(): pl.pallas_call(early_kernel, in_specs=[smem] * 2 + [VMEM] * (1 + len(piec...  7.14 us
    unnamed x14, local copies, waits for them, and re-layouts  7.04 us
    pallas_call x2, Pallas kernels, reverse_sweep(): pl.pallas_call(functools.partial(reverse_kernel, pieces=len(pieces), firs...  4.81 us
    pallas_call x1, Pallas kernels, plan(): pl.pallas_call(functools.partial(plan_kernel, cap=cap, half=col_tiles //...  3.3 us
    pallas_call x1, Pallas kernels, late_sweep(): pl.pallas_call(functools.partial(late_kernel, first=slots + GROUP, at=1,...  2.87 us
  transfers between devices with their start and end apart: 17, of which 12 were waited for; matrix products, arithmetic and copies ran while one was open for 0% of the time, Pallas kernels for 13%

profile of v3, /device:TPU:0, one launch (start us, length us, event | category | flops | bytes accessed | tf_op | source)
XLA Modules:
  0.0 96.2 jit_solution(5671418134067643030)
XLA Ops:
  0.6 0.0 copy-start.2
  0.6 1.0 %copy-done.2 = f32[1024,128]{1,0:T(8,128)S(1)} copy-done((f32[1024,128]{1,0:T(8,128)S(1)}, f32[1024,128]{1,0:T(8,128)}, u32[]{:S(2)}) %copy-start.2) | copy-done | bytes 524312
  1.7 3.1 %collective-permute-start = (bf16[1024,128]{1,0:T(8,128)(2,1)S(1)}, bf16[1024,128]{1,0:T(8,128)(2,1)S(1)}, u32[]{:S(2)}, u32[]{:S(2)}) collective-permute-start(bf16[1024,128]{1,0:T(8,128)(2,1)S(1)} %shard_map.87.refs_0_), channel_id=1, source_target_pairs={{0,8},{8,0},{16,24},{24,16},{1,9},{9,1},{17,25},{25,17},{2,10},{10... | collective-permute-start | bytes 786440 | tf_op jit(solution)/shard_map/ppermute | solution.py:389
  4.8 2.6 %collective-permute-start.1 = (bf16[1024,128]{1,0:T(8,128)(2,1)S(1)}, bf16[1024,128]{1,0:T(8,128)(2,1)S(1)}, u32[]{:S(2)}, u32[]{:S(2)}) collective-permute-start(bf16[1024,128]{1,0:T(8,128)(2,1)S(1)} %shard_map.87.refs_0_), channel_id=1, source_target_pairs={{0,16},{8,24},{16,0},{24,8},{1,17},{9,25},{17,1},{25,9},{2,18},{10... | collective-permute-start | bytes 786440 | tf_op jit(solution)/shard_map/ppermute | solution.py:389
  7.4 0.0 collective-permute-start.2
  8.0 0.0 copy-start
  8.0 4.0 %copy-done = bf16[1,1,320,128,128]{4,3,2,1,0:T(8,128)(2,1)S(1)} copy-done((bf16[1,1,320,128,128]{4,3,2,1,0:T(8,128)(2,1)S(1)}, bf16[1,1,320,128,128]{4,3,2,1,0:T(8,128)(2,1)}, u32[]{:S(2)}) %copy-start) | copy-done | bytes 10485784
  12.0 0.0 copy-start.4
  12.0 0.7 copy-done.4
  12.7 0.0 copy-start.5
  12.7 0.7 copy-done.5
  13.4 0.0 copy-start.1
  13.4 3.3 %shard_map.86 = (s32[832]{0:T(1024)S(1)}, s32[832]{0:T(1024)S(1)}, s32[8]{0:T(128)S(1)}) custom-call(s32[1,1,320]{2,1,0:T(1,128)S(1)} %copy-done.4, s32[1,1,320]{2,1,0:T(1,128)S(1)} %copy-done.5, s32[1,1]{1,0:T(1,128)S(6)} %copy.9.live_ref, bf16[320,128,128]{2,1,0:T(8,128)(2,1)S(1)} %bitcast.2), custom_call_target="tpu_custom_call" | custom-call | flops 4000000000 | tf_op jit(solution)/shard_map/pallas_call | solution.py:94
  16.7 0.0 collective-permute-done.refs_1_
  16.7 0.7 copy-done.1
  17.4 7.1 %shard_map.88 = (f32[64,128,128]{2,1,0:T(8,128)S(1)}, f32[64,8,128]{2,1,0:T(8,128)S(1)}) custom-call(s32[832]{0:T(1024)S(1)} %get-tuple-element.19.codes, s32[8]{0:T(128)S(1)} %get-tuple-element.20.counts, bf16[320,128,128]{2,1,0:T(8,128)(2,1)S(1)} %bitcast.3, bf16[1024,128]{1,0:T(8,128)(2,1)S(1)} %shard_map.87.refs_0_, ...), custom_call_target="tpu_custom_call" | custom-call | flops 2684354560 | bytes 2621440 | tf_op jit(solution)/shard_map/pallas_call | solution.py:185
  24.5 1.7 %collective-permute-done.1.refs_0_ = bf16[1024,128]{1,0:T(8,128)(2,1)S(1)} collective-permute-done((bf16[1024,128]{1,0:T(8,128)(2,1)S(1)}, bf16[1024,128]{1,0:T(8,128)(2,1)S(1)}, u32[]{:S(2)}, u32[]{:S(2)}) %collective-permute-start.1) | collective-permute-done | bytes 262176 | tf_op jit(solution)/shard_map/ppermute | solution.py:389
  26.2 0.0 collective-permute-done.2.refs_1_
  26.2 2.9 %shard_map.89 = (bf16[4,1040,128]{2,1,0:T(8,128)(2,1)S(1)}, bf16[4,1040,128]{2,1,0:T(8,128)(2,1)S(1)}) custom-call(s32[832]{0:T(1024)S(1)} %get-tuple-element.19.codes, s32[8]{0:T(128)S(1)} %get-tuple-element.20.counts, bf16[320,128,128]{2,1,0:T(8,128)(2,1)S(1)} %bitcast.4, f32[64,128,128]{2,1,0:T(8,128)S(1)} %get-tuple-element.21.sums_ref, ...), custom_call_target="tpu_custom_call" | custom-call | flops 2684354560 | bytes 2621440 | tf_op jit(solution)/shard_map/pallas_call | solution.py:230
  29.0 0.1 collective-permute-start.3
  29.1 2.7 %collective-permute-done.3.got_ref = bf16[4,1040,128]{2,1,0:T(8,128)(2,1)S(1)} collective-permute-done((bf16[4,1040,128]{2,1,0:T(8,128)(2,1)S(1)}, bf16[4,1040,128]{2,1,0:T(8,128)(2,1)S(1)}, u32[]{:S(2)}, u32[]{:S(2)}) %collective-permute-start.3) | collective-permute-done | bytes 1064992 | tf_op jit(solution)/shard_map/ppermute | solution.py:389
  31.8 0.0 copy-start.6
  31.8 0.3 shard_map.90
  32.1 1.1 %collective-permute-start.4 = (bf16[1040,128]{1,0:T(8,128)(2,1)S(1)}, bf16[1040,128]{1,0:T(8,128)(2,1)S(1)}, u32[]{:S(2)}, u32[]{:S(2)}) collective-permute-start(bf16[1040,128]{1,0:T(8,128)(2,1)S(1)} %get-tuple-element.26), channel_id=1, source_target_pairs={{0,2},{1,3},{2,0},{3,1},{4,6},{5,7},{6,4},{7,5},{8,10},{9,11},{10,... | collective-permute-start | bytes 798728 | tf_op jit(solution)/shard_map/ppermute | solution.py:389
  33.1 5.1 %collective-permute-start.5 = (bf16[1040,128]{1,0:T(8,128)(2,1)S(1)}, bf16[1040,128]{1,0:T(8,128)(2,1)S(1)}, u32[]{:S(2)}, u32[]{:S(2)}) collective-permute-start(bf16[1040,128]{1,0:T(8,128)(2,1)S(1)} %get-tuple-element.27), channel_id=1, source_target_pairs={{0,4},{1,5},{2,6},{3,7},{4,0},{5,1},{6,2},{7,3},{8,12},{9,13},{10,... | collective-permute-start | bytes 798728 | tf_op jit(solution)/shard_map/ppermute | solution.py:389
  38.2 1.4 %collective-permute-start.6 = (bf16[1040,128]{1,0:T(8,128)(2,1)S(1)}, bf16[1040,128]{1,0:T(8,128)(2,1)S(1)}, u32[]{:S(2)}, u32[]{:S(2)}) collective-permute-start(bf16[1040,128]{1,0:T(8,128)(2,1)S(1)} %get-tuple-element.28), channel_id=1, source_target_pairs={{0,6},{1,7},{2,4},{3,5},{4,2},{5,3},{6,0},{7,1},{8,14},{9,15},{10,... | collective-permute-start | bytes 798728 | tf_op jit(solution)/shard_map/ppermute | solution.py:389
  39.6 0.0 copy-done.6
  39.6 0.2 fusion.label_ref
  39.8 0.8 collective-permute-done.4.refs_0_
  40.6 9.5 %collective-permute-done.5.refs_1_ = bf16[1040,128]{1,0:T(8,128)(2,1)S(1)} collective-permute-done((bf16[1040,128]{1,0:T(8,128)(2,1)S(1)}, bf16[1040,128]{1,0:T(8,128)(2,1)S(1)}, u32[]{:S(2)}, u32[]{:S(2)}) %collective-permute-start.5) | collective-permute-done | bytes 266272 | tf_op jit(solution)/shard_map/ppermute | solution.py:389
  50.1 1.8 %collective-permute-done.6.refs_2_ = bf16[1040,128]{1,0:T(8,128)(2,1)S(1)} collective-permute-done((bf16[1040,128]{1,0:T(8,128)(2,1)S(1)}, bf16[1040,128]{1,0:T(8,128)(2,1)S(1)}, u32[]{:S(2)}, u32[]{:S(2)}) %collective-permute-start.6) | collective-permute-done | bytes 266272 | tf_op jit(solution)/shard_map/ppermute | solution.py:389
  51.9 1.2 %shard_map.91 = (bf16[1024,128]{1,0:T(8,128)(2,1)S(1)}, f32[1024,128]{1,0:T(8,128)}) custom-call(f32[1024,128]{1,0:T(8,128)S(1)} %fusion.label_ref, f32[1040,128]{1,0:T(8,128)S(1)} %get-tuple-element.25.own_ref, bf16[1040,128]{1,0:T(8,128)(2,1)S(1)} %collective-permute-done.4.refs_0_, bf16[1040,128]{1,0:T(8,128)(2,1)S(1)} %collective-permute-done.5.refs_1_, ...), custom_call_target="tpu_custom_call" | custom-call | tf_op jit(solution)/shard_map/pallas_call | solution.py:351
  53.1 0.6 collective-permute-start.10
  53.8 1.4 %collective-permute-start.12 = (bf16[1024,128]{1,0:T(8,128)(2,1)S(1)}, bf16[1024,128]{1,0:T(8,128)(2,1)S(1)}, u32[]{:S(2)}, u32[]{:S(2)}) collective-permute-start(bf16[1024,128]{1,0:T(8,128)(2,1)S(1)} %get-tuple-element.31.refs_0_), channel_id=1, source_target_pairs={{0,6},{1,7},{2,4},{3,5},{4,2},{5,3},{6,0},{7,1},{8,14},{9,15},{10,... | collective-permute-start | bytes 786440 | tf_op jit(solution)/shard_map/ppermute | solution.py:389
  55.2 1.5 %collective-permute-start.8 = (bf16[1024,128]{1,0:T(8,128)(2,1)S(1)}, bf16[1024,128]{1,0:T(8,128)(2,1)S(1)}, u32[]{:S(2)}, u32[]{:S(2)}) collective-permute-start(bf16[1024,128]{1,0:T(8,128)(2,1)S(1)} %get-tuple-element.31.refs_0_), channel_id=1, source_target_pairs={{0,2},{1,3},{2,0},{3,1},{4,6},{5,7},{6,4},{7,5},{8,10},{9,11},{10,... | collective-permute-start | bytes 786440 | tf_op jit(solution)/shard_map/ppermute | solution.py:389
  56.6 0.0 collective-permute-start.7
  56.6 9.9 %collective-permute-done.10.refs_4_ = bf16[1024,128]{1,0:T(8,128)(2,1)S(1)} collective-permute-done((bf16[1024,128]{1,0:T(8,128)(2,1)S(1)}, bf16[1024,128]{1,0:T(8,128)(2,1)S(1)}, u32[]{:S(2)}, u32[]{:S(2)}) %collective-permute-start.10) | collective-permute-done | bytes 262176 | tf_op jit(solution)/shard_map/ppermute | solution.py:389
  66.5 0.0 collective-permute-start.11
  66.5 0.0 collective-permute-done.12.refs_6_
  66.5 0.5 collective-permute-start.13
  67.0 0.7 collective-permute-done.8.refs_2_
  67.7 0.0 collective-permute-start.9
  67.8 0.0 collective-permute-done.7.refs_1_
  67.8 0.3 collective-permute-done.11.refs_5_
  68.1 0.4 collective-permute-done.13.refs_7_
  68.4 0.9 collective-permute-done.9.refs_3_
  69.3 2.4 %shard_map.93 = (bf16[1040,128]{1,0:T(8,128)(2,1)S(1)}, bf16[1040,128]{1,0:T(8,128)(2,1)S(1)}) custom-call(s32[832]{0:T(1024)S(1)} %get-tuple-element.30.codes, s32[8]{0:T(128)S(1)} %get-tuple-element.20.counts, bf16[320,128,128]{2,1,0:T(8,128)(2,1)S(1)} %bitcast.5, bf16[1024,128]{1,0:T(8,128)(2,1)S(1)} %get-tuple-element.31.refs_0_, ...), custom_call_target="tpu_custom_call" | custom-call | flops 2684354560 | bytes 2621440 | tf_op jit(solution)/shard_map/pallas_call | solution.py:272
  71.7 0.9 collective-permute-start.15
  72.6 0.0 copy-start.3
  72.6 0.3 collective-permute-start.16
  73.0 2.4 %shard_map.92 = (bf16[1040,128]{1,0:T(8,128)(2,1)S(1)}, bf16[1040,128]{1,0:T(8,128)(2,1)S(1)}) custom-call(s32[832]{0:T(1024)S(1)} %get-tuple-element.30.codes, s32[8]{0:T(128)S(1)} %get-tuple-element.20.counts, bf16[320,128,128]{2,1,0:T(8,128)(2,1)S(1)} %bitcast.6, bf16[1024,128]{1,0:T(8,128)(2,1)S(1)} %get-tuple-element.31.refs_0_, ...), custom_call_target="tpu_custom_call" | custom-call | flops 2684354560 | bytes 2621440 | tf_op jit(solution)/shard_map/pallas_call | solution.py:272
  75.4 1.8 %collective-permute-start.14 = (bf16[1040,128]{1,0:T(8,128)(2,1)S(1)}, bf16[1040,128]{1,0:T(8,128)(2,1)S(1)}, u32[]{:S(2)}, u32[]{:S(2)}) collective-permute-start(bf16[1040,128]{1,0:T(8,128)(2,1)S(1)} %get-tuple-element.33), channel_id=1, source_target_pairs={{0,8},{8,0},{16,24},{24,16},{1,9},{9,1},{17,25},{25,17},{2,10},{10... | collective-permute-start | bytes 798728 | tf_op jit(solution)/shard_map/ppermute | solution.py:389
  77.2 14.6 %collective-permute-done.15.refs_2_ = bf16[1040,128]{1,0:T(8,128)(2,1)S(1)} collective-permute-done((bf16[1040,128]{1,0:T(8,128)(2,1)S(1)}, bf16[1040,128]{1,0:T(8,128)(2,1)S(1)}, u32[]{:S(2)}, u32[]{:S(2)}) %collective-permute-start.15) | collective-permute-done | bytes 266272 | tf_op jit(solution)/shard_map/ppermute | solution.py:389
  91.8 0.0 collective-permute-done.16.refs_3_
  91.8 3.4 %collective-permute-done.14.refs_1_ = bf16[1040,128]{1,0:T(8,128)(2,1)S(1)} collective-permute-done((bf16[1040,128]{1,0:T(8,128)(2,1)S(1)}, bf16[1040,128]{1,0:T(8,128)(2,1)S(1)}, u32[]{:S(2)}, u32[]{:S(2)}) %collective-permute-start.14) | collective-permute-done | bytes 266272 | tf_op jit(solution)/shard_map/ppermute | solution.py:389
  95.2 0.0 copy-done.3
  95.2 1.1 %shard_map.94 = f32[1024,128]{1,0:T(8,128)} custom-call(s32[8,128]{1,0:T(8,128)S(1)} %bitcast.7, bf16[1040,128]{1,0:T(8,128)(2,1)S(1)} %get-tuple-element.32.refs_0_, bf16[1040,128]{1,0:T(8,128)(2,1)S(1)} %collective-permute-done.14.refs_1_, bf16[1040,128]{1,0:T(8,128)(2,1)S(1)} %collective-permute-done.15.refs_2_, ...), custom_call_target="tpu_custom_call" | custom-call | tf_op jit(solution)/shard_map/pallas_call | solution.py:378
  (1 shorter events, 0.0 us)
Async XLA Ops:
  0.6 1.0 %copy-start.2 = (f32[1024,128]{1,0:T(8,128)S(1)}, f32[1024,128]{1,0:T(8,128)}, u32[]{:S(2)}) copy-start(f32[1024,128]{1,0:T(8,128)} %video_ref.1) | copy-start | bytes 1572868
  1.7 15.0 %collective-permute-start = (bf16[1024,128]{1,0:T(8,128)(2,1)S(1)}, bf16[1024,128]{1,0:T(8,128)(2,1)S(1)}, u32[]{:S(2)}, u32[]{:S(2)}) collective-permute-start(bf16[1024,128]{1,0:T(8,128)(2,1)S(1)} %shard_map.87.refs_0_), channel_id=1, source_target_pairs={{0,8},{8,0},{16,24},{24,16},{1,9},{9,1},{17,25},{25,17},{2,10},{10... | collective-permute-start | bytes 786440 | tf_op jit(solution)/shard_map/ppermute | solution.py:389
  4.8 21.4 %collective-permute-start.1 = (bf16[1024,128]{1,0:T(8,128)(2,1)S(1)}, bf16[1024,128]{1,0:T(8,128)(2,1)S(1)}, u32[]{:S(2)}, u32[]{:S(2)}) collective-permute-start(bf16[1024,128]{1,0:T(8,128)(2,1)S(1)} %shard_map.87.refs_0_), channel_id=1, source_target_pairs={{0,16},{8,24},{16,0},{24,8},{1,17},{9,25},{17,1},{25,9},{2,18},{10... | collective-permute-start | bytes 786440 | tf_op jit(solution)/shard_map/ppermute | solution.py:389
  7.4 18.8 %collective-permute-start.2 = (bf16[1024,128]{1,0:T(8,128)(2,1)S(1)}, bf16[1024,128]{1,0:T(8,128)(2,1)S(1)}, u32[]{:S(2)}, u32[]{:S(2)}) collective-permute-start(bf16[1024,128]{1,0:T(8,128)(2,1)S(1)} %shard_map.87.refs_0_), channel_id=1, source_target_pairs={{0,24},{8,16},{16,8},{24,0},{1,25},{9,17},{17,9},{25,1},{2,26},{10... | collective-permute-start | bytes 786440 | tf_op jit(solution)/shard_map/ppermute | solution.py:389
  8.0 4.0 %copy-start = (bf16[1,1,320,128,128]{4,3,2,1,0:T(8,128)(2,1)S(1)}, bf16[1,1,320,128,128]{4,3,2,1,0:T(8,128)(2,1)}, u32[]{:S(2)}) copy-start(bf16[1,1,320,128,128]{4,3,2,1,0:T(8,128)(2,1)} %param.10) | copy-start | bytes 31457284
  12.0 0.7 copy-start.4
  12.7 0.7 copy-start.5
  13.4 4.0 %copy-start.1 = (bf16[1,1,320,128,128]{4,3,2,1,0:T(8,128)(2,1)S(1)}, bf16[1,1,320,128,128]{4,3,2,1,0:T(8,128)(2,1)}, u32[]{:S(2)}) copy-start(bf16[1,1,320,128,128]{4,3,2,1,0:T(8,128)(2,1)} %param.10) | copy-start | bytes 31457284
  29.0 2.7 %collective-permute-start.3 = (bf16[4,1040,128]{2,1,0:T(8,128)(2,1)S(1)}, bf16[4,1040,128]{2,1,0:T(8,128)(2,1)S(1)}, u32[]{:S(2)}, u32[]{:S(2)}) collective-permute-start(bf16[4,1040,128]{2,1,0:T(8,128)(2,1)S(1)} %get-tuple-element.24), channel_id=1, source_target_pairs={{0,1},{1,0},{2,3},{3,2},{4,5},{5,4},{6,7},{7,6},{8,9},{9,8},{10,11... | collective-permute-start | bytes 3194888 | tf_op jit(solution)/shard_map/ppermute | solution.py:389
  31.8 7.8 %copy-start.6 = (s32[1024]{0:T(1024)S(1)}, s32[1024]{0:T(1024)}, u32[]{:S(2)}) copy-start(s32[1024]{0:T(1024)} %param.8) | copy-start | bytes 12292
  32.1 8.5 %collective-permute-start.4 = (bf16[1040,128]{1,0:T(8,128)(2,1)S(1)}, bf16[1040,128]{1,0:T(8,128)(2,1)S(1)}, u32[]{:S(2)}, u32[]{:S(2)}) collective-permute-start(bf16[1040,128]{1,0:T(8,128)(2,1)S(1)} %get-tuple-element.26), channel_id=1, source_target_pairs={{0,2},{1,3},{2,0},{3,1},{4,6},{5,7},{6,4},{7,5},{8,10},{9,11},{10,... | collective-permute-start | bytes 798728 | tf_op jit(solution)/shard_map/ppermute | solution.py:389
  33.1 17.0 %collective-permute-start.5 = (bf16[1040,128]{1,0:T(8,128)(2,1)S(1)}, bf16[1040,128]{1,0:T(8,128)(2,1)S(1)}, u32[]{:S(2)}, u32[]{:S(2)}) collective-permute-start(bf16[1040,128]{1,0:T(8,128)(2,1)S(1)} %get-tuple-element.27), channel_id=1, source_target_pairs={{0,4},{1,5},{2,6},{3,7},{4,0},{5,1},{6,2},{7,3},{8,12},{9,13},{10,... | collective-permute-start | bytes 798728 | tf_op jit(solution)/shard_map/ppermute | solution.py:389
  38.2 13.7 %collective-permute-start.6 = (bf16[1040,128]{1,0:T(8,128)(2,1)S(1)}, bf16[1040,128]{1,0:T(8,128)(2,1)S(1)}, u32[]{:S(2)}, u32[]{:S(2)}) collective-permute-start(bf16[1040,128]{1,0:T(8,128)(2,1)S(1)} %get-tuple-element.28), channel_id=1, source_target_pairs={{0,6},{1,7},{2,4},{3,5},{4,2},{5,3},{6,0},{7,1},{8,14},{9,15},{10,... | collective-permute-start | bytes 798728 | tf_op jit(solution)/shard_map/ppermute | solution.py:389
  53.1 13.4 %collective-permute-start.10 = (bf16[1024,128]{1,0:T(8,128)(2,1)S(1)}, bf16[1024,128]{1,0:T(8,128)(2,1)S(1)}, u32[]{:S(2)}, u32[]{:S(2)}) collective-permute-start(bf16[1024,128]{1,0:T(8,128)(2,1)S(1)} %get-tuple-element.31.refs_0_), channel_id=1, source_target_pairs={{0,4},{1,5},{2,6},{3,7},{4,0},{5,1},{6,2},{7,3},{8,12},{9,13},{10,... | collective-permute-start | bytes 786440 | tf_op jit(solution)/shard_map/ppermute | solution.py:389
  53.8 12.7 %collective-permute-start.12 = (bf16[1024,128]{1,0:T(8,128)(2,1)S(1)}, bf16[1024,128]{1,0:T(8,128)(2,1)S(1)}, u32[]{:S(2)}, u32[]{:S(2)}) collective-permute-start(bf16[1024,128]{1,0:T(8,128)(2,1)S(1)} %get-tuple-element.31.refs_0_), channel_id=1, source_target_pairs={{0,6},{1,7},{2,4},{3,5},{4,2},{5,3},{6,0},{7,1},{8,14},{9,15},{10,... | collective-permute-start | bytes 786440 | tf_op jit(solution)/shard_map/ppermute | solution.py:389
  55.2 12.6 %collective-permute-start.8 = (bf16[1024,128]{1,0:T(8,128)(2,1)S(1)}, bf16[1024,128]{1,0:T(8,128)(2,1)S(1)}, u32[]{:S(2)}, u32[]{:S(2)}) collective-permute-start(bf16[1024,128]{1,0:T(8,128)(2,1)S(1)} %get-tuple-element.31.refs_0_), channel_id=1, source_target_pairs={{0,2},{1,3},{2,0},{3,1},{4,6},{5,7},{6,4},{7,5},{8,10},{9,11},{10,... | collective-permute-start | bytes 786440 | tf_op jit(solution)/shard_map/ppermute | solution.py:389
  56.6 11.1 %collective-permute-start.7 = (bf16[1024,128]{1,0:T(8,128)(2,1)S(1)}, bf16[1024,128]{1,0:T(8,128)(2,1)S(1)}, u32[]{:S(2)}, u32[]{:S(2)}) collective-permute-start(bf16[1024,128]{1,0:T(8,128)(2,1)S(1)} %get-tuple-element.31.refs_0_), channel_id=1, source_target_pairs={{0,1},{1,0},{2,3},{3,2},{4,5},{5,4},{6,7},{7,6},{8,9},{9,8},{10,11... | collective-permute-start | bytes 786440 | tf_op jit(solution)/shard_map/ppermute | solution.py:389
  66.5 1.5 %collective-permute-start.11 = (bf16[1024,128]{1,0:T(8,128)(2,1)S(1)}, bf16[1024,128]{1,0:T(8,128)(2,1)S(1)}, u32[]{:S(2)}, u32[]{:S(2)}) collective-permute-start(bf16[1024,128]{1,0:T(8,128)(2,1)S(1)} %collective-permute-done.10.refs_4_), channel_id=1, source_target_pairs={{0,1},{1,0},{2,3},{3,2},{4,5},{5,4},{6,7},{7,6},{8,9},{9,8},{10,11... | collective-permute-start | bytes 786440 | tf_op jit(solution)/shard_map/ppermute | solution.py:389
  66.5 1.9 %collective-permute-start.13 = (bf16[1024,128]{1,0:T(8,128)(2,1)S(1)}, bf16[1024,128]{1,0:T(8,128)(2,1)S(1)}, u32[]{:S(2)}, u32[]{:S(2)}) collective-permute-start(bf16[1024,128]{1,0:T(8,128)(2,1)S(1)} %collective-permute-done.12.refs_6_), channel_id=1, source_target_pairs={{0,1},{1,0},{2,3},{3,2},{4,5},{5,4},{6,7},{7,6},{8,9},{9,8},{10,11... | collective-permute-start | bytes 786440 | tf_op jit(solution)/shard_map/ppermute | solution.py:389
  67.7 1.5 %collective-permute-start.9 = (bf16[1024,128]{1,0:T(8,128)(2,1)S(1)}, bf16[1024,128]{1,0:T(8,128)(2,1)S(1)}, u32[]{:S(2)}, u32[]{:S(2)}) collective-permute-start(bf16[1024,128]{1,0:T(8,128)(2,1)S(1)} %collective-permute-done.8.refs_2_), channel_id=1, source_target_pairs={{0,1},{1,0},{2,3},{3,2},{4,5},{5,4},{6,7},{7,6},{8,9},{9,8},{10,11... | collective-permute-start | bytes 786440 | tf_op jit(solution)/shard_map/ppermute | solution.py:389
  71.7 20.1 %collective-permute-start.15 = (bf16[1040,128]{1,0:T(8,128)(2,1)S(1)}, bf16[1040,128]{1,0:T(8,128)(2,1)S(1)}, u32[]{:S(2)}, u32[]{:S(2)}) collective-permute-start(bf16[1040,128]{1,0:T(8,128)(2,1)S(1)} %get-tuple-element.34), channel_id=1, source_target_pairs={{0,16},{8,24},{16,0},{24,8},{1,17},{9,25},{17,1},{25,9},{2,18},{10... | collective-permute-start | bytes 798728 | tf_op jit(solution)/shard_map/ppermute | solution.py:389
  72.6 22.5 %copy-start.3 = (s32[1024]{0:T(1024)S(1)}, s32[1024]{0:T(1024)}, u32[]{:S(2)}) copy-start(s32[1024]{0:T(1024)} %param.9) | copy-start | bytes 12292
  72.6 19.1 %collective-permute-start.16 = (bf16[1040,128]{1,0:T(8,128)(2,1)S(1)}, bf16[1040,128]{1,0:T(8,128)(2,1)S(1)}, u32[]{:S(2)}, u32[]{:S(2)}) collective-permute-start(bf16[1040,128]{1,0:T(8,128)(2,1)S(1)} %get-tuple-element.35), channel_id=1, source_target_pairs={{0,24},{8,16},{16,8},{24,0},{1,25},{9,17},{17,9},{25,1},{2,26},{10... | collective-permute-start | bytes 798728 | tf_op jit(solution)/shard_map/ppermute | solution.py:389
  75.4 19.8 %collective-permute-start.14 = (bf16[1040,128]{1,0:T(8,128)(2,1)S(1)}, bf16[1040,128]{1,0:T(8,128)(2,1)S(1)}, u32[]{:S(2)}, u32[]{:S(2)}) collective-permute-start(bf16[1040,128]{1,0:T(8,128)(2,1)S(1)} %get-tuple-element.33), channel_id=1, source_target_pairs={{0,8},{8,0},{16,24},{24,16},{1,9},{9,1},{17,25},{25,17},{2,10},{10... | collective-permute-start | bytes 798728 | tf_op jit(solution)/shard_map/ppermute | solution.py:389

commit v4 on v3

v4 whole, which is shorter than its diff:
```python
import functools

import jax
import jax.numpy as jnp
from jax import lax
from jax.experimental import pallas as pl
from jax.experimental.pallas import tpu as pltpu
from jax.sharding import PartitionSpec as P

BLEND = 0.75
GROUP = 32
PLACE = 8
NT = (((1,), (1,)), ((), ()))
VMEM = pl.BlockSpec(memory_space=pltpu.VMEM)


def params(mib):
    return pltpu.CompilerParams(vmem_limit_bytes=mib * 2**20)


def split_half(mass):
    high = mass.astype(jnp.bfloat16)
    low = (mass - high.astype(jnp.float32)).astype(jnp.bfloat16)
    return jnp.concatenate([high.astype(jnp.float32), low.astype(jnp.float32)], axis=0).astype(
        jnp.bfloat16
    )


def prep_kernel(video_ref, out_ref):
    out_ref[...] = video_ref[...].astype(jnp.bfloat16)


def prep(video):
    return pl.pallas_call(
        prep_kernel,
        out_shape=jax.ShapeDtypeStruct(video.shape, jnp.bfloat16),
        in_specs=[VMEM],
        out_specs=VMEM,
        compiler_params=params(48),
    )(video)


def plan_kernel(rows, cols, live_ref, _, codes_ref, counts, *, cap, half, shard):
    row_mask, col_mask = lax.axis_index("row") * shard, lax.axis_index("col") * shard
    live = live_ref[0, 0]
    trash = 3 * cap

    def place(block, carry):
        own, near, far = carry
        base = block * PLACE
        found = [(rows[0, 0, base + k], cols[0, 0, base + k]) for k in range(PLACE)]
        for k, (row, col) in enumerate(found):
            slot = base + k
            row, col = row ^ col_mask, col ^ row_mask
            is_far = col >= half
            is_own = col < shard
            spot = jnp.where(is_far, 2 * cap + far, jnp.where(is_own, own, cap + near))
            codes_ref[jnp.where(slot < live, spot, trash)] = slot | (col << 12) | (row << 20)
            one = (slot < live).astype(jnp.int32)
            near += jnp.where(is_far | is_own, 0, one)
            own += jnp.where(is_own, one, 0)
            far += jnp.where(is_far, one, 0)
        return own, near, far

    zero = jnp.int32(0)
    found = lax.fori_loop(0, lax.div(live + (PLACE - 1), PLACE), place, (zero, zero, zero))
    row_dummy = (lax.axis_size("col") * shard) << 20
    for n, count in enumerate(found):
        counts[n] = count
    for n, count in enumerate(found):
        dummy = row_dummy | ((half if n < 2 else 2 * half) << 12)

        def pad(k, carry):
            codes_ref[n * cap + count + k] = dummy
            return carry

        lax.fori_loop(0, GROUP, pad, 0)


def plan(rows, cols, live, tiles, col_tiles, shard):
    cap = rows.shape[2] + GROUP
    smem = pl.BlockSpec(memory_space=pltpu.SMEM)
    return pl.pallas_call(
        functools.partial(plan_kernel, cap=cap, half=col_tiles // 2, shard=shard),
        out_shape=[
            jax.ShapeDtypeStruct((3 * cap + 128,), jnp.int32),
            jax.ShapeDtypeStruct((3,), jnp.int32),
        ],
        in_specs=[smem] * 3 + [VMEM],
        out_specs=[smem] * 2,
        compiler_params=grant(0, [tiles]),
    )(rows, cols, live, tiles)


def walk(codes, counts, lists, visit):
    cap = (codes.shape[0] - 128) // 3
    for n in lists:

        def group(g, carry):
            for k in range(GROUP):
                code = codes[n * cap + g * GROUP + k]
                col = lax.shift_right_logical(code, 12) & 0xFF
                visit(code & 0xFFF, col, lax.shift_right_logical(code, 20))
            return carry

        lax.fori_loop(0, lax.div(counts[n] + (GROUP - 1), GROUP), group, 0)


def fill_panel(panel, piece_refs):
    tiles = piece_refs[0].shape[0] // 128
    for m, piece in enumerate(piece_refs):
        for t in range(tiles):
            panel[m * tiles + t] = piece[t * 128 : (t + 1) * 128, :]


def clear(*sums):
    def one(n, carry):
        for ref in sums:
            ref[n] = jnp.zeros(ref.shape[1:], jnp.float32)
        return carry

    lax.fori_loop(0, sums[0].shape[0] - 1, one, 0)


def fold_rows(tile):
    return jnp.sum(tile.reshape(16, 8, 128), axis=0)


def early_kernel(codes, counts, tiles_ref, *refs):
    *piece_refs, sums_ref, weights_ref, panel, acc, mass = refs
    fill_panel(panel, piece_refs)
    clear(acc, mass)
    ones = jnp.ones((16, 128), jnp.bfloat16)

    def multiply(slot, col, row):
        part = panel[col & (panel.shape[0] - 1)]
        acc[row] += jnp.dot(tiles_ref[slot], part, preferred_element_type=jnp.float32)

    def weigh(slot, col, row):
        sums = lax.dot_general(ones, tiles_ref[slot], NT, preferred_element_type=jnp.float32)
        mass[row] += sums[:8]

    walk(codes, counts, [0], multiply)
    walk(codes, counts, [0, 1, 2], weigh)

    def hand(n, carry):
        sums_ref[n] = acc[n]
        weights_ref[n] = mass[n]
        return carry

    lax.fori_loop(0, acc.shape[0] - 1, hand, 0)


def grant(scratch, arrays):
    size = sum(x.size * x.dtype.itemsize for x in arrays)
    return params((scratch + (size if size > 24 * 2**20 else 0)) // 2**20 + 5)


def effort(slots):
    average = slots // 4
    return pl.CostEstimate(
        flops=16 * average * 128**3, bytes_accessed=average * 128 * 256, transcendentals=0
    )


def early_sweep(codes, counts, tiles, pieces, row_tiles):
    smem, slots = pl.BlockSpec(memory_space=pltpu.SMEM), tiles.shape[0]
    out_shape = [
        jax.ShapeDtypeStruct((row_tiles, 128, 128), jnp.float32),
        jax.ShapeDtypeStruct((row_tiles, 8, 128), jnp.float32),
    ]
    scratch = 4 * (row_tiles + 1) * 136 * 128 + sum(p.size for p in pieces) * 2
    return pl.pallas_call(
        early_kernel,
        in_specs=[smem] * 2 + [VMEM] * (1 + len(pieces)),
        out_specs=[VMEM] * 2,
        scratch_shapes=[
            pltpu.VMEM((sum(p.shape[0] for p in pieces) // 128, 128, 128), jnp.bfloat16),
            pltpu.VMEM((row_tiles + 1, 128, 128), jnp.float32),
            pltpu.VMEM((row_tiles + 1, 8, 128), jnp.float32),
        ],
        out_shape=out_shape,
        compiler_params=grant(scratch, [tiles, *pieces, *out_shape]),
        cost_estimate=effort(slots),
    )(codes, counts, tiles, *pieces)


def late_kernel(codes, counts, tiles_ref, sums_ref, weights_ref, *refs, shard):
    count_out = sums_ref.shape[0] // shard
    piece_refs, out_refs, (panel, acc) = refs[: -2 - count_out], refs[-2 - count_out : -2], refs[-2:]
    fill_panel(panel.at[pl.ds(shard, panel.shape[0] - shard)], piece_refs)
    panel[0] = jnp.zeros((128, 128), jnp.bfloat16)

    def begin(n, carry):
        acc[n] = sums_ref[n]
        return carry

    lax.fori_loop(0, sums_ref.shape[0], begin, 0)

    def multiply(slot, col, row):
        part = panel[col & (panel.shape[0] - 1)]
        acc[row] += jnp.dot(tiles_ref[slot], part, preferred_element_type=jnp.float32)

    walk(codes, counts, [1, 2], multiply)
    for n, target in enumerate(out_refs):
        tops = []
        for t in range(shard):
            target[t * 128 : (t + 1) * 128, :] = acc[n * shard + t].astype(jnp.bfloat16)
            tops.append(weights_ref[n * shard + t, 0:1, :])
        target[shard * 128 :, :] = split_half(jnp.concatenate(tops, axis=0))


def late_sweep(codes, counts, tiles, sums, weights, pieces, shard):
    smem, slots, row_tiles = pl.BlockSpec(memory_space=pltpu.SMEM), tiles.shape[0], sums.shape[0]
    rows = shard * 130
    out_shape = [jax.ShapeDtypeStruct((rows, 128), jnp.bfloat16)] * (row_tiles // shard)
    scratch = 4 * (row_tiles + 1) * 128**2 + sum(p.size for p in pieces) * 2
    return pl.pallas_call(
        functools.partial(late_kernel, shard=shard),
        in_specs=[smem] * 2 + [VMEM] * (3 + len(pieces)),
        out_specs=[VMEM] * len(out_shape),
        scratch_shapes=[
            pltpu.VMEM((shard + sum(p.shape[0] for p in pieces) // 128, 128, 128), jnp.bfloat16),
            pltpu.VMEM((row_tiles + 1, 128, 128), jnp.float32),
        ],
        out_shape=out_shape,
        compiler_params=grant(scratch, [tiles, sums, weights, *pieces, *out_shape]),
        cost_estimate=effort(slots),
    )(codes, counts, tiles, sums, weights, *pieces)


def reverse_kernel(codes, counts, tiles_ref, *refs, pieces, lists, first, shard):
    piece_refs, out_refs, (panel, acc, mass) = refs[:pieces][::-1], refs[pieces:-3], refs[-3:]
    fill_panel(panel, piece_refs)
    clear(acc, mass)

    def multiply(slot, col, row):
        tile, part = tiles_ref[slot], panel[row & (panel.shape[0] - 1)]
        acc[col - first] += jnp.dot(part, tile, preferred_element_type=jnp.float32)
        mass[col - first] += fold_rows(tile.astype(jnp.float32))

    walk(codes, counts, lists, multiply)
    for n, target in enumerate(out_refs):
        tops = []
        for t in range(shard):
            target[t * 128 : (t + 1) * 128, :] = acc[n * shard + t].astype(jnp.bfloat16)
            tops.append(jnp.sum(mass[n * shard + t], axis=0, keepdims=True))
        target[shard * 128 :, :] = split_half(jnp.concatenate(tops, axis=0))


def reverse_sweep(codes, counts, lists, first, tiles, pieces, col_tiles, shard):
    smem, slots = pl.BlockSpec(memory_space=pltpu.SMEM), tiles.shape[0]
    out_shape = [jax.ShapeDtypeStruct((shard * 130, 128), jnp.bfloat16)] * (col_tiles // shard)
    scratch = 4 * (col_tiles + 1) * 136 * 128 + sum(p.size for p in pieces) * 2
    return pl.pallas_call(
        functools.partial(
            reverse_kernel,
            pieces=len(pieces),
            lists=lists,
            first=first,
            shard=shard,
        ),
        in_specs=[smem] * 2 + [VMEM] * (1 + len(pieces)),
        out_specs=[VMEM] * len(out_shape),
        scratch_shapes=[
            pltpu.VMEM((sum(p.shape[0] for p in pieces) // 128, 128, 128), jnp.bfloat16),
            pltpu.VMEM((col_tiles + 1, 128, 128), jnp.float32),
            pltpu.VMEM((col_tiles + 1, 8, 128), jnp.float32),
        ],
        out_shape=out_shape,
        compiler_params=grant(scratch, [tiles, *pieces, *out_shape]),
        cost_estimate=effort(slots),
    )(codes, counts, tiles, *pieces)


def pair_sum_kernel(keep_ref, got_ref, out_ref, *, body_rows):
    total = keep_ref[:body_rows].astype(jnp.float32) + got_ref[:body_rows].astype(jnp.float32)
    out_ref[:body_rows, :] = total.astype(out_ref.dtype)
    mass = both_halves(keep_ref[body_rows:]) + both_halves(got_ref[body_rows:])
    if out_ref.dtype == jnp.float32:
        out_ref[body_rows:, :] = jnp.concatenate([mass, jnp.zeros_like(mass)], axis=0)
    else:
        out_ref[body_rows:, :] = split_half(mass)


def both_halves(block):
    wide = block.astype(jnp.float32)
    half = wide.shape[0] // 2
    return wide[:half] + wide[half:]


def pair_sum(keep, got, body_rows, kind):
    return pl.pallas_call(
        functools.partial(pair_sum_kernel, body_rows=body_rows),
        out_shape=jax.ShapeDtypeStruct(keep.shape, kind),
        in_specs=[VMEM] * 2,
        out_specs=VMEM,
        compiler_params=params(48),
    )(keep, got)


def mix(total, scale, seeds, t):
    classes = lax.broadcasted_iota(jnp.int32, (128, 128), 0)
    labels = jnp.where(classes == seeds[t : t + 1, :], 1.0 - BLEND, 0.0)
    return total * scale[t : t + 1, :] + labels


def audio_kernel(seed_ref, own_ref, *refs, shard):
    got, (half_ref, turned_ref) = refs[:-2], refs[-2:]
    body = shard * 128
    mass = own_ref[body : body + shard, :]
    for g in got:
        mass += both_halves(g[body:])
    scale = BLEND / jnp.sqrt(mass)
    seeds = seed_ref[...]
    for t in range(shard):
        span = slice(t * 128, (t + 1) * 128)
        total = own_ref[span, :]
        for g in got:
            total += g[span, :].astype(jnp.float32)
        scores = mix(total.T, scale, seeds, t)
        turned_ref[span, :] = scores
        half_ref[span, :] = scores.astype(jnp.bfloat16)


def audio_blend(seeds, own, got):
    shard = seeds.shape[0]
    shape = (shard * 128, 128)
    return pl.pallas_call(
        functools.partial(audio_kernel, shard=shard),
        out_shape=[
            jax.ShapeDtypeStruct(shape, jnp.bfloat16),
            jax.ShapeDtypeStruct(shape, jnp.float32),
        ],
        in_specs=[VMEM] * (2 + len(got)),
        out_specs=[VMEM] * 2,
        compiler_params=params(48),
    )(seeds, own, *got)


def flip_kernel(turned_ref, out_ref):
    for t in range(out_ref.shape[0] // 128):
        span = slice(t * 128, (t + 1) * 128)
        out_ref[span, :] = turned_ref[span, :].T


def flip(turned):
    return pl.pallas_call(
        flip_kernel,
        out_shape=jax.ShapeDtypeStruct(turned.shape, jnp.float32),
        in_specs=[VMEM],
        out_specs=VMEM,
        compiler_params=params(48),
    )(turned)


def video_kernel(seed_ref, *refs, shard):
    got, out_ref = refs[:-1], refs[-1]
    body = shard * 128
    scale = BLEND / jnp.sqrt(sum(both_halves(r[body:]) for r in got))
    seeds = seed_ref[...]
    for t in range(shard):
        span = slice(t * 128, (t + 1) * 128)
        total = sum(r[span, :].astype(jnp.float32) for r in got)
        out_ref[span, :] = mix(total, scale, seeds, t).T


def video_blend(seeds, pieces):
    shard = seeds.shape[0]
    return pl.pallas_call(
        functools.partial(video_kernel, shard=shard),
        out_shape=jax.ShapeDtypeStruct((shard * 128, 128), jnp.float32),
        in_specs=[VMEM] * (1 + len(pieces)),
        out_specs=VMEM,
        compiler_params=params(48),
    )(seeds, *pieces)


def partner(value, axis, mask):
    size = lax.axis_size(axis)
    return lax.ppermute(value, axis, [(i, i ^ mask) for i in range(size)])


def body(video_scores_in, audio_seed, video_seed, tile_values, tile_rows, tile_cols, tile_count):
    tiles = tile_values[0, 0]
    shard = video_scores_in.shape[0] // 128
    n_row, n_col = lax.axis_size("row"), lax.axis_size("col")
    row_tiles, col_tiles = n_col * shard, n_row * shard
    audio_seeds = audio_seed.reshape(shard, 128)
    video_seeds = video_seed.reshape(shard, 128)

    own = prep(video_scores_in)
    others = [partner(own, "row", m) for m in range(1, n_row)]
    codes, counts = plan(tile_rows, tile_cols, tile_count, tiles, col_tiles, shard)
    sums, weights = early_sweep(codes, counts, tiles, [own], row_tiles)
    payloads = late_sweep(codes, counts, tiles, sums, weights, others, shard)
    owned = {}
    for n in [*range(2, n_col, 2), 0]:
        kind = jnp.bfloat16 if n else jnp.float32
        got = partner(payloads[n + 1], "col", 1)
        owned[n] = pair_sum(payloads[n], got, shard * 128, kind)
    arrived = [partner(owned[n], "col", n) for n in range(2, n_col, 2)]
    half, turned = audio_blend(audio_seeds, owned[0], arrived)

    mine = [half] + [partner(half, "col", m) for m in range(2, n_col, 2)]
    pieces = [q for p in mine for q in (p, partner(p, "col", 1))]
    half_tiles = col_tiles // 2
    pieces = pieces[::-1]
    far = reverse_sweep(codes, counts, [2], half_tiles, tiles, pieces, half_tiles, shard)
    near = reverse_sweep(codes, counts, [0, 1], 0, tiles, pieces, half_tiles, shard)
    sums = list(near) + list(far)
    results = [sums[0]] + [partner(sums[m], "row", m) for m in range(1, n_row)]
    return flip(turned), video_blend(video_seeds, results)


def solution(mesh):
    in_specs = (
        P(("col", "row"), None),
        P(("row", "col")),
        P(("col", "row")),
        P("row", "col", None, None, None),
        P("row", "col", None),
        P("row", "col", None),
        P("row", "col"),
    )
    out_specs = (P(("row", "col"), None), P(("col", "row"), None))
    return jax.shard_map(body, mesh=mesh, in_specs=in_specs, out_specs=out_specs, check_vma=False)
```

time: 95.8 us -> 95.1 us (level)
  starting transfers between devices: 20.4 us -> 18.6 us
  Pallas kernels: 20.7 us -> 22.3 us
  waiting for transfers between devices: 46.5 us -> 45.5 us
    pallas_call x3 -> x4, Pallas kernels: 7.68 us -> 10 us  [the longest x2 5.27 us: reverse_sweep(): pl.pallas_call(functools.partial(reverse_kernel, pieces=len(pieces), list...]
    ppermute x17 -> x20, starting transfers between devices: 20.4 us -> 18.6 us  [partner(): return lax.ppermute(value, axis, [(i, i ^ mask) for i in range(size)])]
    ppermute x17 -> x20, waiting for transfers between devices: 46.5 us -> 45.5 us  [partner(): return lax.ppermute(value, axis, [(i, i ^ mask) for i in range(size)])]
    pallas_call x1, Pallas kernels: 1.2 us -> 0.24 us  [audio_blend(): pl.pallas_call(functools.partial(audio_kernel, shard=shard), out_shape=[j...]
  transfers between devices with their start and end apart: 17 -> 20, of which waited for: 12 -> 11; matrix products, arithmetic and copies ran while one was open for 0% -> 0% of each run, Pallas kernels for 13% -> 16%
where the time goes in v4:
time: 95.1 us; the launch traced here: 94.9 us
  waiting for transfers between devices  45.5 us (48%)
  Pallas kernels  22.3 us (23%)
  starting transfers between devices  18.6 us (20%)
  local copies, waits for them, and re-layouts  7.06 us (7%)
  between operations  1.4 us (1%)
    ppermute x20, waiting for transfers between devices, partner(): return lax.ppermute(value, axis, [(i, i ^ mask) for i in range(size)])  45.5 us
    ppermute x20, starting transfers between devices, partner(): return lax.ppermute(value, axis, [(i, i ^ mask) for i in range(size)])  18.6 us
    pallas_call x1, Pallas kernels, early_sweep(): pl.pallas_call(early_kernel, in_specs=[smem] * 2 + [VMEM] * (1 + len(piec...  7.37 us
    unnamed x14, local copies, waits for them, and re-layouts  7.06 us
    pallas_call x2, Pallas kernels, reverse_sweep(): pl.pallas_call(functools.partial(reverse_kernel, pieces=len(pieces), list...  5.27 us
    pallas_call x1, Pallas kernels, late_sweep(): pl.pallas_call(functools.partial(late_kernel, shard=shard), in_specs=[sme...  3.78 us
    pallas_call x1, Pallas kernels, plan(): pl.pallas_call(functools.partial(plan_kernel, cap=cap, half=col_tiles //...  3.29 us
  transfers between devices with their start and end apart: 20, of which 11 were waited for; matrix products, arithmetic and copies ran while one was open for 0% of the time, Pallas kernels for 16%

profile of v4, /device:TPU:0, one launch (start us, length us, event | category | flops | bytes accessed | tf_op | source)
XLA Modules:
  0.0 94.9 jit_solution(6011614548626584797)
XLA Ops:
  0.6 0.0 copy-start.2
  0.6 1.0 %copy-done.2 = f32[1024,128]{1,0:T(8,128)S(1)} copy-done((f32[1024,128]{1,0:T(8,128)S(1)}, f32[1024,128]{1,0:T(8,128)}, u32[]{:S(2)}) %copy-start.2) | copy-done | bytes 524312
  1.7 5.1 %collective-permute-start.2 = (bf16[1024,128]{1,0:T(8,128)(2,1)S(1)}, bf16[1024,128]{1,0:T(8,128)(2,1)S(1)}, u32[]{:S(2)}, u32[]{:S(2)}) collective-permute-start(bf16[1024,128]{1,0:T(8,128)(2,1)S(1)} %shard_map.87.refs_0_), channel_id=1, source_target_pairs={{0,24},{8,16},{16,8},{24,0},{1,25},{9,17},{17,9},{25,1},{2,26},{10... | collective-permute-start | bytes 786440 | tf_op jit(solution)/shard_map/ppermute | solution.py:381
  6.8 0.0 collective-permute-start.1
  6.8 0.6 collective-permute-start
  8.1 0.0 copy-start
  8.1 4.0 %copy-done = bf16[1,1,320,128,128]{4,3,2,1,0:T(8,128)(2,1)S(1)} copy-done((bf16[1,1,320,128,128]{4,3,2,1,0:T(8,128)(2,1)S(1)}, bf16[1,1,320,128,128]{4,3,2,1,0:T(8,128)(2,1)}, u32[]{:S(2)}) %copy-start) | copy-done | bytes 10485784
  12.1 0.0 copy-start.5
  12.1 0.7 copy-done.5
  12.8 0.7 copy-done.6
  13.5 3.3 %shard_map.86 = (s32[1184]{0:T(1024)S(1)}, s32[3]{0:T(128)S(1)}) custom-call(s32[1,1,320]{2,1,0:T(1,128)S(1)} %copy-done.5, s32[1,1,320]{2,1,0:T(1,128)S(1)} %copy-done.6, s32[1,1]{1,0:T(1,128)S(6)} %copy.9.live_ref, bf16[320,128,128]{2,1,0:T(8,128)(2,1)S(1)} %bitcast.3), custom_call_target="tpu_custom_call" | custom-call | tf_op jit(solution)/shard_map/pallas_call | solution.py:83
  16.8 0.7 copy-done.1
  17.4 7.4 %shard_map.88 = (f32[64,128,128]{2,1,0:T(8,128)S(1)}, f32[64,8,128]{2,1,0:T(8,128)S(1)}) custom-call(s32[1184]{0:T(1024)S(1)} %get-tuple-element.20.codes, s32[3]{0:T(128)S(1)} %get-tuple-element.21.counts, bf16[320,128,128]{2,1,0:T(8,128)(2,1)S(1)} %bitcast.4, bf16[1024,128]{1,0:T(8,128)(2,1)S(1)} %shard_map.87.refs_0_), custom_call_target="tpu_custom_call" | custom-call | flops 2684354560 | bytes 2621440 | tf_op jit(solution)/shard_map/pallas_call | solution.py:173
  24.8 0.0 copy-start.3
  24.8 0.0 collective-permute-done.2.refs_2_
  24.8 4.3 %collective-permute-done.1.refs_1_ = bf16[1024,128]{1,0:T(8,128)(2,1)S(1)} collective-permute-done((bf16[1024,128]{1,0:T(8,128)(2,1)S(1)}, bf16[1024,128]{1,0:T(8,128)(2,1)S(1)}, u32[]{:S(2)}, u32[]{:S(2)}) %collective-permute-start.1) | collective-permute-done | bytes 262176 | tf_op jit(solution)/shard_map/ppermute | solution.py:381
  29.1 0.0 collective-permute-done.refs_0_
  29.1 3.8 %shard_map.89 = (bf16[1040,128]{1,0:T(8,128)(2,1)S(1)}, bf16[1040,128]{1,0:T(8,128)(2,1)S(1)}, bf16[1040,128]{1,0:T(8,128)(2,1)S(1)}, bf16[1040,128]{1,0:T(8,128...) custom-call(s32[1184]{0:T(1024)S(1)} %get-tuple-element.20.codes, ...), custom_call_target="tpu_custom_call" | custom-call | flops 2684354560 | bytes 2621440 | tf_op jit(solution)/shard_map/pallas_call | solution.py:218
  32.9 0.7 collective-permute-start.4
  33.6 0.1 collective-permute-start.6
  33.7 0.4 collective-permute-start.8
  34.1 0.1 collective-permute-start.3
  34.2 0.6 collective-permute-done.4.got_ref
  34.8 0.1 shard_map.91
  34.8 0.3 collective-permute-start.5
  35.2 0.0 collective-permute-done.6.got_ref
  35.2 0.1 shard_map.92
  35.2 3.0 %collective-permute-start.7 = (bf16[1040,128]{1,0:T(8,128)(2,1)S(1)}, bf16[1040,128]{1,0:T(8,128)(2,1)S(1)}, u32[]{:S(2)}, u32[]{:S(2)}) collective-permute-start(bf16[1040,128]{1,0:T(8,128)(2,1)S(1)} %shard_map.92), channel_id=1, source_target_pairs={{0,4},{1,5},{2,6},{3,7},{4,0},{5,1},{6,2},{7,3},{8,12},{9,13},{10,... | collective-permute-start | bytes 798728 | tf_op jit(solution)/shard_map/ppermute | solution.py:381
  38.3 0.0 collective-permute-done.8.got_ref
  38.3 0.1 shard_map.93
  38.4 0.5 collective-permute-start.9
  38.9 0.0 collective-permute-done.3.got_ref
  38.9 0.1 shard_map.90.own_ref
  39.0 5.1 %collective-permute-done.5.refs_0_ = bf16[1040,128]{1,0:T(8,128)(2,1)S(1)} collective-permute-done((bf16[1040,128]{1,0:T(8,128)(2,1)S(1)}, bf16[1040,128]{1,0:T(8,128)(2,1)S(1)}, u32[]{:S(2)}, u32[]{:S(2)}) %collective-permute-start.5) | collective-permute-done | bytes 266272 | tf_op jit(solution)/shard_map/ppermute | solution.py:381
  44.1 5.5 %collective-permute-done.7.refs_1_ = bf16[1040,128]{1,0:T(8,128)(2,1)S(1)} collective-permute-done((bf16[1040,128]{1,0:T(8,128)(2,1)S(1)}, bf16[1040,128]{1,0:T(8,128)(2,1)S(1)}, u32[]{:S(2)}, u32[]{:S(2)}) %collective-permute-start.7) | collective-permute-done | bytes 266272 | tf_op jit(solution)/shard_map/ppermute | solution.py:381
  49.7 1.1 %collective-permute-done.9.refs_2_ = bf16[1040,128]{1,0:T(8,128)(2,1)S(1)} collective-permute-done((bf16[1040,128]{1,0:T(8,128)(2,1)S(1)}, bf16[1040,128]{1,0:T(8,128)(2,1)S(1)}, u32[]{:S(2)}, u32[]{:S(2)}) %collective-permute-start.9) | collective-permute-done | bytes 266272 | tf_op jit(solution)/shard_map/ppermute | solution.py:381
  50.7 0.0 copy-done.3
  50.7 0.2 shard_map.94
  51.0 0.0 copy-start.4
  51.0 1.1 %collective-permute-start.14 = (bf16[1024,128]{1,0:T(8,128)(2,1)S(1)}, bf16[1024,128]{1,0:T(8,128)(2,1)S(1)}, u32[]{:S(2)}, u32[]{:S(2)}) collective-permute-start(bf16[1024,128]{1,0:T(8,128)(2,1)S(1)} %get-tuple-element.33.refs_7_), channel_id=1, source_target_pairs={{0,2},{1,3},{2,0},{3,1},{4,6},{5,7},{6,4},{7,5},{8,10},{9,11},{10,... | collective-permute-start | bytes 786440 | tf_op jit(solution)/shard_map/ppermute | solution.py:381
  52.1 1.4 %collective-permute-start.12 = (bf16[1024,128]{1,0:T(8,128)(2,1)S(1)}, bf16[1024,128]{1,0:T(8,128)(2,1)S(1)}, u32[]{:S(2)}, u32[]{:S(2)}) collective-permute-start(bf16[1024,128]{1,0:T(8,128)(2,1)S(1)} %get-tuple-element.33.refs_7_), channel_id=1, source_target_pairs={{0,4},{1,5},{2,6},{3,7},{4,0},{5,1},{6,2},{7,3},{8,12},{9,13},{10,... | collective-permute-start | bytes 786440 | tf_op jit(solution)/shard_map/ppermute | solution.py:381
  53.5 1.0 %collective-permute-start.10 = (bf16[1024,128]{1,0:T(8,128)(2,1)S(1)}, bf16[1024,128]{1,0:T(8,128)(2,1)S(1)}, u32[]{:S(2)}, u32[]{:S(2)}) collective-permute-start(bf16[1024,128]{1,0:T(8,128)(2,1)S(1)} %get-tuple-element.33.refs_7_), channel_id=1, source_target_pairs={{0,6},{1,7},{2,4},{3,5},{4,2},{5,3},{6,0},{7,1},{8,14},{9,15},{10,... | collective-permute-start | bytes 786440 | tf_op jit(solution)/shard_map/ppermute | solution.py:381
  54.5 0.0 collective-permute-start.16
  54.5 5.8 %collective-permute-done.14.refs_5_ = bf16[1024,128]{1,0:T(8,128)(2,1)S(1)} collective-permute-done((bf16[1024,128]{1,0:T(8,128)(2,1)S(1)}, bf16[1024,128]{1,0:T(8,128)(2,1)S(1)}, u32[]{:S(2)}, u32[]{:S(2)}) %collective-permute-start.14) | collective-permute-done | bytes 262176 | tf_op jit(solution)/shard_map/ppermute | solution.py:381
  60.3 0.0 collective-permute-start.15
  60.3 4.6 %collective-permute-done.12.refs_3_ = bf16[1024,128]{1,0:T(8,128)(2,1)S(1)} collective-permute-done((bf16[1024,128]{1,0:T(8,128)(2,1)S(1)}, bf16[1024,128]{1,0:T(8,128)(2,1)S(1)}, u32[]{:S(2)}, u32[]{:S(2)}) %collective-permute-start.12) | collective-permute-done | bytes 262176 | tf_op jit(solution)/shard_map/ppermute | solution.py:381
  64.9 0.0 collective-permute-start.13
  64.9 0.0 collective-permute-done.10.refs_1_
  64.9 0.5 collective-permute-start.11
  65.4 0.0 collective-permute-done.16.refs_6_
  65.4 0.0 collective-permute-done.15.refs_4_
  65.4 1.0 %collective-permute-done.13.refs_2_ = bf16[1024,128]{1,0:T(8,128)(2,1)S(1)} collective-permute-done((bf16[1024,128]{1,0:T(8,128)(2,1)S(1)}, bf16[1024,128]{1,0:T(8,128)(2,1)S(1)}, u32[]{:S(2)}, u32[]{:S(2)}) %collective-permute-start.13) | collective-permute-done | bytes 262176 | tf_op jit(solution)/shard_map/ppermute | solution.py:381
  66.4 0.4 collective-permute-done.11.refs_0_
  66.8 2.4 %shard_map.97 = (bf16[1040,128]{1,0:T(8,128)(2,1)S(1)}, bf16[1040,128]{1,0:T(8,128)(2,1)S(1)}) custom-call(s32[1184]{0:T(1024)S(1)} %get-tuple-element.20.codes, s32[3]{0:T(128)S(1)} %get-tuple-element.21.counts, bf16[320,128,128]{2,1,0:T(8,128)(2,1)S(1)} %bitcast.6, bf16[1024,128]{1,0:T(8,128)(2,1)S(1)} %collective-permute-done.11.refs_0_, ...), custom_call_target="tpu_custom_call" | custom-call | flops 2684354560 | bytes 2621440 | tf_op jit(solution)/shard_map/pallas_call | solution.py:255
  69.2 0.1 collective-permute-start.18
  69.3 1.2 %collective-permute-start.19 = (bf16[1040,128]{1,0:T(8,128)(2,1)S(1)}, bf16[1040,128]{1,0:T(8,128)(2,1)S(1)}, u32[]{:S(2)}, u32[]{:S(2)}) collective-permute-start(bf16[1040,128]{1,0:T(8,128)(2,1)S(1)} %get-tuple-element.37), channel_id=1, source_target_pairs={{0,24},{8,16},{16,8},{24,0},{1,25},{9,17},{17,9},{25,1},{2,26},{10... | collective-permute-start | bytes 798728 | tf_op jit(solution)/shard_map/ppermute | solution.py:381
  70.5 2.9 %shard_map.96 = (bf16[1040,128]{1,0:T(8,128)(2,1)S(1)}, bf16[1040,128]{1,0:T(8,128)(2,1)S(1)}) custom-call(s32[1184]{0:T(1024)S(1)} %get-tuple-element.20.codes, s32[3]{0:T(128)S(1)} %get-tuple-element.21.counts, bf16[320,128,128]{2,1,0:T(8,128)(2,1)S(1)} %bitcast.7, bf16[1024,128]{1,0:T(8,128)(2,1)S(1)} %collective-permute-done.11.refs_0_, ...), custom_call_target="tpu_custom_call" | custom-call | flops 2684354560 | bytes 2621440 | tf_op jit(solution)/shard_map/pallas_call | solution.py:255
  73.4 2.4 %collective-permute-start.17 = (bf16[1040,128]{1,0:T(8,128)(2,1)S(1)}, bf16[1040,128]{1,0:T(8,128)(2,1)S(1)}, u32[]{:S(2)}, u32[]{:S(2)}) collective-permute-start(bf16[1040,128]{1,0:T(8,128)(2,1)S(1)} %get-tuple-element.35), channel_id=1, source_target_pairs={{0,8},{8,0},{16,24},{24,16},{1,9},{9,1},{17,25},{25,17},{2,10},{10... | collective-permute-start | bytes 798728 | tf_op jit(solution)/shard_map/ppermute | solution.py:381
  75.7 1.0 %shard_map.95 = f32[1024,128]{1,0:T(8,128)} custom-call(f32[1024,128]{1,0:T(8,128)S(1)} %get-tuple-element.32.turned_ref), custom_call_target="tpu_custom_call" | custom-call | tf_op jit(solution)/shard_map/pallas_call | solution.py:348
  76.7 11.9 %collective-permute-done.18.refs_2_ = bf16[1040,128]{1,0:T(8,128)(2,1)S(1)} collective-permute-done((bf16[1040,128]{1,0:T(8,128)(2,1)S(1)}, bf16[1040,128]{1,0:T(8,128)(2,1)S(1)}, u32[]{:S(2)}, u32[]{:S(2)}) %collective-permute-start.18) | collective-permute-done | bytes 266272 | tf_op jit(solution)/shard_map/ppermute | solution.py:381
  88.6 0.0 collective-permute-done.19.refs_3_
  88.6 5.3 %collective-permute-done.17.refs_1_ = bf16[1040,128]{1,0:T(8,128)(2,1)S(1)} collective-permute-done((bf16[1040,128]{1,0:T(8,128)(2,1)S(1)}, bf16[1040,128]{1,0:T(8,128)(2,1)S(1)}, u32[]{:S(2)}, u32[]{:S(2)}) %collective-permute-start.17) | collective-permute-done | bytes 266272 | tf_op jit(solution)/shard_map/ppermute | solution.py:381
  93.9 0.0 copy-done.4
  93.9 1.1 %shard_map.98 = f32[1024,128]{1,0:T(8,128)} custom-call(s32[8,128]{1,0:T(8,128)S(1)} %bitcast.9, bf16[1040,128]{1,0:T(8,128)(2,1)S(1)} %get-tuple-element.34.refs_0_, bf16[1040,128]{1,0:T(8,128)(2,1)S(1)} %collective-permute-done.17.refs_1_, bf16[1040,128]{1,0:T(8,128)(2,1)S(1)} %collective-permute-done.18.refs_2_, ...), custom_call_target="tpu_custom_call" | custom-call | tf_op jit(solution)/shard_map/pallas_call | solution.py:370
  (3 shorter events, 0.0 us)
Async XLA Ops:
  0.6 1.0 %copy-start.2 = (f32[1024,128]{1,0:T(8,128)S(1)}, f32[1024,128]{1,0:T(8,128)}, u32[]{:S(2)}) copy-start(f32[1024,128]{1,0:T(8,128)} %video_ref.1) | copy-start | bytes 1572868
  1.7 23.1 %collective-permute-start.2 = (bf16[1024,128]{1,0:T(8,128)(2,1)S(1)}, bf16[1024,128]{1,0:T(8,128)(2,1)S(1)}, u32[]{:S(2)}, u32[]{:S(2)}) collective-permute-start(bf16[1024,128]{1,0:T(8,128)(2,1)S(1)} %shard_map.87.refs_0_), channel_id=1, source_target_pairs={{0,24},{8,16},{16,8},{24,0},{1,25},{9,17},{17,9},{25,1},{2,26},{10... | collective-permute-start | bytes 786440 | tf_op jit(solution)/shard_map/ppermute | solution.py:381
  6.8 22.3 %collective-permute-start.1 = (bf16[1024,128]{1,0:T(8,128)(2,1)S(1)}, bf16[1024,128]{1,0:T(8,128)(2,1)S(1)}, u32[]{:S(2)}, u32[]{:S(2)}) collective-permute-start(bf16[1024,128]{1,0:T(8,128)(2,1)S(1)} %shard_map.87.refs_0_), channel_id=1, source_target_pairs={{0,16},{8,24},{16,0},{24,8},{1,17},{9,25},{17,1},{25,9},{2,18},{10... | collective-permute-start | bytes 786440 | tf_op jit(solution)/shard_map/ppermute | solution.py:381
  6.8 22.3 %collective-permute-start = (bf16[1024,128]{1,0:T(8,128)(2,1)S(1)}, bf16[1024,128]{1,0:T(8,128)(2,1)S(1)}, u32[]{:S(2)}, u32[]{:S(2)}) collective-permute-start(bf16[1024,128]{1,0:T(8,128)(2,1)S(1)} %shard_map.87.refs_0_), channel_id=1, source_target_pairs={{0,8},{8,0},{16,24},{24,16},{1,9},{9,1},{17,25},{25,17},{2,10},{10... | collective-permute-start | bytes 786440 | tf_op jit(solution)/shard_map/ppermute | solution.py:381
  8.1 4.0 %copy-start = (bf16[1,1,320,128,128]{4,3,2,1,0:T(8,128)(2,1)S(1)}, bf16[1,1,320,128,128]{4,3,2,1,0:T(8,128)(2,1)}, u32[]{:S(2)}) copy-start(bf16[1,1,320,128,128]{4,3,2,1,0:T(8,128)(2,1)} %param.10) | copy-start | bytes 31457284
  12.1 0.7 copy-start.5
  12.8 0.7 copy-start.6
  13.5 4.0 %copy-start.1 = (bf16[1,1,320,128,128]{4,3,2,1,0:T(8,128)(2,1)S(1)}, bf16[1,1,320,128,128]{4,3,2,1,0:T(8,128)(2,1)}, u32[]{:S(2)}) copy-start(bf16[1,1,320,128,128]{4,3,2,1,0:T(8,128)(2,1)} %param.10) | copy-start | bytes 31457284
  24.8 25.9 %copy-start.3 = (s32[1024]{0:T(1024)S(1)}, s32[1024]{0:T(1024)}, u32[]{:S(2)}) copy-start(s32[1024]{0:T(1024)} %param.8) | copy-start | bytes 12292
  32.9 1.9 %collective-permute-start.4 = (bf16[1040,128]{1,0:T(8,128)(2,1)S(1)}, bf16[1040,128]{1,0:T(8,128)(2,1)S(1)}, u32[]{:S(2)}, u32[]{:S(2)}) collective-permute-start(bf16[1040,128]{1,0:T(8,128)(2,1)S(1)} %get-tuple-element.27), channel_id=1, source_target_pairs={{0,1},{1,0},{2,3},{3,2},{4,5},{5,4},{6,7},{7,6},{8,9},{9,8},{10,11... | collective-permute-start | bytes 798728 | tf_op jit(solution)/shard_map/ppermute | solution.py:381
  33.6 1.6 %collective-permute-start.6 = (bf16[1040,128]{1,0:T(8,128)(2,1)S(1)}, bf16[1040,128]{1,0:T(8,128)(2,1)S(1)}, u32[]{:S(2)}, u32[]{:S(2)}) collective-permute-start(bf16[1040,128]{1,0:T(8,128)(2,1)S(1)} %get-tuple-element.29), channel_id=1, source_target_pairs={{0,1},{1,0},{2,3},{3,2},{4,5},{5,4},{6,7},{7,6},{8,9},{9,8},{10,11... | collective-permute-start | bytes 798728 | tf_op jit(solution)/shard_map/ppermute | solution.py:381
  33.7 4.6 %collective-permute-start.8 = (bf16[1040,128]{1,0:T(8,128)(2,1)S(1)}, bf16[1040,128]{1,0:T(8,128)(2,1)S(1)}, u32[]{:S(2)}, u32[]{:S(2)}) collective-permute-start(bf16[1040,128]{1,0:T(8,128)(2,1)S(1)} %get-tuple-element.31), channel_id=1, source_target_pairs={{0,1},{1,0},{2,3},{3,2},{4,5},{5,4},{6,7},{7,6},{8,9},{9,8},{10,11... | collective-permute-start | bytes 798728 | tf_op jit(solution)/shard_map/ppermute | solution.py:381
  34.1 4.8 %collective-permute-start.3 = (bf16[1040,128]{1,0:T(8,128)(2,1)S(1)}, bf16[1040,128]{1,0:T(8,128)(2,1)S(1)}, u32[]{:S(2)}, u32[]{:S(2)}) collective-permute-start(bf16[1040,128]{1,0:T(8,128)(2,1)S(1)} %get-tuple-element.25), channel_id=1, source_target_pairs={{0,1},{1,0},{2,3},{3,2},{4,5},{5,4},{6,7},{7,6},{8,9},{9,8},{10,11... | collective-permute-start | bytes 798728 | tf_op jit(solution)/shard_map/ppermute | solution.py:381
  34.8 9.3 %collective-permute-start.5 = (bf16[1040,128]{1,0:T(8,128)(2,1)S(1)}, bf16[1040,128]{1,0:T(8,128)(2,1)S(1)}, u32[]{:S(2)}, u32[]{:S(2)}) collective-permute-start(bf16[1040,128]{1,0:T(8,128)(2,1)S(1)} %shard_map.91), channel_id=1, source_target_pairs={{0,2},{1,3},{2,0},{3,1},{4,6},{5,7},{6,4},{7,5},{8,10},{9,11},{10,... | collective-permute-start | bytes 798728 | tf_op jit(solution)/shard_map/ppermute | solution.py:381
  35.2 14.4 %collective-permute-start.7 = (bf16[1040,128]{1,0:T(8,128)(2,1)S(1)}, bf16[1040,128]{1,0:T(8,128)(2,1)S(1)}, u32[]{:S(2)}, u32[]{:S(2)}) collective-permute-start(bf16[1040,128]{1,0:T(8,128)(2,1)S(1)} %shard_map.92), channel_id=1, source_target_pairs={{0,4},{1,5},{2,6},{3,7},{4,0},{5,1},{6,2},{7,3},{8,12},{9,13},{10,... | collective-permute-start | bytes 798728 | tf_op jit(solution)/shard_map/ppermute | solution.py:381
  38.4 12.4 %collective-permute-start.9 = (bf16[1040,128]{1,0:T(8,128)(2,1)S(1)}, bf16[1040,128]{1,0:T(8,128)(2,1)S(1)}, u32[]{:S(2)}, u32[]{:S(2)}) collective-permute-start(bf16[1040,128]{1,0:T(8,128)(2,1)S(1)} %shard_map.93), channel_id=1, source_target_pairs={{0,6},{1,7},{2,4},{3,5},{4,2},{5,3},{6,0},{7,1},{8,14},{9,15},{10,... | collective-permute-start | bytes 798728 | tf_op jit(solution)/shard_map/ppermute | solution.py:381
  51.0 42.9 %copy-start.4 = (s32[1024]{0:T(1024)S(1)}, s32[1024]{0:T(1024)}, u32[]{:S(2)}) copy-start(s32[1024]{0:T(1024)} %param.9) | copy-start | bytes 12292
  51.0 9.3 %collective-permute-start.14 = (bf16[1024,128]{1,0:T(8,128)(2,1)S(1)}, bf16[1024,128]{1,0:T(8,128)(2,1)S(1)}, u32[]{:S(2)}, u32[]{:S(2)}) collective-permute-start(bf16[1024,128]{1,0:T(8,128)(2,1)S(1)} %get-tuple-element.33.refs_7_), channel_id=1, source_target_pairs={{0,2},{1,3},{2,0},{3,1},{4,6},{5,7},{6,4},{7,5},{8,10},{9,11},{10,... | collective-permute-start | bytes 786440 | tf_op jit(solution)/shard_map/ppermute | solution.py:381
  52.1 12.9 %collective-permute-start.12 = (bf16[1024,128]{1,0:T(8,128)(2,1)S(1)}, bf16[1024,128]{1,0:T(8,128)(2,1)S(1)}, u32[]{:S(2)}, u32[]{:S(2)}) collective-permute-start(bf16[1024,128]{1,0:T(8,128)(2,1)S(1)} %get-tuple-element.33.refs_7_), channel_id=1, source_target_pairs={{0,4},{1,5},{2,6},{3,7},{4,0},{5,1},{6,2},{7,3},{8,12},{9,13},{10,... | collective-permute-start | bytes 786440 | tf_op jit(solution)/shard_map/ppermute | solution.py:381
  53.5 11.4 %collective-permute-start.10 = (bf16[1024,128]{1,0:T(8,128)(2,1)S(1)}, bf16[1024,128]{1,0:T(8,128)(2,1)S(1)}, u32[]{:S(2)}, u32[]{:S(2)}) collective-permute-start(bf16[1024,128]{1,0:T(8,128)(2,1)S(1)} %get-tuple-element.33.refs_7_), channel_id=1, source_target_pairs={{0,6},{1,7},{2,4},{3,5},{4,2},{5,3},{6,0},{7,1},{8,14},{9,15},{10,... | collective-permute-start | bytes 786440 | tf_op jit(solution)/shard_map/ppermute | solution.py:381
  54.5 10.9 %collective-permute-start.16 = (bf16[1024,128]{1,0:T(8,128)(2,1)S(1)}, bf16[1024,128]{1,0:T(8,128)(2,1)S(1)}, u32[]{:S(2)}, u32[]{:S(2)}) collective-permute-start(bf16[1024,128]{1,0:T(8,128)(2,1)S(1)} %get-tuple-element.33.refs_7_), channel_id=1, source_target_pairs={{0,1},{1,0},{2,3},{3,2},{4,5},{5,4},{6,7},{7,6},{8,9},{9,8},{10,11... | collective-permute-start | bytes 786440 | tf_op jit(solution)/shard_map/ppermute | solution.py:381
  60.3 5.1 %collective-permute-start.15 = (bf16[1024,128]{1,0:T(8,128)(2,1)S(1)}, bf16[1024,128]{1,0:T(8,128)(2,1)S(1)}, u32[]{:S(2)}, u32[]{:S(2)}) collective-permute-start(bf16[1024,128]{1,0:T(8,128)(2,1)S(1)} %collective-permute-done.14.refs_5_), channel_id=1, source_target_pairs={{0,1},{1,0},{2,3},{3,2},{4,5},{5,4},{6,7},{7,6},{8,9},{9,8},{10,11... | collective-permute-start | bytes 786440 | tf_op jit(solution)/shard_map/ppermute | solution.py:381
  64.9 1.5 %collective-permute-start.13 = (bf16[1024,128]{1,0:T(8,128)(2,1)S(1)}, bf16[1024,128]{1,0:T(8,128)(2,1)S(1)}, u32[]{:S(2)}, u32[]{:S(2)}) collective-permute-start(bf16[1024,128]{1,0:T(8,128)(2,1)S(1)} %collective-permute-done.12.refs_3_), channel_id=1, source_target_pairs={{0,1},{1,0},{2,3},{3,2},{4,5},{5,4},{6,7},{7,6},{8,9},{9,8},{10,11... | collective-permute-start | bytes 786440 | tf_op jit(solution)/shard_map/ppermute | solution.py:381
  64.9 1.9 %collective-permute-start.11 = (bf16[1024,128]{1,0:T(8,128)(2,1)S(1)}, bf16[1024,128]{1,0:T(8,128)(2,1)S(1)}, u32[]{:S(2)}, u32[]{:S(2)}) collective-permute-start(bf16[1024,128]{1,0:T(8,128)(2,1)S(1)} %collective-permute-done.10.refs_1_), channel_id=1, source_target_pairs={{0,1},{1,0},{2,3},{3,2},{4,5},{5,4},{6,7},{7,6},{8,9},{9,8},{10,11... | collective-permute-start | bytes 786440 | tf_op jit(solution)/shard_map/ppermute | solution.py:381
  69.2 19.4 %collective-permute-start.18 = (bf16[1040,128]{1,0:T(8,128)(2,1)S(1)}, bf16[1040,128]{1,0:T(8,128)(2,1)S(1)}, u32[]{:S(2)}, u32[]{:S(2)}) collective-permute-start(bf16[1040,128]{1,0:T(8,128)(2,1)S(1)} %get-tuple-element.36), channel_id=1, source_target_pairs={{0,16},{8,24},{16,0},{24,8},{1,17},{9,25},{17,1},{25,9},{2,18},{10... | collective-permute-start | bytes 798728 | tf_op jit(solution)/shard_map/ppermute | solution.py:381
  69.3 19.3 %collective-permute-start.19 = (bf16[1040,128]{1,0:T(8,128)(2,1)S(1)}, bf16[1040,128]{1,0:T(8,128)(2,1)S(1)}, u32[]{:S(2)}, u32[]{:S(2)}) collective-permute-start(bf16[1040,128]{1,0:T(8,128)(2,1)S(1)} %get-tuple-element.37), channel_id=1, source_target_pairs={{0,24},{8,16},{16,8},{24,0},{1,25},{9,17},{17,9},{25,1},{2,26},{10... | collective-permute-start | bytes 798728 | tf_op jit(solution)/shard_map/ppermute | solution.py:381
  73.4 20.5 %collective-permute-start.17 = (bf16[1040,128]{1,0:T(8,128)(2,1)S(1)}, bf16[1040,128]{1,0:T(8,128)(2,1)S(1)}, u32[]{:S(2)}, u32[]{:S(2)}) collective-permute-start(bf16[1040,128]{1,0:T(8,128)(2,1)S(1)} %get-tuple-element.35), channel_id=1, source_target_pairs={{0,8},{8,0},{16,24},{24,16},{1,9},{9,1},{17,25},{25,17},{2,10},{10... | collective-permute-start | bytes 798728 | tf_op jit(solution)/shard_map/ppermute | solution.py:381

commit v5 on v4

--- a/solution.py
+++ b/solution.py
@@ -10,7 +10,6 @@
 BLEND = 0.75
 GROUP = 32
 PLACE = 8
-NT = (((1,), (1,)), ((), ()))
 VMEM = pl.BlockSpec(memory_space=pltpu.VMEM)
 
 
@@ -43,30 +42,25 @@
 def plan_kernel(rows, cols, live_ref, _, codes_ref, counts, *, cap, half, shard):
     row_mask, col_mask = lax.axis_index("row") * shard, lax.axis_index("col") * shard
     live = live_ref[0, 0]
-    trash = 3 * cap
+    for n in range(4):
+        counts[n] = 0
 
     def place(block, carry):
-        own, near, far = carry
         base = block * PLACE
         found = [(rows[0, 0, base + k], cols[0, 0, base + k]) for k in range(PLACE)]
         for k, (row, col) in enumerate(found):
             slot = base + k
             row, col = row ^ col_mask, col ^ row_mask
-            is_far = col >= half
-            is_own = col < shard
-            spot = jnp.where(is_far, 2 * cap + far, jnp.where(is_own, own, cap + near))
-            codes_ref[jnp.where(slot < live, spot, trash)] = slot | (col << 12) | (row << 20)
-            one = (slot < live).astype(jnp.int32)
-            near += jnp.where(is_far | is_own, 0, one)
-            own += jnp.where(is_own, one, 0)
-            far += jnp.where(is_far, one, 0)
-        return own, near, far
-
-    zero = jnp.int32(0)
-    found = lax.fori_loop(0, lax.div(live + (PLACE - 1), PLACE), place, (zero, zero, zero))
+            region = (col >= shard).astype(jnp.int32) + (col >= half).astype(jnp.int32)
+            region = jnp.where(slot < live, region, 3)
+            count = counts[region]
+            codes_ref[region * cap + count] = slot | (col << 12) | (row << 20)
+            counts[region] = count + 1
+        return carry
+
+    lax.fori_loop(0, lax.div(live + (PLACE - 1), PLACE), place, 0)
+    found = [counts[n] for n in range(3)]
     row_dummy = (lax.axis_size("col") * shard) << 20
-    for n, count in enumerate(found):
-        counts[n] = count
     for n, count in enumerate(found):
         dummy = row_dummy | ((half if n < 2 else 2 * half) << 12)
 
@@ -84,7 +78,7 @@
         functools.partial(plan_kernel, cap=cap, half=col_tiles // 2, shard=shard),
         out_shape=[
             jax.ShapeDtypeStruct((3 * cap + 128,), jnp.int32),
-            jax.ShapeDtypeStruct((3,), jnp.int32),
+            jax.ShapeDtypeStruct((4,), jnp.int32),
         ],
         in_specs=[smem] * 3 + [VMEM],
         out_specs=[smem] * 2,
@@ -126,29 +120,52 @@
     return jnp.sum(tile.reshape(16, 8, 128), axis=0)
 
 
-def early_kernel(codes, counts, tiles_ref, *refs):
-    *piece_refs, sums_ref, weights_ref, panel, acc, mass = refs
-    fill_panel(panel, piece_refs)
-    clear(acc, mass)
-    ones = jnp.ones((16, 128), jnp.bfloat16)
+def early_kernel(codes, counts, tiles_ref, own_ref, sums_ref, weights_ref, panel, mass):
+    fill_panel(panel, [own_ref])
+    clear(mass)
+    ones = jnp.ones((128, 128), jnp.bfloat16)
+
+    def begin(n, carry):
+        sums_ref[n] = jnp.zeros((128, 128), jnp.float32)
+        return carry
 
     def multiply(slot, col, row):
         part = panel[col & (panel.shape[0] - 1)]
-        acc[row] += jnp.dot(tiles_ref[slot], part, preferred_element_type=jnp.float32)
+        sums_ref[row] += jnp.dot(tiles_ref[slot], part, preferred_element_type=jnp.float32)
 
     def weigh(slot, col, row):
-        sums = lax.dot_general(ones, tiles_ref[slot], NT, preferred_element_type=jnp.float32)
-        mass[row] += sums[:8]
-
+        mass[row] += jnp.dot(tiles_ref[slot], ones, preferred_element_type=jnp.float32)
+
+    lax.fori_loop(0, sums_ref.shape[0], begin, 0)
     walk(codes, counts, [0], multiply)
     walk(codes, counts, [0, 1, 2], weigh)
 
+    diagonal = lax.broadcasted_iota(jnp.int32, (128, 128), 0) == lax.broadcasted_iota(
+        jnp.int32, (128, 128), 1
+    )
+
     def hand(n, carry):
-        sums_ref[n] = acc[n]
-        weights_ref[n] = mass[n]
-        return carry
-
-    lax.fori_loop(0, acc.shape[0] - 1, hand, 0)
+        weights_ref[n] = fold_rows(jnp.where(diagonal, mass[n], 0.0))
+        return carry
+
+    lax.fori_loop(0, weights_ref.shape[0], hand, 0)
+
+
+def middle_kernel(codes, counts, tiles_ref, sums_ref, *refs, shard):
+    *piece_refs, out_ref, panel = refs
+    fill_panel(panel.at[pl.ds(shard, panel.shape[0] - shard)], piece_refs)
+    panel[0] = jnp.zeros((128, 128), jnp.bfloat16)
+
+    def begin(n, carry):
+        out_ref[n] = sums_ref[n]
+        return carry
+
+    def multiply(slot, col, row):
+        part = panel[col & (panel.shape[0] - 1)]
+        out_ref[row] += jnp.dot(tiles_ref[slot], part, preferred_element_type=jnp.float32)
+
+    lax.fori_loop(0, sums_ref.shape[0], begin, 0)
+    walk(codes, counts, [1], multiply)
 
 
 def grant(scratch, arrays):
@@ -163,55 +180,66 @@
     )
 
 
-def early_sweep(codes, counts, tiles, pieces, row_tiles):
+def early_sweep(codes, counts, tiles, own, row_tiles):
     smem, slots = pl.BlockSpec(memory_space=pltpu.SMEM), tiles.shape[0]
     out_shape = [
-        jax.ShapeDtypeStruct((row_tiles, 128, 128), jnp.float32),
+        jax.ShapeDtypeStruct((row_tiles + 1, 128, 128), jnp.float32),
         jax.ShapeDtypeStruct((row_tiles, 8, 128), jnp.float32),
     ]
-    scratch = 4 * (row_tiles + 1) * 136 * 128 + sum(p.size for p in pieces) * 2
     return pl.pallas_call(
         early_kernel,
-        in_specs=[smem] * 2 + [VMEM] * (1 + len(pieces)),
+        in_specs=[smem] * 2 + [VMEM] * 2,
         out_specs=[VMEM] * 2,
         scratch_shapes=[
-            pltpu.VMEM((sum(p.shape[0] for p in pieces) // 128, 128, 128), jnp.bfloat16),
+            pltpu.VMEM((own.shape[0] // 128, 128, 128), jnp.bfloat16),
             pltpu.VMEM((row_tiles + 1, 128, 128), jnp.float32),
-            pltpu.VMEM((row_tiles + 1, 8, 128), jnp.float32),
         ],
         out_shape=out_shape,
-        compiler_params=grant(scratch, [tiles, *pieces, *out_shape]),
+        compiler_params=grant(4 * (row_tiles + 5) * 128**2, [tiles, own, *out_shape]),
         cost_estimate=effort(slots),
-    )(codes, counts, tiles, *pieces)
+    )(codes, counts, tiles, own)
+
+
+def middle_sweep(codes, counts, tiles, sums, pieces, shard):
+    smem, slots = pl.BlockSpec(memory_space=pltpu.SMEM), tiles.shape[0]
+    panel = shard + sum(p.shape[0] for p in pieces) // 128
+    return pl.pallas_call(
+        functools.partial(middle_kernel, shard=shard),
+        in_specs=[smem] * 2 + [VMEM] * (2 + len(pieces)),
+        out_specs=VMEM,
+        scratch_shapes=[pltpu.VMEM((panel, 128, 128), jnp.bfloat16)],
+        out_shape=jax.ShapeDtypeStruct(sums.shape, jnp.float32),
+        compiler_params=grant(2 * panel * 128**2, [tiles, sums, sums, *pieces]),
+        cost_estimate=effort(slots),
+    )(codes, counts, tiles, sums, *pieces)
 
 
 def late_kernel(codes, counts, tiles_ref, sums_ref, weights_ref, *refs, shard):
-    count_out = sums_ref.shape[0] // shard
+    count_out = weights_ref.shape[0] // shard
     piece_refs, out_refs, (panel, acc) = refs[: -2 - count_out], refs[-2 - count_out : -2], refs[-2:]
-    fill_panel(panel.at[pl.ds(shard, panel.shape[0] - shard)], piece_refs)
-    panel[0] = jnp.zeros((128, 128), jnp.bfloat16)
+    fill_panel(panel, piece_refs)
 
     def begin(n, carry):
         acc[n] = sums_ref[n]
         return carry
 
-    lax.fori_loop(0, sums_ref.shape[0], begin, 0)
+    lax.fori_loop(0, weights_ref.shape[0], begin, 0)
 
     def multiply(slot, col, row):
         part = panel[col & (panel.shape[0] - 1)]
         acc[row] += jnp.dot(tiles_ref[slot], part, preferred_element_type=jnp.float32)
 
-    walk(codes, counts, [1, 2], multiply)
+    walk(codes, counts, [2], multiply)
     for n, target in enumerate(out_refs):
         tops = []
         for t in range(shard):
             target[t * 128 : (t + 1) * 128, :] = acc[n * shard + t].astype(jnp.bfloat16)
-            tops.append(weights_ref[n * shard + t, 0:1, :])
+            tops.append(jnp.sum(weights_ref[n * shard + t], axis=0, keepdims=True))
         target[shard * 128 :, :] = split_half(jnp.concatenate(tops, axis=0))
 
 
 def late_sweep(codes, counts, tiles, sums, weights, pieces, shard):
-    smem, slots, row_tiles = pl.BlockSpec(memory_space=pltpu.SMEM), tiles.shape[0], sums.shape[0]
+    smem, slots, row_tiles = pl.BlockSpec(memory_space=pltpu.SMEM), tiles.shape[0], weights.shape[0]
     rows = shard * 130
     out_shape = [jax.ShapeDtypeStruct((rows, 128), jnp.bfloat16)] * (row_tiles // shard)
     scratch = 4 * (row_tiles + 1) * 128**2 + sum(p.size for p in pieces) * 2
@@ -220,7 +248,7 @@
         in_specs=[smem] * 2 + [VMEM] * (3 + len(pieces)),
         out_specs=[VMEM] * len(out_shape),
         scratch_shapes=[
-            pltpu.VMEM((shard + sum(p.shape[0] for p in pieces) // 128, 128, 128), jnp.bfloat16),
+            pltpu.VMEM((sum(p.shape[0] for p in pieces) // 128, 128, 128), jnp.bfloat16),
             pltpu.VMEM((row_tiles + 1, 128, 128), jnp.float32),
         ],
         out_shape=out_shape,
@@ -230,7 +258,7 @@
 
 
 def reverse_kernel(codes, counts, tiles_ref, *refs, pieces, lists, first, shard):
-    piece_refs, out_refs, (panel, acc, mass) = refs[:pieces][::-1], refs[pieces:-3], refs[-3:]
+    piece_refs, out_refs, (panel, acc, mass) = refs[:pieces], refs[pieces:-3], refs[-3:]
     fill_panel(panel, piece_refs)
     clear(acc, mass)
 
@@ -392,20 +420,21 @@
     own = prep(video_scores_in)
     others = [partner(own, "row", m) for m in range(1, n_row)]
     codes, counts = plan(tile_rows, tile_cols, tile_count, tiles, col_tiles, shard)
-    sums, weights = early_sweep(codes, counts, tiles, [own], row_tiles)
-    payloads = late_sweep(codes, counts, tiles, sums, weights, others, shard)
+    sums, weights = early_sweep(codes, counts, tiles, own, row_tiles)
+    near, far = others[: n_row // 2 - 1], others[n_row // 2 - 1 :]
+    sums = middle_sweep(codes, counts, tiles, sums, near, shard)
+    payloads = late_sweep(codes, counts, tiles, sums, weights, far, shard)
     owned = {}
     for n in [*range(2, n_col, 2), 0]:
         kind = jnp.bfloat16 if n else jnp.float32
         got = partner(payloads[n + 1], "col", 1)
         owned[n] = pair_sum(payloads[n], got, shard * 128, kind)
-    arrived = [partner(owned[n], "col", n) for n in range(2, n_col, 2)]
+    arrived = [partner(owned[n], "col", n) for n in range(n_col - 2, 0, -2)]
     half, turned = audio_blend(audio_seeds, owned[0], arrived)
 
     mine = [half] + [partner(half, "col", m) for m in range(2, n_col, 2)]
     pieces = [q for p in mine for q in (p, partner(p, "col", 1))]
     half_tiles = col_tiles // 2
-    pieces = pieces[::-1]
     far = reverse_sweep(codes, counts, [2], half_tiles, tiles, pieces, half_tiles, shard)
     near = reverse_sweep(codes, counts, [0, 1], 0, tiles, pieces, half_tiles, shard)
     sums = list(near) + list(far)

time: 95.1 us -> 94.5 us (level); the launches traced: 94.9 us -> 93.1 us
  waiting for transfers between devices: 45.5 us -> 41.6 us
  starting transfers between devices: 18.6 us -> 21.9 us
  Pallas kernels: 22.3 us -> 20.9 us
    ppermute x20, waiting for transfers between devices: 45.5 us -> 41.6 us  [partner(): return lax.ppermute(value, axis, [(i, i ^ mask) for i in range(size)])]
    ppermute x20, starting transfers between devices: 18.6 us -> 21.9 us  [partner(): return lax.ppermute(value, axis, [(i, i ^ mask) for i in range(size)])]
    pallas_call x1, Pallas kernels: 3.78 us -> 2.77 us  [late_sweep(): pl.pallas_call(functools.partial(late_kernel, shard=shard), in_specs=[sme...]
    pallas_call x1 -> x2, Pallas kernels: 7.37 us -> 7.73 us  [the longest x1 6.19 us: early_sweep(): pl.pallas_call(early_kernel, in_specs=[smem] * 2 + [VMEM] * 2, out_specs=...]
  transfers between devices with their start and end apart: 20 -> 20, of which waited for: 11 -> 10; matrix products, arithmetic and copies ran while one was open for 0% -> 0% of each run, Pallas kernels for 16% -> 15%
where the time goes in v5:
time: 94.5 us; the launch traced here: 93.1 us
  waiting for transfers between devices  41.6 us (44%)
  starting transfers between devices  21.9 us (23%)
  Pallas kernels  20.9 us (22%)
  local copies, waits for them, and re-layouts  7.34 us (8%)
  between operations  1.39 us (1%)
    ppermute x20, waiting for transfers between devices, partner(): return lax.ppermute(value, axis, [(i, i ^ mask) for i in range(size)])  41.6 us
    ppermute x20, starting transfers between devices, partner(): return lax.ppermute(value, axis, [(i, i ^ mask) for i in range(size)])  21.9 us
    unnamed x14, local copies, waits for them, and re-layouts  7.34 us
    pallas_call x1, Pallas kernels, early_sweep(): pl.pallas_call(early_kernel, in_specs=[smem] * 2 + [VMEM] * 2, out_specs=...  6.19 us
    pallas_call x2, Pallas kernels, reverse_sweep(): pl.pallas_call(functools.partial(reverse_kernel, pieces=len(pieces), list...  4.79 us
    pallas_call x1, Pallas kernels, plan(): pl.pallas_call(functools.partial(plan_kernel, cap=cap, half=col_tiles //...  3.01 us
    pallas_call x1, Pallas kernels, late_sweep(): pl.pallas_call(functools.partial(late_kernel, shard=shard), in_specs=[sme...  2.77 us
  transfers between devices with their start and end apart: 20, of which 10 were waited for; matrix products, arithmetic and copies ran while one was open for 0% of the time, Pallas kernels for 15%

profile of v5, /device:TPU:0, one launch (start us, length us, event | category | flops | bytes accessed | tf_op | source)
XLA Modules:
  0.0 93.1 jit_solution(11292295550307195053)
XLA Ops:
  0.6 0.0 copy-start.2
  0.6 1.0 %copy-done.2 = f32[1024,128]{1,0:T(8,128)S(1)} copy-done((f32[1024,128]{1,0:T(8,128)S(1)}, f32[1024,128]{1,0:T(8,128)}, u32[]{:S(2)}) %copy-start.2) | copy-done | bytes 524312
  1.7 3.1 %collective-permute-start = (bf16[1024,128]{1,0:T(8,128)(2,1)S(1)}, bf16[1024,128]{1,0:T(8,128)(2,1)S(1)}, u32[]{:S(2)}, u32[]{:S(2)}) collective-permute-start(bf16[1024,128]{1,0:T(8,128)(2,1)S(1)} %shard_map.87.own_ref), channel_id=1, source_target_pairs={{0,8},{8,0},{16,24},{24,16},{1,9},{9,1},{17,25},{25,17},{2,10},{10... | collective-permute-start | bytes 786440 | tf_op jit(solution)/shard_map/ppermute | solution.py:409
  4.8 2.6 %collective-permute-start.1 = (bf16[1024,128]{1,0:T(8,128)(2,1)S(1)}, bf16[1024,128]{1,0:T(8,128)(2,1)S(1)}, u32[]{:S(2)}, u32[]{:S(2)}) collective-permute-start(bf16[1024,128]{1,0:T(8,128)(2,1)S(1)} %shard_map.87.own_ref), channel_id=1, source_target_pairs={{0,16},{8,24},{16,0},{24,8},{1,17},{9,25},{17,1},{25,9},{2,18},{10... | collective-permute-start | bytes 786440 | tf_op jit(solution)/shard_map/ppermute | solution.py:409
  7.4 0.0 collective-permute-start.2
  8.0 0.0 copy-start
  8.0 4.0 %copy-done = bf16[1,1,320,128,128]{4,3,2,1,0:T(8,128)(2,1)S(1)} copy-done((bf16[1,1,320,128,128]{4,3,2,1,0:T(8,128)(2,1)S(1)}, bf16[1,1,320,128,128]{4,3,2,1,0:T(8,128)(2,1)}, u32[]{:S(2)}) %copy-start) | copy-done | bytes 10485784
  12.0 0.0 copy-start.5
  12.0 0.7 copy-done.5
  12.7 0.0 copy-start.6
  12.7 0.7 copy-done.6
  13.4 3.0 %shard_map.86 = (s32[1184]{0:T(1024)S(1)}, s32[4]{0:T(128)S(1)}) custom-call(s32[1,1,320]{2,1,0:T(1,128)S(1)} %copy-done.5, s32[1,1,320]{2,1,0:T(1,128)S(1)} %copy-done.6, s32[1,1]{1,0:T(1,128)S(6)} %copy.9.live_ref, bf16[320,128,128]{2,1,0:T(8,128)(2,1)S(1)} %bitcast.3), custom_call_target="tpu_custom_call" | custom-call | tf_op jit(solution)/shard_map/pallas_call | solution.py:77
  16.4 1.0 %copy-done.1 = bf16[1,1,320,128,128]{4,3,2,1,0:T(8,128)(2,1)S(1)} copy-done((bf16[1,1,320,128,128]{4,3,2,1,0:T(8,128)(2,1)S(1)}, bf16[1,1,320,128,128]{4,3,2,1,0:T(8,128)(2,1)}, u32[]{:S(2)}) %copy-start.1) | copy-done | bytes 10485784
  17.4 6.2 %shard_map.88 = (f32[65,128,128]{2,1,0:T(8,128)S(1)}, f32[64,8,128]{2,1,0:T(8,128)S(1)}) custom-call(s32[1184]{0:T(1024)S(1)} %get-tuple-element.20.codes, s32[4]{0:T(128)S(1)} %get-tuple-element.21.counts, bf16[320,128,128]{2,1,0:T(8,128)(2,1)S(1)} %bitcast.4, bf16[1024,128]{1,0:T(8,128)(2,1)S(1)} %shard_map.87.own_ref), custom_call_target="tpu_custom_call" | custom-call | flops 2684354560 | bytes 2621440 | tf_op jit(solution)/shard_map/pallas_call | solution.py:189
  23.5 0.0 collective-permute-done.refs_0_
  23.6 1.5 %shard_map.89.sums_ref = f32[65,128,128]{2,1,0:T(8,128)S(1)} custom-call(s32[1184]{0:T(1024)S(1)} %get-tuple-element.20.codes, s32[4]{0:T(128)S(1)} %get-tuple-element.21.counts, bf16[320,128,128]{2,1,0:T(8,128)(2,1)S(1)} %bitcast.5, f32[65,128,128]{2,1,0:T(8,128)S(1)} %get-tuple-element.22.sums_ref, bf16[1024,128]{1,0:T(8,128)(2,1)S(1)} %collective-permute-done.refs_0_), custom_call_target="tpu_custom_call" | custom-call | flops 2684354560 | bytes 2621440 | tf_op jit(solution)/shard_map/pallas_call | solution.py:206
  25.1 1.1 %collective-permute-done.1.refs_0_ = bf16[1024,128]{1,0:T(8,128)(2,1)S(1)} collective-permute-done((bf16[1024,128]{1,0:T(8,128)(2,1)S(1)}, bf16[1024,128]{1,0:T(8,128)(2,1)S(1)}, u32[]{:S(2)}, u32[]{:S(2)}) %collective-permute-start.1) | collective-permute-done | bytes 262176 | tf_op jit(solution)/shard_map/ppermute | solution.py:409
  26.2 0.0 collective-permute-done.2.refs_1_
  26.2 2.8 %shard_map.90 = (bf16[1040,128]{1,0:T(8,128)(2,1)S(1)}, bf16[1040,128]{1,0:T(8,128)(2,1)S(1)}, bf16[1040,128]{1,0:T(8,128)(2,1)S(1)}, bf16[1040,128]{1,0:T(8,128...) custom-call(s32[1184]{0:T(1024)S(1)} %get-tuple-element.20.codes, ...), custom_call_target="tpu_custom_call" | custom-call | flops 2684354560 | bytes 2621440 | tf_op jit(solution)/shard_map/pallas_call | solution.py:246
  28.9 0.1 collective-permute-start.8
  29.0 0.5 collective-permute-start.6
  29.5 0.1 collective-permute-start.4
  29.6 0.4 collective-permute-start.3
  30.0 0.5 collective-permute-done.8.got_ref
  30.6 0.1 shard_map.94
  30.6 1.1 %collective-permute-start.9 = (bf16[1040,128]{1,0:T(8,128)(2,1)S(1)}, bf16[1040,128]{1,0:T(8,128)(2,1)S(1)}, u32[]{:S(2)}, u32[]{:S(2)}) collective-permute-start(bf16[1040,128]{1,0:T(8,128)(2,1)S(1)} %shard_map.94), channel_id=1, source_target_pairs={{0,2},{1,3},{2,0},{3,1},{4,6},{5,7},{6,4},{7,5},{8,10},{9,11},{10,... | collective-permute-start | bytes 798728 | tf_op jit(solution)/shard_map/ppermute | solution.py:409
  31.7 0.0 collective-permute-done.6.got_ref
  31.7 0.1 shard_map.93
  31.8 2.2 %collective-permute-start.7 = (bf16[1040,128]{1,0:T(8,128)(2,1)S(1)}, bf16[1040,128]{1,0:T(8,128)(2,1)S(1)}, u32[]{:S(2)}, u32[]{:S(2)}) collective-permute-start(bf16[1040,128]{1,0:T(8,128)(2,1)S(1)} %shard_map.93), channel_id=1, source_target_pairs={{0,4},{1,5},{2,6},{3,7},{4,0},{5,1},{6,2},{7,3},{8,12},{9,13},{10,... | collective-permute-start | bytes 798728 | tf_op jit(solution)/shard_map/ppermute | solution.py:409
  34.0 0.0 collective-permute-done.4.got_ref
  34.0 0.1 shard_map.92
  34.0 0.4 collective-permute-start.5
  34.4 0.0 collective-permute-done.3.got_ref
  34.5 0.1 shard_map.91.own_ref
  34.5 5.4 %collective-permute-done.9.refs_2_ = bf16[1040,128]{1,0:T(8,128)(2,1)S(1)} collective-permute-done((bf16[1040,128]{1,0:T(8,128)(2,1)S(1)}, bf16[1040,128]{1,0:T(8,128)(2,1)S(1)}, u32[]{:S(2)}, u32[]{:S(2)}) %collective-permute-start.9) | collective-permute-done | bytes 266272 | tf_op jit(solution)/shard_map/ppermute | solution.py:409
  39.9 6.2 %collective-permute-done.7.refs_1_ = bf16[1040,128]{1,0:T(8,128)(2,1)S(1)} collective-permute-done((bf16[1040,128]{1,0:T(8,128)(2,1)S(1)}, bf16[1040,128]{1,0:T(8,128)(2,1)S(1)}, u32[]{:S(2)}, u32[]{:S(2)}) %collective-permute-start.7) | collective-permute-done | bytes 266272 | tf_op jit(solution)/shard_map/ppermute | solution.py:409
  46.1 0.0 collective-permute-done.5.refs_0_
  46.1 0.0 copy-done.3
  46.1 0.2 shard_map.95
  46.3 1.4 %collective-permute-start.11 = (bf16[1024,128]{1,0:T(8,128)(2,1)S(1)}, bf16[1024,128]{1,0:T(8,128)(2,1)S(1)}, u32[]{:S(2)}, u32[]{:S(2)}) collective-permute-start(bf16[1024,128]{1,0:T(8,128)(2,1)S(1)} %get-tuple-element.33.refs_0_), channel_id=1, source_target_pairs={{0,2},{1,3},{2,0},{3,1},{4,6},{5,7},{6,4},{7,5},{8,10},{9,11},{10,... | collective-permute-start | bytes 786440 | tf_op jit(solution)/shard_map/ppermute | solution.py:409
  47.7 1.0 %collective-permute-start.13 = (bf16[1024,128]{1,0:T(8,128)(2,1)S(1)}, bf16[1024,128]{1,0:T(8,128)(2,1)S(1)}, u32[]{:S(2)}, u32[]{:S(2)}) collective-permute-start(bf16[1024,128]{1,0:T(8,128)(2,1)S(1)} %get-tuple-element.33.refs_0_), channel_id=1, source_target_pairs={{0,4},{1,5},{2,6},{3,7},{4,0},{5,1},{6,2},{7,3},{8,12},{9,13},{10,... | collective-permute-start | bytes 786440 | tf_op jit(solution)/shard_map/ppermute | solution.py:409
  48.7 1.2 %collective-permute-start.15 = (bf16[1024,128]{1,0:T(8,128)(2,1)S(1)}, bf16[1024,128]{1,0:T(8,128)(2,1)S(1)}, u32[]{:S(2)}, u32[]{:S(2)}) collective-permute-start(bf16[1024,128]{1,0:T(8,128)(2,1)S(1)} %get-tuple-element.33.refs_0_), channel_id=1, source_target_pairs={{0,6},{1,7},{2,4},{3,5},{4,2},{5,3},{6,0},{7,1},{8,14},{9,15},{10,... | collective-permute-start | bytes 786440 | tf_op jit(solution)/shard_map/ppermute | solution.py:409
  49.9 0.0 collective-permute-start.10
  49.9 5.8 %collective-permute-done.11.refs_2_ = bf16[1024,128]{1,0:T(8,128)(2,1)S(1)} collective-permute-done((bf16[1024,128]{1,0:T(8,128)(2,1)S(1)}, bf16[1024,128]{1,0:T(8,128)(2,1)S(1)}, u32[]{:S(2)}, u32[]{:S(2)}) %collective-permute-start.11) | collective-permute-done | bytes 262176 | tf_op jit(solution)/shard_map/ppermute | solution.py:409
  55.6 0.0 collective-permute-start.12
  55.6 4.9 %collective-permute-done.13.refs_4_ = bf16[1024,128]{1,0:T(8,128)(2,1)S(1)} collective-permute-done((bf16[1024,128]{1,0:T(8,128)(2,1)S(1)}, bf16[1024,128]{1,0:T(8,128)(2,1)S(1)}, u32[]{:S(2)}, u32[]{:S(2)}) %collective-permute-start.13) | collective-permute-done | bytes 262176 | tf_op jit(solution)/shard_map/ppermute | solution.py:409
  60.6 0.0 collective-permute-start.14
  60.6 0.0 collective-permute-done.15.refs_6_
  60.6 0.5 collective-permute-start.16
  61.1 0.0 collective-permute-done.10.refs_1_
  61.1 0.0 collective-permute-done.12.refs_3_
  61.1 1.0 %collective-permute-done.14.refs_5_ = bf16[1024,128]{1,0:T(8,128)(2,1)S(1)} collective-permute-done((bf16[1024,128]{1,0:T(8,128)(2,1)S(1)}, bf16[1024,128]{1,0:T(8,128)(2,1)S(1)}, u32[]{:S(2)}, u32[]{:S(2)}) %collective-permute-start.14) | collective-permute-done | bytes 262176 | tf_op jit(solution)/shard_map/ppermute | solution.py:409
  62.1 0.4 collective-permute-done.16.refs_7_
  62.5 2.4 %shard_map.98 = (bf16[1040,128]{1,0:T(8,128)(2,1)S(1)}, bf16[1040,128]{1,0:T(8,128)(2,1)S(1)}) custom-call(s32[1184]{0:T(1024)S(1)} %get-tuple-element.20.codes, s32[4]{0:T(128)S(1)} %get-tuple-element.21.counts, bf16[320,128,128]{2,1,0:T(8,128)(2,1)S(1)} %bitcast.7, bf16[1024,128]{1,0:T(8,128)(2,1)S(1)} %get-tuple-element.33.refs_0_, ...), custom_call_target="tpu_custom_call" | custom-call | flops 2684354560 | bytes 2621440 | tf_op jit(solution)/shard_map/pallas_call | solution.py:283
  64.9 6.2 %collective-permute-start.18 = (bf16[1040,128]{1,0:T(8,128)(2,1)S(1)}, bf16[1040,128]{1,0:T(8,128)(2,1)S(1)}, u32[]{:S(2)}, u32[]{:S(2)}) collective-permute-start(bf16[1040,128]{1,0:T(8,128)(2,1)S(1)} %get-tuple-element.36), channel_id=1, source_target_pairs={{0,16},{8,24},{16,0},{24,8},{1,17},{9,25},{17,1},{25,9},{2,18},{10... | collective-permute-start | bytes 798728 | tf_op jit(solution)/shard_map/ppermute | solution.py:409
  71.1 0.3 collective-permute-start.19
  71.4 2.4 %shard_map.97 = (bf16[1040,128]{1,0:T(8,128)(2,1)S(1)}, bf16[1040,128]{1,0:T(8,128)(2,1)S(1)}) custom-call(s32[1184]{0:T(1024)S(1)} %get-tuple-element.20.codes, s32[4]{0:T(128)S(1)} %get-tuple-element.21.counts, bf16[320,128,128]{2,1,0:T(8,128)(2,1)S(1)} %bitcast.8, bf16[1024,128]{1,0:T(8,128)(2,1)S(1)} %get-tuple-element.33.refs_0_, ...), custom_call_target="tpu_custom_call" | custom-call | flops 2684354560 | bytes 2621440 | tf_op jit(solution)/shard_map/pallas_call | solution.py:283
  73.8 0.9 collective-permute-start.17
  74.7 1.0 %shard_map.96 = f32[1024,128]{1,0:T(8,128)} custom-call(f32[1024,128]{1,0:T(8,128)S(1)} %get-tuple-element.32.turned_ref), custom_call_target="tpu_custom_call" | custom-call | tf_op jit(solution)/shard_map/pallas_call | solution.py:376
  75.7 13.2 %collective-permute-done.18.refs_2_ = bf16[1040,128]{1,0:T(8,128)(2,1)S(1)} collective-permute-done((bf16[1040,128]{1,0:T(8,128)(2,1)S(1)}, bf16[1040,128]{1,0:T(8,128)(2,1)S(1)}, u32[]{:S(2)}, u32[]{:S(2)}) %collective-permute-start.18) | collective-permute-done | bytes 266272 | tf_op jit(solution)/shard_map/ppermute | solution.py:409
  88.9 0.0 collective-permute-done.19.refs_3_
  88.9 3.1 %collective-permute-done.17.refs_1_ = bf16[1040,128]{1,0:T(8,128)(2,1)S(1)} collective-permute-done((bf16[1040,128]{1,0:T(8,128)(2,1)S(1)}, bf16[1040,128]{1,0:T(8,128)(2,1)S(1)}, u32[]{:S(2)}, u32[]{:S(2)}) %collective-permute-start.17) | collective-permute-done | bytes 266272 | tf_op jit(solution)/shard_map/ppermute | solution.py:409
  92.0 0.0 copy-done.4
  92.0 1.1 %shard_map.99 = f32[1024,128]{1,0:T(8,128)} custom-call(s32[8,128]{1,0:T(8,128)S(1)} %bitcast.10, bf16[1040,128]{1,0:T(8,128)(2,1)S(1)} %get-tuple-element.34.refs_0_, bf16[1040,128]{1,0:T(8,128)(2,1)S(1)} %collective-permute-done.17.refs_1_, bf16[1040,128]{1,0:T(8,128)(2,1)S(1)} %collective-permute-done.18.refs_2_, ...), custom_call_target="tpu_custom_call" | custom-call | tf_op jit(solution)/shard_map/pallas_call | solution.py:398
  (4 shorter events, 0.0 us)
Async XLA Ops:
  0.6 1.0 %copy-start.2 = (f32[1024,128]{1,0:T(8,128)S(1)}, f32[1024,128]{1,0:T(8,128)}, u32[]{:S(2)}) copy-start(f32[1024,128]{1,0:T(8,128)} %video_ref.1) | copy-start | bytes 1572868
  1.7 21.8 %collective-permute-start = (bf16[1024,128]{1,0:T(8,128)(2,1)S(1)}, bf16[1024,128]{1,0:T(8,128)(2,1)S(1)}, u32[]{:S(2)}, u32[]{:S(2)}) collective-permute-start(bf16[1024,128]{1,0:T(8,128)(2,1)S(1)} %shard_map.87.own_ref), channel_id=1, source_target_pairs={{0,8},{8,0},{16,24},{24,16},{1,9},{9,1},{17,25},{25,17},{2,10},{10... | collective-permute-start | bytes 786440 | tf_op jit(solution)/shard_map/ppermute | solution.py:409
  4.8 21.4 %collective-permute-start.1 = (bf16[1024,128]{1,0:T(8,128)(2,1)S(1)}, bf16[1024,128]{1,0:T(8,128)(2,1)S(1)}, u32[]{:S(2)}, u32[]{:S(2)}) collective-permute-start(bf16[1024,128]{1,0:T(8,128)(2,1)S(1)} %shard_map.87.own_ref), channel_id=1, source_target_pairs={{0,16},{8,24},{16,0},{24,8},{1,17},{9,25},{17,1},{25,9},{2,18},{10... | collective-permute-start | bytes 786440 | tf_op jit(solution)/shard_map/ppermute | solution.py:409
  7.4 18.8 %collective-permute-start.2 = (bf16[1024,128]{1,0:T(8,128)(2,1)S(1)}, bf16[1024,128]{1,0:T(8,128)(2,1)S(1)}, u32[]{:S(2)}, u32[]{:S(2)}) collective-permute-start(bf16[1024,128]{1,0:T(8,128)(2,1)S(1)} %shard_map.87.own_ref), channel_id=1, source_target_pairs={{0,24},{8,16},{16,8},{24,0},{1,25},{9,17},{17,9},{25,1},{2,26},{10... | collective-permute-start | bytes 786440 | tf_op jit(solution)/shard_map/ppermute | solution.py:409
  8.0 4.0 %copy-start = (bf16[1,1,320,128,128]{4,3,2,1,0:T(8,128)(2,1)S(1)}, bf16[1,1,320,128,128]{4,3,2,1,0:T(8,128)(2,1)}, u32[]{:S(2)}) copy-start(bf16[1,1,320,128,128]{4,3,2,1,0:T(8,128)(2,1)} %param.10) | copy-start | bytes 31457284
  12.0 0.7 copy-start.5
  12.7 0.7 copy-start.6
  13.4 4.0 %copy-start.1 = (bf16[1,1,320,128,128]{4,3,2,1,0:T(8,128)(2,1)S(1)}, bf16[1,1,320,128,128]{4,3,2,1,0:T(8,128)(2,1)}, u32[]{:S(2)}) copy-start(bf16[1,1,320,128,128]{4,3,2,1,0:T(8,128)(2,1)} %param.10) | copy-start | bytes 31457284
  26.2 19.9 %copy-start.3 = (s32[1024]{0:T(1024)S(1)}, s32[1024]{0:T(1024)}, u32[]{:S(2)}) copy-start(s32[1024]{0:T(1024)} %param.8) | copy-start | bytes 12292
  28.9 1.6 %collective-permute-start.8 = (bf16[1040,128]{1,0:T(8,128)(2,1)S(1)}, bf16[1040,128]{1,0:T(8,128)(2,1)S(1)}, u32[]{:S(2)}, u32[]{:S(2)}) collective-permute-start(bf16[1040,128]{1,0:T(8,128)(2,1)S(1)} %get-tuple-element.31), channel_id=1, source_target_pairs={{0,1},{1,0},{2,3},{3,2},{4,5},{5,4},{6,7},{7,6},{8,9},{9,8},{10,11... | collective-permute-start | bytes 798728 | tf_op jit(solution)/shard_map/ppermute | solution.py:409
  29.0 2.7 %collective-permute-start.6 = (bf16[1040,128]{1,0:T(8,128)(2,1)S(1)}, bf16[1040,128]{1,0:T(8,128)(2,1)S(1)}, u32[]{:S(2)}, u32[]{:S(2)}) collective-permute-start(bf16[1040,128]{1,0:T(8,128)(2,1)S(1)} %get-tuple-element.29), channel_id=1, source_target_pairs={{0,1},{1,0},{2,3},{3,2},{4,5},{5,4},{6,7},{7,6},{8,9},{9,8},{10,11... | collective-permute-start | bytes 798728 | tf_op jit(solution)/shard_map/ppermute | solution.py:409
  29.5 4.5 %collective-permute-start.4 = (bf16[1040,128]{1,0:T(8,128)(2,1)S(1)}, bf16[1040,128]{1,0:T(8,128)(2,1)S(1)}, u32[]{:S(2)}, u32[]{:S(2)}) collective-permute-start(bf16[1040,128]{1,0:T(8,128)(2,1)S(1)} %get-tuple-element.27), channel_id=1, source_target_pairs={{0,1},{1,0},{2,3},{3,2},{4,5},{5,4},{6,7},{7,6},{8,9},{9,8},{10,11... | collective-permute-start | bytes 798728 | tf_op jit(solution)/shard_map/ppermute | solution.py:409
  29.6 4.9 %collective-permute-start.3 = (bf16[1040,128]{1,0:T(8,128)(2,1)S(1)}, bf16[1040,128]{1,0:T(8,128)(2,1)S(1)}, u32[]{:S(2)}, u32[]{:S(2)}) collective-permute-start(bf16[1040,128]{1,0:T(8,128)(2,1)S(1)} %get-tuple-element.25), channel_id=1, source_target_pairs={{0,1},{1,0},{2,3},{3,2},{4,5},{5,4},{6,7},{7,6},{8,9},{9,8},{10,11... | collective-permute-start | bytes 798728 | tf_op jit(solution)/shard_map/ppermute | solution.py:409
  30.6 9.3 %collective-permute-start.9 = (bf16[1040,128]{1,0:T(8,128)(2,1)S(1)}, bf16[1040,128]{1,0:T(8,128)(2,1)S(1)}, u32[]{:S(2)}, u32[]{:S(2)}) collective-permute-start(bf16[1040,128]{1,0:T(8,128)(2,1)S(1)} %shard_map.94), channel_id=1, source_target_pairs={{0,2},{1,3},{2,0},{3,1},{4,6},{5,7},{6,4},{7,5},{8,10},{9,11},{10,... | collective-permute-start | bytes 798728 | tf_op jit(solution)/shard_map/ppermute | solution.py:409
  31.8 14.3 %collective-permute-start.7 = (bf16[1040,128]{1,0:T(8,128)(2,1)S(1)}, bf16[1040,128]{1,0:T(8,128)(2,1)S(1)}, u32[]{:S(2)}, u32[]{:S(2)}) collective-permute-start(bf16[1040,128]{1,0:T(8,128)(2,1)S(1)} %shard_map.93), channel_id=1, source_target_pairs={{0,4},{1,5},{2,6},{3,7},{4,0},{5,1},{6,2},{7,3},{8,12},{9,13},{10,... | collective-permute-start | bytes 798728 | tf_op jit(solution)/shard_map/ppermute | solution.py:409
  34.0 12.1 %collective-permute-start.5 = (bf16[1040,128]{1,0:T(8,128)(2,1)S(1)}, bf16[1040,128]{1,0:T(8,128)(2,1)S(1)}, u32[]{:S(2)}, u32[]{:S(2)}) collective-permute-start(bf16[1040,128]{1,0:T(8,128)(2,1)S(1)} %shard_map.92), channel_id=1, source_target_pairs={{0,6},{1,7},{2,4},{3,5},{4,2},{5,3},{6,0},{7,1},{8,14},{9,15},{10,... | collective-permute-start | bytes 798728 | tf_op jit(solution)/shard_map/ppermute | solution.py:409
  46.3 9.3 %collective-permute-start.11 = (bf16[1024,128]{1,0:T(8,128)(2,1)S(1)}, bf16[1024,128]{1,0:T(8,128)(2,1)S(1)}, u32[]{:S(2)}, u32[]{:S(2)}) collective-permute-start(bf16[1024,128]{1,0:T(8,128)(2,1)S(1)} %get-tuple-element.33.refs_0_), channel_id=1, source_target_pairs={{0,2},{1,3},{2,0},{3,1},{4,6},{5,7},{6,4},{7,5},{8,10},{9,11},{10,... | collective-permute-start | bytes 786440 | tf_op jit(solution)/shard_map/ppermute | solution.py:409
  47.7 12.9 %collective-permute-start.13 = (bf16[1024,128]{1,0:T(8,128)(2,1)S(1)}, bf16[1024,128]{1,0:T(8,128)(2,1)S(1)}, u32[]{:S(2)}, u32[]{:S(2)}) collective-permute-start(bf16[1024,128]{1,0:T(8,128)(2,1)S(1)} %get-tuple-element.33.refs_0_), channel_id=1, source_target_pairs={{0,4},{1,5},{2,6},{3,7},{4,0},{5,1},{6,2},{7,3},{8,12},{9,13},{10,... | collective-permute-start | bytes 786440 | tf_op jit(solution)/shard_map/ppermute | solution.py:409
  48.7 11.9 %collective-permute-start.15 = (bf16[1024,128]{1,0:T(8,128)(2,1)S(1)}, bf16[1024,128]{1,0:T(8,128)(2,1)S(1)}, u32[]{:S(2)}, u32[]{:S(2)}) collective-permute-start(bf16[1024,128]{1,0:T(8,128)(2,1)S(1)} %get-tuple-element.33.refs_0_), channel_id=1, source_target_pairs={{0,6},{1,7},{2,4},{3,5},{4,2},{5,3},{6,0},{7,1},{8,14},{9,15},{10,... | collective-permute-start | bytes 786440 | tf_op jit(solution)/shard_map/ppermute | solution.py:409
  49.9 11.2 %collective-permute-start.10 = (bf16[1024,128]{1,0:T(8,128)(2,1)S(1)}, bf16[1024,128]{1,0:T(8,128)(2,1)S(1)}, u32[]{:S(2)}, u32[]{:S(2)}) collective-permute-start(bf16[1024,128]{1,0:T(8,128)(2,1)S(1)} %get-tuple-element.33.refs_0_), channel_id=1, source_target_pairs={{0,1},{1,0},{2,3},{3,2},{4,5},{5,4},{6,7},{7,6},{8,9},{9,8},{10,11... | collective-permute-start | bytes 786440 | tf_op jit(solution)/shard_map/ppermute | solution.py:409
  55.6 5.5 %collective-permute-start.12 = (bf16[1024,128]{1,0:T(8,128)(2,1)S(1)}, bf16[1024,128]{1,0:T(8,128)(2,1)S(1)}, u32[]{:S(2)}, u32[]{:S(2)}) collective-permute-start(bf16[1024,128]{1,0:T(8,128)(2,1)S(1)} %collective-permute-done.11.refs_2_), channel_id=1, source_target_pairs={{0,1},{1,0},{2,3},{3,2},{4,5},{5,4},{6,7},{7,6},{8,9},{9,8},{10,11... | collective-permute-start | bytes 786440 | tf_op jit(solution)/shard_map/ppermute | solution.py:409
  60.6 1.5 %collective-permute-start.14 = (bf16[1024,128]{1,0:T(8,128)(2,1)S(1)}, bf16[1024,128]{1,0:T(8,128)(2,1)S(1)}, u32[]{:S(2)}, u32[]{:S(2)}) collective-permute-start(bf16[1024,128]{1,0:T(8,128)(2,1)S(1)} %collective-permute-done.13.refs_4_), channel_id=1, source_target_pairs={{0,1},{1,0},{2,3},{3,2},{4,5},{5,4},{6,7},{7,6},{8,9},{9,8},{10,11... | collective-permute-start | bytes 786440 | tf_op jit(solution)/shard_map/ppermute | solution.py:409
  60.6 1.9 %collective-permute-start.16 = (bf16[1024,128]{1,0:T(8,128)(2,1)S(1)}, bf16[1024,128]{1,0:T(8,128)(2,1)S(1)}, u32[]{:S(2)}, u32[]{:S(2)}) collective-permute-start(bf16[1024,128]{1,0:T(8,128)(2,1)S(1)} %collective-permute-done.15.refs_6_), channel_id=1, source_target_pairs={{0,1},{1,0},{2,3},{3,2},{4,5},{5,4},{6,7},{7,6},{8,9},{9,8},{10,11... | collective-permute-start | bytes 786440 | tf_op jit(solution)/shard_map/ppermute | solution.py:409
  64.9 24.0 %collective-permute-start.18 = (bf16[1040,128]{1,0:T(8,128)(2,1)S(1)}, bf16[1040,128]{1,0:T(8,128)(2,1)S(1)}, u32[]{:S(2)}, u32[]{:S(2)}) collective-permute-start(bf16[1040,128]{1,0:T(8,128)(2,1)S(1)} %get-tuple-element.36), channel_id=1, source_target_pairs={{0,16},{8,24},{16,0},{24,8},{1,17},{9,25},{17,1},{25,9},{2,18},{10... | collective-permute-start | bytes 798728 | tf_op jit(solution)/shard_map/ppermute | solution.py:409
  71.1 21.0 %copy-start.4 = (s32[1024]{0:T(1024)S(1)}, s32[1024]{0:T(1024)}, u32[]{:S(2)}) copy-start(s32[1024]{0:T(1024)} %param.9) | copy-start | bytes 12292
  71.1 17.9 %collective-permute-start.19 = (bf16[1040,128]{1,0:T(8,128)(2,1)S(1)}, bf16[1040,128]{1,0:T(8,128)(2,1)S(1)}, u32[]{:S(2)}, u32[]{:S(2)}) collective-permute-start(bf16[1040,128]{1,0:T(8,128)(2,1)S(1)} %get-tuple-element.37), channel_id=1, source_target_pairs={{0,24},{8,16},{16,8},{24,0},{1,25},{9,17},{17,9},{25,1},{2,26},{10... | collective-permute-start | bytes 798728 | tf_op jit(solution)/shard_map/ppermute | solution.py:409
  73.8 18.2 %collective-permute-start.17 = (bf16[1040,128]{1,0:T(8,128)(2,1)S(1)}, bf16[1040,128]{1,0:T(8,128)(2,1)S(1)}, u32[]{:S(2)}, u32[]{:S(2)}) collective-permute-start(bf16[1040,128]{1,0:T(8,128)(2,1)S(1)} %get-tuple-element.35), channel_id=1, source_target_pairs={{0,8},{8,0},{16,24},{24,16},{1,9},{9,1},{17,25},{25,17},{2,10},{10... | collective-permute-start | bytes 798728 | tf_op jit(solution)/shard_map/ppermute | solution.py:409

commit v6 on v5

--- a/solution.py
+++ b/solution.py
@@ -90,14 +90,19 @@
     cap = (codes.shape[0] - 128) // 3
     for n in lists:
 
-        def group(g, carry):
-            for k in range(GROUP):
-                code = codes[n * cap + g * GROUP + k]
+        def group(start, size):
+            for k in range(size):
+                code = codes[n * cap + start + k]
                 col = lax.shift_right_logical(code, 12) & 0xFF
                 visit(code & 0xFFF, col, lax.shift_right_logical(code, 20))
+
+        def whole(g, carry):
+            group(g * GROUP, GROUP)
             return carry
 
-        lax.fori_loop(0, lax.div(counts[n] + (GROUP - 1), GROUP), group, 0)
+        full = lax.div(counts[n] + (GROUP // 2 - 1), GROUP)
+        lax.fori_loop(0, full, whole, 0)
+        pl.when(counts[n] > full * GROUP)(lambda: group(full * GROUP, GROUP // 2))
 
 
 def fill_panel(panel, piece_refs):

time: 94.5 us -> 94.2 us (level); the launches traced: 93.1 us -> 94 us
  Pallas kernels: 20.9 us -> 26.8 us
  starting transfers between devices: 21.9 us -> 16.6 us
  waiting for transfers between devices: 41.6 us -> 42.7 us
  local copies, waits for them, and re-layouts: 7.34 us -> 6.38 us
    ppermute x20, starting transfers between devices: 21.9 us -> 16.6 us  [partner(): return lax.ppermute(value, axis, [(i, i ^ mask) for i in range(size)])]
    pallas_call x1, Pallas kernels: 6.19 us -> 8.04 us  [early_sweep(): pl.pallas_call(early_kernel, in_specs=[smem] * 2 + [VMEM] * 2, out_specs=...]
    pallas_call x2, Pallas kernels: 4.79 us -> 6.36 us  [reverse_sweep(): pl.pallas_call(functools.partial(reverse_kernel, pieces=len(pieces), list...]
    pallas_call x1, Pallas kernels: 3.01 us -> 4.22 us  [plan(): pl.pallas_call(functools.partial(plan_kernel, cap=cap, half=col_tiles //...]
    ppermute x20, waiting for transfers between devices: 41.6 us -> 42.7 us  [partner(): return lax.ppermute(value, axis, [(i, i ^ mask) for i in range(size)])]
    unnamed x14, local copies, waits for them, and re-layouts: 7.34 us -> 6.38 us
  transfers between devices with their start and end apart: 20 -> 20, of which waited for: 10 -> 10; matrix products, arithmetic and copies ran while one was open for 0% -> 0% of each run, Pallas kernels for 15% -> 20%
where the time goes in v6:
time: 94.2 us; the launch traced here: 94 us
  waiting for transfers between devices  42.7 us (45%)
  Pallas kernels  26.8 us (28%)
  starting transfers between devices  16.6 us (18%)
  local copies, waits for them, and re-layouts  6.38 us (7%)
  between operations  1.44 us (2%)
    ppermute x20, waiting for transfers between devices, partner(): return lax.ppermute(value, axis, [(i, i ^ mask) for i in range(size)])  42.7 us
    ppermute x20, starting transfers between devices, partner(): return lax.ppermute(value, axis, [(i, i ^ mask) for i in range(size)])  16.6 us
    pallas_call x1, Pallas kernels, early_sweep(): pl.pallas_call(early_kernel, in_specs=[smem] * 2 + [VMEM] * 2, out_specs=...  8.04 us
    unnamed x14, local copies, waits for them, and re-layouts  6.38 us
    pallas_call x2, Pallas kernels, reverse_sweep(): pl.pallas_call(functools.partial(reverse_kernel, pieces=len(pieces), list...  6.36 us
    pallas_call x1, Pallas kernels, plan(): pl.pallas_call(functools.partial(plan_kernel, cap=cap, half=col_tiles //...  4.22 us
    pallas_call x1, Pallas kernels, late_sweep(): pl.pallas_call(functools.partial(late_kernel, shard=shard), in_specs=[sme...  3.59 us
    pallas_call x1, Pallas kernels, middle_sweep(): pl.pallas_call(functools.partial(middle_kernel, shard=shard), in_specs=[s...  2.04 us
  transfers between devices with their start and end apart: 20, of which 10 were waited for; matrix products, arithmetic and copies ran while one was open for 0% of the time, Pallas kernels for 20%

profile of v6, /device:TPU:0, one launch (start us, length us, event | category | flops | bytes accessed | tf_op | source)
XLA Modules:
  0.0 94.0 jit_solution(11004908077811340560)
XLA Ops:
  0.6 0.0 copy-start.2
  0.6 1.0 %copy-done.2 = f32[1024,128]{1,0:T(8,128)S(1)} copy-done((f32[1024,128]{1,0:T(8,128)S(1)}, f32[1024,128]{1,0:T(8,128)}, u32[]{:S(2)}) %copy-start.2) | copy-done | bytes 524312
  1.7 3.1 %collective-permute-start = (bf16[1024,128]{1,0:T(8,128)(2,1)S(1)}, bf16[1024,128]{1,0:T(8,128)(2,1)S(1)}, u32[]{:S(2)}, u32[]{:S(2)}) collective-permute-start(bf16[1024,128]{1,0:T(8,128)(2,1)S(1)} %shard_map.87.own_ref), channel_id=1, source_target_pairs={{0,8},{8,0},{16,24},{24,16},{1,9},{9,1},{17,25},{25,17},{2,10},{10... | collective-permute-start | bytes 786440 | tf_op jit(solution)/shard_map/ppermute | solution.py:414
  4.8 2.6 %collective-permute-start.1 = (bf16[1024,128]{1,0:T(8,128)(2,1)S(1)}, bf16[1024,128]{1,0:T(8,128)(2,1)S(1)}, u32[]{:S(2)}, u32[]{:S(2)}) collective-permute-start(bf16[1024,128]{1,0:T(8,128)(2,1)S(1)} %shard_map.87.own_ref), channel_id=1, source_target_pairs={{0,16},{8,24},{16,0},{24,8},{1,17},{9,25},{17,1},{25,9},{2,18},{10... | collective-permute-start | bytes 786440 | tf_op jit(solution)/shard_map/ppermute | solution.py:414
  7.4 0.0 collective-permute-start.2
  8.0 0.0 copy-start
  8.0 4.0 %copy-done = bf16[1,1,320,128,128]{4,3,2,1,0:T(8,128)(2,1)S(1)} copy-done((bf16[1,1,320,128,128]{4,3,2,1,0:T(8,128)(2,1)S(1)}, bf16[1,1,320,128,128]{4,3,2,1,0:T(8,128)(2,1)}, u32[]{:S(2)}) %copy-start) | copy-done | bytes 10485784
  12.0 0.0 copy-start.5
  12.0 0.7 copy-done.5
  12.7 0.7 copy-done.6
  13.4 4.2 %shard_map.86 = (s32[1184]{0:T(1024)S(1)}, s32[4]{0:T(128)S(1)}) custom-call(s32[1,1,320]{2,1,0:T(1,128)S(1)} %copy-done.5, s32[1,1,320]{2,1,0:T(1,128)S(1)} %copy-done.6, s32[1,1]{1,0:T(1,128)S(6)} %copy.9.live_ref, bf16[320,128,128]{2,1,0:T(8,128)(2,1)S(1)} %bitcast.3), custom_call_target="tpu_custom_call" | custom-call | tf_op jit(solution)/shard_map/pallas_call | solution.py:77
  17.6 0.0 copy-done.1
  17.6 8.0 %shard_map.88 = (f32[65,128,128]{2,1,0:T(8,128)S(1)}, f32[64,8,128]{2,1,0:T(8,128)S(1)}) custom-call(s32[1184]{0:T(1024)S(1)} %get-tuple-element.20.codes, s32[4]{0:T(128)S(1)} %get-tuple-element.21.counts, bf16[320,128,128]{2,1,0:T(8,128)(2,1)S(1)} %bitcast.4, bf16[1024,128]{1,0:T(8,128)(2,1)S(1)} %shard_map.87.own_ref), custom_call_target="tpu_custom_call" | custom-call | flops 2684354560 | bytes 2621440 | tf_op jit(solution)/shard_map/pallas_call | solution.py:194
  25.7 0.0 collective-permute-done.refs_0_
  25.7 2.0 %shard_map.89.sums_ref = f32[65,128,128]{2,1,0:T(8,128)S(1)} custom-call(s32[1184]{0:T(1024)S(1)} %get-tuple-element.20.codes, s32[4]{0:T(128)S(1)} %get-tuple-element.21.counts, bf16[320,128,128]{2,1,0:T(8,128)(2,1)S(1)} %bitcast.5, f32[65,128,128]{2,1,0:T(8,128)S(1)} %get-tuple-element.22.sums_ref, bf16[1024,128]{1,0:T(8,128)(2,1)S(1)} %collective-permute-done.refs_0_), custom_call_target="tpu_custom_call" | custom-call | flops 2684354560 | bytes 2621440 | tf_op jit(solution)/shard_map/pallas_call | solution.py:211
  27.7 0.0 collective-permute-done.1.refs_0_
  27.7 0.0 collective-permute-done.2.refs_1_
  27.7 0.0 copy-start.3
  27.8 3.6 %shard_map.90 = (bf16[1040,128]{1,0:T(8,128)(2,1)S(1)}, bf16[1040,128]{1,0:T(8,128)(2,1)S(1)}, bf16[1040,128]{1,0:T(8,128)(2,1)S(1)}, bf16[1040,128]{1,0:T(8,128...) custom-call(s32[1184]{0:T(1024)S(1)} %get-tuple-element.20.codes, ...), custom_call_target="tpu_custom_call" | custom-call | flops 2684354560 | bytes 2621440 | tf_op jit(solution)/shard_map/pallas_call | solution.py:251
  31.4 0.1 collective-permute-start.8
  31.4 0.5 collective-permute-start.6
  31.9 0.1 collective-permute-start.4
  32.0 0.4 collective-permute-start.3
  32.4 0.5 collective-permute-done.8.got_ref
  33.0 0.1 shard_map.94
  33.0 0.1 collective-permute-start.9
  33.1 0.2 collective-permute-done.6.got_ref
  33.3 0.1 shard_map.93
  33.4 3.6 %collective-permute-start.7 = (bf16[1040,128]{1,0:T(8,128)(2,1)S(1)}, bf16[1040,128]{1,0:T(8,128)(2,1)S(1)}, u32[]{:S(2)}, u32[]{:S(2)}) collective-permute-start(bf16[1040,128]{1,0:T(8,128)(2,1)S(1)} %shard_map.93), channel_id=1, source_target_pairs={{0,4},{1,5},{2,6},{3,7},{4,0},{5,1},{6,2},{7,3},{8,12},{9,13},{10,... | collective-permute-start | bytes 798728 | tf_op jit(solution)/shard_map/ppermute | solution.py:414
  37.0 0.0 collective-permute-done.4.got_ref
  37.0 0.1 shard_map.92
  37.1 0.1 collective-permute-start.5
  37.2 0.0 collective-permute-done.3.got_ref
  37.2 0.1 shard_map.91.own_ref
  37.2 5.1 %collective-permute-done.9.refs_2_ = bf16[1040,128]{1,0:T(8,128)(2,1)S(1)} collective-permute-done((bf16[1040,128]{1,0:T(8,128)(2,1)S(1)}, bf16[1040,128]{1,0:T(8,128)(2,1)S(1)}, u32[]{:S(2)}, u32[]{:S(2)}) %collective-permute-start.9) | collective-permute-done | bytes 266272 | tf_op jit(solution)/shard_map/ppermute | solution.py:414
  42.3 6.8 %collective-permute-done.7.refs_1_ = bf16[1040,128]{1,0:T(8,128)(2,1)S(1)} collective-permute-done((bf16[1040,128]{1,0:T(8,128)(2,1)S(1)}, bf16[1040,128]{1,0:T(8,128)(2,1)S(1)}, u32[]{:S(2)}, u32[]{:S(2)}) %collective-permute-start.7) | collective-permute-done | bytes 266272 | tf_op jit(solution)/shard_map/ppermute | solution.py:414
  49.1 0.0 collective-permute-done.5.refs_0_
  49.1 0.0 copy-done.3
  49.1 0.2 shard_map.95
  49.4 1.4 %collective-permute-start.11 = (bf16[1024,128]{1,0:T(8,128)(2,1)S(1)}, bf16[1024,128]{1,0:T(8,128)(2,1)S(1)}, u32[]{:S(2)}, u32[]{:S(2)}) collective-permute-start(bf16[1024,128]{1,0:T(8,128)(2,1)S(1)} %get-tuple-element.33.refs_0_), channel_id=1, source_target_pairs={{0,2},{1,3},{2,0},{3,1},{4,6},{5,7},{6,4},{7,5},{8,10},{9,11},{10,... | collective-permute-start | bytes 786440 | tf_op jit(solution)/shard_map/ppermute | solution.py:414
  50.7 0.9 %collective-permute-start.13 = (bf16[1024,128]{1,0:T(8,128)(2,1)S(1)}, bf16[1024,128]{1,0:T(8,128)(2,1)S(1)}, u32[]{:S(2)}, u32[]{:S(2)}) collective-permute-start(bf16[1024,128]{1,0:T(8,128)(2,1)S(1)} %get-tuple-element.33.refs_0_), channel_id=1, source_target_pairs={{0,4},{1,5},{2,6},{3,7},{4,0},{5,1},{6,2},{7,3},{8,12},{9,13},{10,... | collective-permute-start | bytes 786440 | tf_op jit(solution)/shard_map/ppermute | solution.py:414
  51.7 1.2 %collective-permute-start.15 = (bf16[1024,128]{1,0:T(8,128)(2,1)S(1)}, bf16[1024,128]{1,0:T(8,128)(2,1)S(1)}, u32[]{:S(2)}, u32[]{:S(2)}) collective-permute-start(bf16[1024,128]{1,0:T(8,128)(2,1)S(1)} %get-tuple-element.33.refs_0_), channel_id=1, source_target_pairs={{0,6},{1,7},{2,4},{3,5},{4,2},{5,3},{6,0},{7,1},{8,14},{9,15},{10,... | collective-permute-start | bytes 786440 | tf_op jit(solution)/shard_map/ppermute | solution.py:414
  52.9 0.0 collective-permute-start.10
  52.9 5.8 %collective-permute-done.11.refs_2_ = bf16[1024,128]{1,0:T(8,128)(2,1)S(1)} collective-permute-done((bf16[1024,128]{1,0:T(8,128)(2,1)S(1)}, bf16[1024,128]{1,0:T(8,128)(2,1)S(1)}, u32[]{:S(2)}, u32[]{:S(2)}) %collective-permute-start.11) | collective-permute-done | bytes 262176 | tf_op jit(solution)/shard_map/ppermute | solution.py:414
  58.7 0.0 collective-permute-start.12
  58.7 4.9 %collective-permute-done.13.refs_4_ = bf16[1024,128]{1,0:T(8,128)(2,1)S(1)} collective-permute-done((bf16[1024,128]{1,0:T(8,128)(2,1)S(1)}, bf16[1024,128]{1,0:T(8,128)(2,1)S(1)}, u32[]{:S(2)}, u32[]{:S(2)}) %collective-permute-start.13) | collective-permute-done | bytes 262176 | tf_op jit(solution)/shard_map/ppermute | solution.py:414
  63.6 0.0 collective-permute-start.14
  63.6 0.0 collective-permute-done.15.refs_6_
  63.6 0.5 collective-permute-start.16
  64.1 0.0 collective-permute-done.10.refs_1_
  64.1 0.0 collective-permute-done.12.refs_3_
  64.1 1.0 %collective-permute-done.14.refs_5_ = bf16[1024,128]{1,0:T(8,128)(2,1)S(1)} collective-permute-done((bf16[1024,128]{1,0:T(8,128)(2,1)S(1)}, bf16[1024,128]{1,0:T(8,128)(2,1)S(1)}, u32[]{:S(2)}, u32[]{:S(2)}) %collective-permute-start.14) | collective-permute-done | bytes 262176 | tf_op jit(solution)/shard_map/ppermute | solution.py:414
  65.1 0.4 collective-permute-done.16.refs_7_
  65.5 3.2 %shard_map.98 = (bf16[1040,128]{1,0:T(8,128)(2,1)S(1)}, bf16[1040,128]{1,0:T(8,128)(2,1)S(1)}) custom-call(s32[1184]{0:T(1024)S(1)} %get-tuple-element.20.codes, s32[4]{0:T(128)S(1)} %get-tuple-element.21.counts, bf16[320,128,128]{2,1,0:T(8,128)(2,1)S(1)} %bitcast.7, bf16[1024,128]{1,0:T(8,128)(2,1)S(1)} %get-tuple-element.33.refs_0_, ...), custom_call_target="tpu_custom_call" | custom-call | flops 2684354560 | bytes 2621440 | tf_op jit(solution)/shard_map/pallas_call | solution.py:288
  68.7 0.6 collective-permute-start.18
  69.3 1.2 %collective-permute-start.19 = (bf16[1040,128]{1,0:T(8,128)(2,1)S(1)}, bf16[1040,128]{1,0:T(8,128)(2,1)S(1)}, u32[]{:S(2)}, u32[]{:S(2)}) collective-permute-start(bf16[1040,128]{1,0:T(8,128)(2,1)S(1)} %get-tuple-element.37), channel_id=1, source_target_pairs={{0,24},{8,16},{16,8},{24,0},{1,25},{9,17},{17,9},{25,1},{2,26},{10... | collective-permute-start | bytes 798728 | tf_op jit(solution)/shard_map/ppermute | solution.py:414
  70.5 3.2 %shard_map.97 = (bf16[1040,128]{1,0:T(8,128)(2,1)S(1)}, bf16[1040,128]{1,0:T(8,128)(2,1)S(1)}) custom-call(s32[1184]{0:T(1024)S(1)} %get-tuple-element.20.codes, s32[4]{0:T(128)S(1)} %get-tuple-element.21.counts, bf16[320,128,128]{2,1,0:T(8,128)(2,1)S(1)} %bitcast.8, bf16[1024,128]{1,0:T(8,128)(2,1)S(1)} %get-tuple-element.33.refs_0_, ...), custom_call_target="tpu_custom_call" | custom-call | flops 2684354560 | bytes 2621440 | tf_op jit(solution)/shard_map/pallas_call | solution.py:288
  73.7 0.2 collective-permute-start.17
  73.9 1.0 %shard_map.96 = f32[1024,128]{1,0:T(8,128)} custom-call(f32[1024,128]{1,0:T(8,128)S(1)} %get-tuple-element.32.turned_ref), custom_call_target="tpu_custom_call" | custom-call | tf_op jit(solution)/shard_map/pallas_call | solution.py:381
  74.9 14.4 %collective-permute-done.18.refs_2_ = bf16[1040,128]{1,0:T(8,128)(2,1)S(1)} collective-permute-done((bf16[1040,128]{1,0:T(8,128)(2,1)S(1)}, bf16[1040,128]{1,0:T(8,128)(2,1)S(1)}, u32[]{:S(2)}, u32[]{:S(2)}) %collective-permute-start.18) | collective-permute-done | bytes 266272 | tf_op jit(solution)/shard_map/ppermute | solution.py:414
  89.3 0.0 collective-permute-done.19.refs_3_
  89.3 3.6 %collective-permute-done.17.refs_1_ = bf16[1040,128]{1,0:T(8,128)(2,1)S(1)} collective-permute-done((bf16[1040,128]{1,0:T(8,128)(2,1)S(1)}, bf16[1040,128]{1,0:T(8,128)(2,1)S(1)}, u32[]{:S(2)}, u32[]{:S(2)}) %collective-permute-start.17) | collective-permute-done | bytes 266272 | tf_op jit(solution)/shard_map/ppermute | solution.py:414
  92.9 0.0 copy-done.4
  92.9 1.1 %shard_map.99 = f32[1024,128]{1,0:T(8,128)} custom-call(s32[8,128]{1,0:T(8,128)S(1)} %bitcast.10, bf16[1040,128]{1,0:T(8,128)(2,1)S(1)} %get-tuple-element.34.refs_0_, bf16[1040,128]{1,0:T(8,128)(2,1)S(1)} %collective-permute-done.17.refs_1_, bf16[1040,128]{1,0:T(8,128)(2,1)S(1)} %collective-permute-done.18.refs_2_, ...), custom_call_target="tpu_custom_call" | custom-call | tf_op jit(solution)/shard_map/pallas_call | solution.py:403
  (4 shorter events, 0.0 us)
Async XLA Ops:
  0.6 1.0 %copy-start.2 = (f32[1024,128]{1,0:T(8,128)S(1)}, f32[1024,128]{1,0:T(8,128)}, u32[]{:S(2)}) copy-start(f32[1024,128]{1,0:T(8,128)} %video_ref.1) | copy-start | bytes 1572868
  1.7 24.0 %collective-permute-start = (bf16[1024,128]{1,0:T(8,128)(2,1)S(1)}, bf16[1024,128]{1,0:T(8,128)(2,1)S(1)}, u32[]{:S(2)}, u32[]{:S(2)}) collective-permute-start(bf16[1024,128]{1,0:T(8,128)(2,1)S(1)} %shard_map.87.own_ref), channel_id=1, source_target_pairs={{0,8},{8,0},{16,24},{24,16},{1,9},{9,1},{17,25},{25,17},{2,10},{10... | collective-permute-start | bytes 786440 | tf_op jit(solution)/shard_map/ppermute | solution.py:414
  4.8 22.9 %collective-permute-start.1 = (bf16[1024,128]{1,0:T(8,128)(2,1)S(1)}, bf16[1024,128]{1,0:T(8,128)(2,1)S(1)}, u32[]{:S(2)}, u32[]{:S(2)}) collective-permute-start(bf16[1024,128]{1,0:T(8,128)(2,1)S(1)} %shard_map.87.own_ref), channel_id=1, source_target_pairs={{0,16},{8,24},{16,0},{24,8},{1,17},{9,25},{17,1},{25,9},{2,18},{10... | collective-permute-start | bytes 786440 | tf_op jit(solution)/shard_map/ppermute | solution.py:414
  7.4 20.4 %collective-permute-start.2 = (bf16[1024,128]{1,0:T(8,128)(2,1)S(1)}, bf16[1024,128]{1,0:T(8,128)(2,1)S(1)}, u32[]{:S(2)}, u32[]{:S(2)}) collective-permute-start(bf16[1024,128]{1,0:T(8,128)(2,1)S(1)} %shard_map.87.own_ref), channel_id=1, source_target_pairs={{0,24},{8,16},{16,8},{24,0},{1,25},{9,17},{17,9},{25,1},{2,26},{10... | collective-permute-start | bytes 786440 | tf_op jit(solution)/shard_map/ppermute | solution.py:414
  8.0 4.0 %copy-start = (bf16[1,1,320,128,128]{4,3,2,1,0:T(8,128)(2,1)S(1)}, bf16[1,1,320,128,128]{4,3,2,1,0:T(8,128)(2,1)}, u32[]{:S(2)}) copy-start(bf16[1,1,320,128,128]{4,3,2,1,0:T(8,128)(2,1)} %param.10) | copy-start | bytes 31457284
  12.0 0.7 copy-start.5
  12.7 0.7 copy-start.6
  13.4 4.2 %copy-start.1 = (bf16[1,1,320,128,128]{4,3,2,1,0:T(8,128)(2,1)S(1)}, bf16[1,1,320,128,128]{4,3,2,1,0:T(8,128)(2,1)}, u32[]{:S(2)}) copy-start(bf16[1,1,320,128,128]{4,3,2,1,0:T(8,128)(2,1)} %param.10) | copy-start | bytes 31457284
  27.7 21.4 %copy-start.3 = (s32[1024]{0:T(1024)S(1)}, s32[1024]{0:T(1024)}, u32[]{:S(2)}) copy-start(s32[1024]{0:T(1024)} %param.8) | copy-start | bytes 12292
  31.4 1.6 %collective-permute-start.8 = (bf16[1040,128]{1,0:T(8,128)(2,1)S(1)}, bf16[1040,128]{1,0:T(8,128)(2,1)S(1)}, u32[]{:S(2)}, u32[]{:S(2)}) collective-permute-start(bf16[1040,128]{1,0:T(8,128)(2,1)S(1)} %get-tuple-element.31), channel_id=1, source_target_pairs={{0,1},{1,0},{2,3},{3,2},{4,5},{5,4},{6,7},{7,6},{8,9},{9,8},{10,11... | collective-permute-start | bytes 798728 | tf_op jit(solution)/shard_map/ppermute | solution.py:414
  31.4 1.9 %collective-permute-start.6 = (bf16[1040,128]{1,0:T(8,128)(2,1)S(1)}, bf16[1040,128]{1,0:T(8,128)(2,1)S(1)}, u32[]{:S(2)}, u32[]{:S(2)}) collective-permute-start(bf16[1040,128]{1,0:T(8,128)(2,1)S(1)} %get-tuple-element.29), channel_id=1, source_target_pairs={{0,1},{1,0},{2,3},{3,2},{4,5},{5,4},{6,7},{7,6},{8,9},{9,8},{10,11... | collective-permute-start | bytes 798728 | tf_op jit(solution)/shard_map/ppermute | solution.py:414
  31.9 5.1 %collective-permute-start.4 = (bf16[1040,128]{1,0:T(8,128)(2,1)S(1)}, bf16[1040,128]{1,0:T(8,128)(2,1)S(1)}, u32[]{:S(2)}, u32[]{:S(2)}) collective-permute-start(bf16[1040,128]{1,0:T(8,128)(2,1)S(1)} %get-tuple-element.27), channel_id=1, source_target_pairs={{0,1},{1,0},{2,3},{3,2},{4,5},{5,4},{6,7},{7,6},{8,9},{9,8},{10,11... | collective-permute-start | bytes 798728 | tf_op jit(solution)/shard_map/ppermute | solution.py:414
  32.0 5.1 %collective-permute-start.3 = (bf16[1040,128]{1,0:T(8,128)(2,1)S(1)}, bf16[1040,128]{1,0:T(8,128)(2,1)S(1)}, u32[]{:S(2)}, u32[]{:S(2)}) collective-permute-start(bf16[1040,128]{1,0:T(8,128)(2,1)S(1)} %get-tuple-element.25), channel_id=1, source_target_pairs={{0,1},{1,0},{2,3},{3,2},{4,5},{5,4},{6,7},{7,6},{8,9},{9,8},{10,11... | collective-permute-start | bytes 798728 | tf_op jit(solution)/shard_map/ppermute | solution.py:414
  33.0 9.3 %collective-permute-start.9 = (bf16[1040,128]{1,0:T(8,128)(2,1)S(1)}, bf16[1040,128]{1,0:T(8,128)(2,1)S(1)}, u32[]{:S(2)}, u32[]{:S(2)}) collective-permute-start(bf16[1040,128]{1,0:T(8,128)(2,1)S(1)} %shard_map.94), channel_id=1, source_target_pairs={{0,2},{1,3},{2,0},{3,1},{4,6},{5,7},{6,4},{7,5},{8,10},{9,11},{10,... | collective-permute-start | bytes 798728 | tf_op jit(solution)/shard_map/ppermute | solution.py:414
  33.4 15.7 %collective-permute-start.7 = (bf16[1040,128]{1,0:T(8,128)(2,1)S(1)}, bf16[1040,128]{1,0:T(8,128)(2,1)S(1)}, u32[]{:S(2)}, u32[]{:S(2)}) collective-permute-start(bf16[1040,128]{1,0:T(8,128)(2,1)S(1)} %shard_map.93), channel_id=1, source_target_pairs={{0,4},{1,5},{2,6},{3,7},{4,0},{5,1},{6,2},{7,3},{8,12},{9,13},{10,... | collective-permute-start | bytes 798728 | tf_op jit(solution)/shard_map/ppermute | solution.py:414
  37.1 12.1 %collective-permute-start.5 = (bf16[1040,128]{1,0:T(8,128)(2,1)S(1)}, bf16[1040,128]{1,0:T(8,128)(2,1)S(1)}, u32[]{:S(2)}, u32[]{:S(2)}) collective-permute-start(bf16[1040,128]{1,0:T(8,128)(2,1)S(1)} %shard_map.92), channel_id=1, source_target_pairs={{0,6},{1,7},{2,4},{3,5},{4,2},{5,3},{6,0},{7,1},{8,14},{9,15},{10,... | collective-permute-start | bytes 798728 | tf_op jit(solution)/shard_map/ppermute | solution.py:414
  49.4 9.3 %collective-permute-start.11 = (bf16[1024,128]{1,0:T(8,128)(2,1)S(1)}, bf16[1024,128]{1,0:T(8,128)(2,1)S(1)}, u32[]{:S(2)}, u32[]{:S(2)}) collective-permute-start(bf16[1024,128]{1,0:T(8,128)(2,1)S(1)} %get-tuple-element.33.refs_0_), channel_id=1, source_target_pairs={{0,2},{1,3},{2,0},{3,1},{4,6},{5,7},{6,4},{7,5},{8,10},{9,11},{10,... | collective-permute-start | bytes 786440 | tf_op jit(solution)/shard_map/ppermute | solution.py:414
  50.7 12.9 %collective-permute-start.13 = (bf16[1024,128]{1,0:T(8,128)(2,1)S(1)}, bf16[1024,128]{1,0:T(8,128)(2,1)S(1)}, u32[]{:S(2)}, u32[]{:S(2)}) collective-permute-start(bf16[1024,128]{1,0:T(8,128)(2,1)S(1)} %get-tuple-element.33.refs_0_), channel_id=1, source_target_pairs={{0,4},{1,5},{2,6},{3,7},{4,0},{5,1},{6,2},{7,3},{8,12},{9,13},{10,... | collective-permute-start | bytes 786440 | tf_op jit(solution)/shard_map/ppermute | solution.py:414
  51.7 11.9 %collective-permute-start.15 = (bf16[1024,128]{1,0:T(8,128)(2,1)S(1)}, bf16[1024,128]{1,0:T(8,128)(2,1)S(1)}, u32[]{:S(2)}, u32[]{:S(2)}) collective-permute-start(bf16[1024,128]{1,0:T(8,128)(2,1)S(1)} %get-tuple-element.33.refs_0_), channel_id=1, source_target_pairs={{0,6},{1,7},{2,4},{3,5},{4,2},{5,3},{6,0},{7,1},{8,14},{9,15},{10,... | collective-permute-start | bytes 786440 | tf_op jit(solution)/shard_map/ppermute | solution.py:414
  52.9 11.2 %collective-permute-start.10 = (bf16[1024,128]{1,0:T(8,128)(2,1)S(1)}, bf16[1024,128]{1,0:T(8,128)(2,1)S(1)}, u32[]{:S(2)}, u32[]{:S(2)}) collective-permute-start(bf16[1024,128]{1,0:T(8,128)(2,1)S(1)} %get-tuple-element.33.refs_0_), channel_id=1, source_target_pairs={{0,1},{1,0},{2,3},{3,2},{4,5},{5,4},{6,7},{7,6},{8,9},{9,8},{10,11... | collective-permute-start | bytes 786440 | tf_op jit(solution)/shard_map/ppermute | solution.py:414
  58.7 5.5 %collective-permute-start.12 = (bf16[1024,128]{1,0:T(8,128)(2,1)S(1)}, bf16[1024,128]{1,0:T(8,128)(2,1)S(1)}, u32[]{:S(2)}, u32[]{:S(2)}) collective-permute-start(bf16[1024,128]{1,0:T(8,128)(2,1)S(1)} %collective-permute-done.11.refs_2_), channel_id=1, source_target_pairs={{0,1},{1,0},{2,3},{3,2},{4,5},{5,4},{6,7},{7,6},{8,9},{9,8},{10,11... | collective-permute-start | bytes 786440 | tf_op jit(solution)/shard_map/ppermute | solution.py:414
  63.6 1.5 %collective-permute-start.14 = (bf16[1024,128]{1,0:T(8,128)(2,1)S(1)}, bf16[1024,128]{1,0:T(8,128)(2,1)S(1)}, u32[]{:S(2)}, u32[]{:S(2)}) collective-permute-start(bf16[1024,128]{1,0:T(8,128)(2,1)S(1)} %collective-permute-done.13.refs_4_), channel_id=1, source_target_pairs={{0,1},{1,0},{2,3},{3,2},{4,5},{5,4},{6,7},{7,6},{8,9},{9,8},{10,11... | collective-permute-start | bytes 786440 | tf_op jit(solution)/shard_map/ppermute | solution.py:414
  63.6 1.9 %collective-permute-start.16 = (bf16[1024,128]{1,0:T(8,128)(2,1)S(1)}, bf16[1024,128]{1,0:T(8,128)(2,1)S(1)}, u32[]{:S(2)}, u32[]{:S(2)}) collective-permute-start(bf16[1024,128]{1,0:T(8,128)(2,1)S(1)} %collective-permute-done.15.refs_6_), channel_id=1, source_target_pairs={{0,1},{1,0},{2,3},{3,2},{4,5},{5,4},{6,7},{7,6},{8,9},{9,8},{10,11... | collective-permute-start | bytes 786440 | tf_op jit(solution)/shard_map/ppermute | solution.py:414
  68.7 20.6 %collective-permute-start.18 = (bf16[1040,128]{1,0:T(8,128)(2,1)S(1)}, bf16[1040,128]{1,0:T(8,128)(2,1)S(1)}, u32[]{:S(2)}, u32[]{:S(2)}) collective-permute-start(bf16[1040,128]{1,0:T(8,128)(2,1)S(1)} %get-tuple-element.36), channel_id=1, source_target_pairs={{0,16},{8,24},{16,0},{24,8},{1,17},{9,25},{17,1},{25,9},{2,18},{10... | collective-permute-start | bytes 798728 | tf_op jit(solution)/shard_map/ppermute | solution.py:414
  69.3 23.7 %copy-start.4 = (s32[1024]{0:T(1024)S(1)}, s32[1024]{0:T(1024)}, u32[]{:S(2)}) copy-start(s32[1024]{0:T(1024)} %param.9) | copy-start | bytes 12292
  69.3 20.1 %collective-permute-start.19 = (bf16[1040,128]{1,0:T(8,128)(2,1)S(1)}, bf16[1040,128]{1,0:T(8,128)(2,1)S(1)}, u32[]{:S(2)}, u32[]{:S(2)}) collective-permute-start(bf16[1040,128]{1,0:T(8,128)(2,1)S(1)} %get-tuple-element.37), channel_id=1, source_target_pairs={{0,24},{8,16},{16,8},{24,0},{1,25},{9,17},{17,9},{25,1},{2,26},{10... | collective-permute-start | bytes 798728 | tf_op jit(solution)/shard_map/ppermute | solution.py:414
  73.7 19.2 %collective-permute-start.17 = (bf16[1040,128]{1,0:T(8,128)(2,1)S(1)}, bf16[1040,128]{1,0:T(8,128)(2,1)S(1)}, u32[]{:S(2)}, u32[]{:S(2)}) collective-permute-start(bf16[1040,128]{1,0:T(8,128)(2,1)S(1)} %get-tuple-element.35), channel_id=1, source_target_pairs={{0,8},{8,0},{16,24},{24,16},{1,9},{9,1},{17,25},{25,17},{2,10},{10... | collective-permute-start | bytes 798728 | tf_op jit(solution)/shard_map/ppermute | solution.py:414
